TPU v7x, 512 devices: a whole 4x8x8 slice. The times are simulated.
512 devices in a mesh: rep: 8 (over z_hi, x), seq: 64 (over z_lo, y, core).
Axes of the slice: x: 4, y: 8, z: 8 (z_hi: 2, z_lo: 4; z = z_hi * 4 + z_lo), core: 2. Of those that a mesh axis runs over, the one named last changes fastest.
Arguments:
- queries: bfloat16 [8, 8192, 4096], P('rep', 'seq'), may hold values from -6 to 6
- keys: bfloat16 [8, 8192, 512], P('rep', 'seq'), may hold values from -6 to 6
- values: bfloat16 [8, 8192, 512], P('rep', 'seq'), may hold values from -6 to 6
- doc_ids: int32 [8, 8192], P('rep', 'seq'), may hold values from 0 to 63, never falling along the last dimension, each value on 1 to 256 neighbouring positions
- coeffs: bfloat16 [8, 8192, 256], P('rep', 'seq'), may hold values from -6 to 6
- shard_dest: int32 [8, 64], P('rep', 'seq'), may hold values from 0 to 63, each once within a row
- basis: bfloat16 [256, 8192], P(None, 'seq'), may hold values from -0.0625 to 0.0625
Outputs:
- attended: bfloat16 [8, 8192, 4096], P('rep', 'seq')
- grad_proj: float32 [4096, 256], P('seq')
Inputs may be any that keep to these rules, and one draw needn't show every extreme that they name: Each replica's row holds every number once; sender j of seq holds the coefficients of sequence block shard_dest[r, j]. `doc_ids`: never falling along a sequence; each document has at most 256 tokens, and one has exactly 256.
All inputs are finite; a program needn't handle non-finite values.
Results may differ from a plain program's by a relative error of at most 0.0056.
Values may be sent and summed in bfloat16 or wider, within the bound.
No kernel may reach another device: no remote copies, remote signals or barrier semaphores. Data moves between devices by JAX's collectives and lax.ppermute only.
A program may use at most 64 MiB of HBM per device.

v0:
```python
import math

import jax
import jax.numpy as jnp
from jax import lax
from jax.sharding import PartitionSpec as P

QUERY_HEADS = 32
KEY_VALUE_HEADS = 4
HEAD_SIZE = 128
EARLIER_BLOCKS = 2


def shifted(block, axis, distance):
    devices = range(lax.axis_size(axis))
    route = [(i - distance, i) for i in devices if i - distance in devices]
    return lax.ppermute(block, axis, route)


def attend_group(group_queries, group_keys, group_values, visible, scale):
    scores = (
        jnp.einsum("tgd,sd->gts", group_queries, group_keys, preferred_element_type=jnp.float32)
        * scale
    )
    scores = jnp.where(visible[None], scores, jnp.float32(-1e30))
    highest = jnp.max(scores, axis=-1, keepdims=True)
    expos = jnp.exp(scores - highest)
    totals = jnp.sum(expos, axis=-1, keepdims=True)
    weights = (expos / totals).astype(jnp.bfloat16)
    return jnp.einsum(
        "gts,sd->tgd", weights, group_values, preferred_element_type=jnp.float32
    ).astype(jnp.bfloat16)


def attend(query_row_block, key_row_block, value_row_block, visible):
    token_count = query_row_block.shape[0]
    grouped_heads = query_row_block.reshape(
        token_count, KEY_VALUE_HEADS, QUERY_HEADS // KEY_VALUE_HEADS, HEAD_SIZE
    ).transpose(1, 0, 2, 3)
    key_tensor = key_row_block.reshape(-1, KEY_VALUE_HEADS, HEAD_SIZE).transpose(1, 0, 2)
    value_tensor = value_row_block.reshape(-1, KEY_VALUE_HEADS, HEAD_SIZE).transpose(1, 0, 2)
    scale = HEAD_SIZE ** (-0.5)

    def per_head(operands):
        return attend_group(operands[0], operands[1], operands[2], visible, scale)

    mixed = lax.map(per_head, (grouped_heads, key_tensor, value_tensor))
    return mixed.transpose(1, 0, 2, 3).reshape(token_count, QUERY_HEADS * HEAD_SIZE)


def local(queries, keys, values, doc_ids, coeffs, shard_dest, basis):
    seq_count = lax.axis_size("seq")
    rep_count = lax.axis_size("rep")
    token_count = queries.shape[1]
    own_tags = (doc_ids[0] + 1).astype(jnp.bfloat16)
    own_pair = jnp.stack([keys[0], values[0]], axis=0)
    own_block = (own_pair, own_tags)
    earlier = []
    for distance in range(1, EARLIER_BLOCKS + 1):
        earlier.insert(0, shifted((own_block[0], own_block[1]), "seq", distance))
    window_keys = jnp.concatenate([item[0][0] for item in earlier] + [keys[0]], axis=0)
    window_values = jnp.concatenate([item[0][1] for item in earlier] + [values[0]], axis=0)
    window_tags = jnp.concatenate([item[1] for item in earlier] + [own_tags], axis=0)
    key_pos = jnp.arange(window_keys.shape[0], dtype=jnp.int32) - EARLIER_BLOCKS * token_count
    query_pos = jnp.arange(token_count, dtype=jnp.int32)
    visible = (window_tags[None, :] == own_tags[:, None]) & (key_pos[None, :] <= query_pos[:, None])
    attended = attend(queries[0], window_keys, window_values, visible)
    targets = (jnp.arange(seq_count, dtype=jnp.int32) == shard_dest[0, 0]).astype(jnp.bfloat16)
    outgoing = targets[:, None, None] * coeffs[0][None, :, :]
    arrived = lax.all_to_all(outgoing, "seq", split_axis=0, concat_axis=0, tiled=True)
    received = jnp.sum(arrived, axis=0, dtype=jnp.float32).astype(jnp.bfloat16)
    columns = lax.all_gather(basis, "seq", axis=1, tiled=True)
    rebuilt = jnp.dot(received, columns, preferred_element_type=jnp.float32)
    projected_wide = jnp.dot(
        rebuilt, columns.astype(jnp.float32).T, precision=lax.Precision.HIGHEST
    )
    projected = projected_wide.astype(jnp.bfloat16)
    columns = attended
    partial_rows = lax.psum_scatter(
        lax.dot_general(
            columns, projected, (((0,), (0,)), ((), ())), preferred_element_type=jnp.float32
        ),
        "seq",
        scatter_dimension=0,
        tiled=True,
    )
    summed = lax.psum(partial_rows, "rep")
    grad_proj = summed * (1.0 / math.sqrt(rep_count * seq_count * token_count))
    return (attended[None], grad_proj)


def solution(mesh):
    in_specs = (
        P("rep", "seq", None),
        P("rep", "seq", None),
        P("rep", "seq", None),
        P("rep", "seq"),
        P("rep", "seq", None),
        P("rep", "seq"),
        P(None, "seq"),
    )
    out_specs = (P("rep", "seq", None), P("seq", None))
    return jax.shard_map(local, mesh=mesh, in_specs=in_specs, out_specs=out_specs, check_vma=False)
```

profile of v0, /device:TPU:8, one launch (start us, length us, event | category | flops | bytes accessed | tf_op | source)
XLA Modules:
  0.0 628.3 jit_solution(3516366991436335908)
XLA Ops:
  7.8 3.1 broadcast_multiply_fusion
  11.0 0.0 copy-start.2
  11.0 0.0 copy-start.3
  11.0 0.0 copy-start.4
  11.0 13.9 %all-to-all-start = ((bf16[64,128,256]{2,1,0:T(8,128)(2,1)}), bf16[64,128,256]{2,1,0:T(8,128)(2,1)}, u32[]{:S(2)}, u32[]{:S(2)}) async-start(bf16[64,128,256]{2,1,0:T(8,128)(2,1)} %broadcast_multiply_fusion), calls=%async_computation | async-start | bytes 8388608 | tf_op jit(solution)/shard_map/all_to_all | solution.py:70
  24.8 0.0 copy-start.1
  24.9 0.0 all-gather.2.cloned.1.call-start
  24.9 0.7 all-gather.2.cloned.1.call-update
  25.6 0.0 reduce-scatter.2.cloned.1.call-start
  25.6 0.0 copy-done.2
  25.6 0.1 copy.25
  25.8 0.0 copy-done.3
  25.8 0.1 copy.24
  25.9 0.7 pad_maximum_fusion
  26.6 2.0 collective-permute-start.1
  28.7 3.4 collective-permute-start
  32.1 0.0 copy-done.4
  32.1 3.1 collective-permute-start.3
  35.2 4.6 collective-permute-start.2
  39.8 0.0 copy-done.1
  39.8 0.7 copy.28
  40.5 88.3 %collective-permute-done.3 = bf16[128]{0:T(256)(128)(2,1)S(1)} collective-permute-done((bf16[128]{0:T(256)(128)(2,1)S(1)}, bf16[128]{0:T(256)(128)(2,1)S(1)}, u32[]{:S(2)}, u32[]{:S(2)}) %collective-permute-start.3) | collective-permute-done | bytes 288 | tf_op jit(solution)/shard_map/ppermute | solution.py:17
  128.8 0.0 collective-permute-done.2
  128.8 0.0 collective-permute-done.1
  128.8 1.0 fusion.52
  129.8 0.0 collective-permute-done
  129.8 1.0 fusion.51
  130.8 0.1 maximum_bitcast_fusion
  130.9 7.5 %while.11 = (s32[]{:T(128)}, bf16[4,128,8,128]{1,3,2,0:T(8,128)(2,1)S(1)}, bf16[4,384,128]{1,2,0:T(8,128)(2,1)S(1)}, bf16[4,384,128]{1,2,0:T(8,128)(2,1)S(1)}, b...) while((s32[]{:T(128)}, ...), condition=%wide.region_3.4_spmd.clone, body=%wide.region_0.3_spmd.clone.sunk | while | flops 305907456 | bytes 1242725 | solution.py:47
  130.9 0.2 fusion.74
  131.1 0.7 fusion.75
  131.8 1.0 fusion.76
  132.8 0.2 fusion.74
  133.0 0.7 fusion.75
  133.7 1.0 fusion.76
  134.7 0.2 fusion.74
  134.8 0.7 fusion.75
  135.5 1.0 fusion.76
  136.6 0.2 fusion.74
  136.7 0.7 fusion.75
  137.4 1.0 fusion.76
  138.4 0.0 all-to-all-done
  138.4 2.8 reduce_sum.21
  141.2 75.7 %all-gather.2.cloned.1.call-done = bf16[256,8192]{1,0:T(8,128)(2,1)} async-done(((bf16[256,128]{1,0:T(8,128)(2,1)}), bf16[256,8192]{1,0:T(8,128)(2,1)}) %all-gather.2.cloned.1.call-update) | async-done | bytes 4194320 | tf_op jit(solution)/shard_map/all_gather | solution.py:72
  216.9 0.0 copy-start
  216.9 3.1 fusion.53
  220.0 0.4 copy-done
  220.3 4.3 convolution_convert_fusion.1
  224.6 2.6 fusion.54
  227.3 0.0 reduce-scatter.2.cloned.1.call-update
  227.3 0.0 all-reduce.2.cloned.1.call-start
  227.3 278.2 %reduce-scatter.2.cloned.1.call-done = f32[64,256]{1,0:T(8,128)} async-done(((f32[4096,256]{1,0:T(8,128)}), f32[64,256]{1,0:T(8,128)}) %reduce-scatter.2.cloned.1.call-update) | async-done | bytes 65552 | tf_op jit(solution)/shard_map/reduce_scatter | solution.py:79
  505.6 0.0 all-reduce.2.cloned.1.call-update
  505.6 1.3 copy.33
  506.9 113.4 %all-reduce.2.cloned.1.call-done = f32[64,256]{1,0:T(8,128)} async-done(((f32[64,256]{1,0:T(8,128)}), f32[64,256]{1,0:T(8,128)}) %all-reduce.2.cloned.1.call-update) | async-done | bytes 65552 | tf_op jit(solution)/shard_map/psum | solution.py:87
  620.3 1.5 broadcast_multiply_fusion.1
  (5 shorter events, 0.0 us)
Async XLA Ops:
  11.0 14.7 %copy-start.2 = (bf16[1,128,512]{2,1,0:T(8,128)(2,1)S(1)}, bf16[1,128,512]{2,1,0:T(8,128)(2,1)}, u32[]{:S(2)}) copy-start(bf16[1,128,512]{2,1,0:T(8,128)(2,1)} %param.11) | copy-start | bytes 393220
  11.0 14.8 %copy-start.3 = (bf16[1,128,512]{2,1,0:T(8,128)(2,1)S(1)}, bf16[1,128,512]{2,1,0:T(8,128)(2,1)}, u32[]{:S(2)}) copy-start(bf16[1,128,512]{2,1,0:T(8,128)(2,1)} %param.10) | copy-start | bytes 393220
  11.0 21.1 %copy-start.4 = (s32[1,128]{1,0:T(1,128)S(1)}, s32[1,128]{1,0:T(1,128)}, u32[]{:S(2)}) copy-start(s32[1,128]{1,0:T(1,128)} %param.12) | copy-start | bytes 1540
  11.0 127.4 %all-to-all-start = ((bf16[64,128,256]{2,1,0:T(8,128)(2,1)}), bf16[64,128,256]{2,1,0:T(8,128)(2,1)}, u32[]{:S(2)}, u32[]{:S(2)}) async-start(bf16[64,128,256]{2,1,0:T(8,128)(2,1)} %broadcast_multiply_fusion), calls=%async_computation | async-start | bytes 8388608 | tf_op jit(solution)/shard_map/all_to_all | solution.py:70
  24.8 14.9 %copy-start.1 = (bf16[1,128,4096]{2,1,0:T(8,128)(2,1)S(1)}, bf16[1,128,4096]{2,1,0:T(8,128)(2,1)}, u32[]{:S(2)}) copy-start(bf16[1,128,4096]{2,1,0:T(8,128)(2,1)} %param.9) | copy-start | bytes 3145732
  24.9 192.0 %all-gather.2.cloned.1.call-start = ((), (), s32[]{:S(2)}) async-start(), calls=%async_computation.2 | async-start | bytes 4259840 | tf_op jit(solution)/shard_map/all_gather | solution.py:72
  25.6 480.0 %reduce-scatter.2.cloned.1.call-start = ((), (), s32[]{:S(2)}) async-start(), calls=%async_computation.3 | async-start | bytes 4259840 | tf_op jit(solution)/shard_map/reduce_scatter | solution.py:79
  26.6 102.1 %collective-permute-start.1 = (bf16[2,128,512]{1,2,0:T(8,128)(2,1)}, bf16[2,128,512]{1,2,0:T(8,128)(2,1)}, u32[]{:S(2)}, u32[]{:S(2)}) collective-permute-start(bf16[2,128,512]{1,2,0:T(8,128)(2,1)} %pad_maximum_fusion), channel_id=1, source_target_pairs={{0,1},{1,2},{2,3},{3,4},{4,5},{5,6},{6,7},{7,8},{8,9},{9,10},{10,1... | collective-permute-start | bytes 786440 | tf_op jit(solution)/shard_map/ppermute | solution.py:17
  28.7 101.1 %collective-permute-start = (bf16[2,128,512]{1,2,0:T(8,128)(2,1)}, bf16[2,128,512]{1,2,0:T(8,128)(2,1)}, u32[]{:S(2)}, u32[]{:S(2)}) collective-permute-start(bf16[2,128,512]{1,2,0:T(8,128)(2,1)} %pad_maximum_fusion), channel_id=1, source_target_pairs={{0,2},{1,3},{2,4},{3,5},{4,6},{5,7},{6,8},{7,9},{8,10},{9,11},{10,... | collective-permute-start | bytes 786440 | tf_op jit(solution)/shard_map/ppermute | solution.py:17
  32.1 96.7 %collective-permute-start.3 = (bf16[128]{0:T(256)(128)(2,1)S(1)}, bf16[128]{0:T(256)(128)(2,1)S(1)}, u32[]{:S(2)}, u32[]{:S(2)}) collective-permute-start(bf16[128]{0:T(256)(128)(2,1)S(1)} %convert_bitcast_fusion), channel_id=1, source_target_pairs={{0,1},{1,2},{2,3},{3,4},{4,5},{5,6},{6,7},{7,8},{8,9},{9,10},{10,1... | collective-permute-start | bytes 776 | tf_op jit(solution)/shard_map/ppermute | solution.py:17
  35.2 93.6 %collective-permute-start.2 = (bf16[128]{0:T(256)(128)(2,1)S(1)}, bf16[128]{0:T(256)(128)(2,1)S(1)}, u32[]{:S(2)}, u32[]{:S(2)}) collective-permute-start(bf16[128]{0:T(256)(128)(2,1)S(1)} %convert_bitcast_fusion), channel_id=1, source_target_pairs={{0,2},{1,3},{2,4},{3,5},{4,6},{5,7},{6,8},{7,9},{8,10},{9,11},{10,... | collective-permute-start | bytes 776 | tf_op jit(solution)/shard_map/ppermute | solution.py:17
  216.9 3.4 copy-start
  227.3 393.0 %all-reduce.2.cloned.1.call-start = ((), (), s32[]{:S(2)}) async-start(), calls=%async_computation.4 | async-start | bytes 131072 | tf_op jit(solution)/shard_map/psum | solution.py:87
Sparse Core Ops, SparseCore 0:
  27.8 189.0 all-gather.1
  227.4 278.1 reduce-scatter.1
  508.7 111.5 all-reduce.1
where the time goes:
time: 629 us; the launch traced here: 628 us
  waiting for transfers between devices  556 us (88%)
  starting transfers between devices  27 us (4%)
  matrix products  16.7 us (3%)
  between operations  14.6 us (2%)
  other arithmetic  8.96 us (1%)
    reduce_scatter x1, waiting for transfers between devices, local(): lax.psum_scatter(lax.dot_general(columns, projected, (((0,), (0,)), ((),...  278 us
    psum x1, waiting for transfers between devices, local(): summed = lax.psum(partial_rows, 'rep')  113 us
    ppermute x4, waiting for transfers between devices, shifted(): return lax.ppermute(block, axis, route)  88.3 us
    all_gather x1, waiting for transfers between devices, local(): columns = lax.all_gather(basis, 'seq', axis=1, tiled=True)  75.7 us
    all_to_all x1, starting transfers between devices, local(): lax.all_to_all(outgoing, 'seq', split_axis=0, concat_axis=0, tiled=True)  13.9 us
    ppermute x4, starting transfers between devices, shifted(): return lax.ppermute(block, axis, route)  13.1 us
  transfers between devices with their start and end apart: 8, of which 4 were waited for; matrix products, arithmetic and copies ran while one was open for 2% of the time, Pallas kernels for 0%

commit v1 on v0

v1 whole, which is shorter than its diff:
```python
import functools
import math

import jax
import jax.numpy as jnp
from jax import lax
from jax.experimental import pallas as pl
from jax.experimental.pallas import tpu as pltpu
from jax.sharding import PartitionSpec as P

QUERY_HEADS = 32
KEY_VALUE_HEADS = 4
HEAD_SIZE = 128
GROUP = QUERY_HEADS // KEY_VALUE_HEADS
TOKENS = 128
R = 256
SEQ = 64
REP = 8
CHIPS = SEQ // 2
HALF = HEAD_SIZE // 2
LOG2E = math.log2(math.e)
VMEM_LIMIT = 48 * 1024 * 1024


def shifted(block, distance):
    return lax.ppermute(block, "seq", [(i, i + distance) for i in range(SEQ - distance)])


def other_core(block):
    return lax.ppermute(block, "seq", [(i, i ^ 1) for i in range(SEQ)])


NT = (((1,), (1,)), ((), ()))


def attention_kernel(core_ref, q_ref, own_ref, one_ref, two_ref, tags_ref, out_ref, keep_ref, send_ref):
    core = core_ref[0]
    tags = tags_ref[...]
    query_tags = jnp.broadcast_to(tags[2:3, :], (TOKENS, TOKENS))
    key_pos = lax.broadcasted_iota(jnp.int32, (TOKENS, TOKENS), 0)
    query_pos = lax.broadcasted_iota(jnp.int32, (TOKENS, TOKENS), 1)
    visible = []
    for i in range(3):
        key_tags = jnp.broadcast_to(tags[i : i + 1, :], (TOKENS, TOKENS)).T
        seen = key_tags == query_tags
        if i == 2:
            seen = seen & (key_pos <= query_pos)
        visible.append(seen)
    factor = HEAD_SIZE ** (-0.5) * LOG2E
    blocks = (two_ref, one_ref, own_ref)
    for g in range(KEY_VALUE_HEADS):
        at = g * HEAD_SIZE
        keys = [b[:, at : at + HEAD_SIZE] for b in blocks]
        values = [
            b[:, 512 + at : 512 + at + HEAD_SIZE].astype(jnp.float32).T.astype(jnp.bfloat16)
            for b in blocks
        ]
        values = jnp.concatenate(values, axis=1)
        for j in range(GROUP):
            h = g * GROUP + j
            q = q_ref[:, h * HEAD_SIZE : (h + 1) * HEAD_SIZE]
            scores = [
                jnp.where(
                    visible[i],
                    lax.dot_general(keys[i], q, NT, preferred_element_type=jnp.float32),
                    jnp.float32(-1e30),
                )
                for i in range(3)
            ]
            highest = jnp.max(
                jnp.maximum(jnp.maximum(scores[0], scores[1]), scores[2]), axis=0, keepdims=True
            )
            expos = [jnp.exp2((s - highest) * factor) for s in scores]
            totals = jnp.sum(expos[0] + expos[1] + expos[2], axis=0, keepdims=True)
            inverse = 1.0 / totals
            weights = jnp.concatenate([(e * inverse).astype(jnp.bfloat16) for e in expos], axis=0)
            mixed = jnp.dot(values, weights, preferred_element_type=jnp.float32)
            out_ref[:, h * HEAD_SIZE : (h + 1) * HEAD_SIZE] = mixed.T.astype(jnp.bfloat16)
            low, high = mixed[:HALF], mixed[HALF:]
            keep_ref[h * HALF : (h + 1) * HALF, :] = jnp.where(core == 0, low, high).astype(jnp.bfloat16)
            send_ref[h * HALF : (h + 1) * HALF, :] = jnp.where(core == 0, high, low).astype(jnp.bfloat16)


def attention(core, q, own, one, two, tags):
    vmem = pl.BlockSpec(memory_space=pltpu.VMEM)
    return pl.pallas_call(
        attention_kernel,
        out_shape=(
            jax.ShapeDtypeStruct((TOKENS, QUERY_HEADS * HEAD_SIZE), jnp.bfloat16),
            jax.ShapeDtypeStruct((QUERY_HEADS * HALF, TOKENS), jnp.bfloat16),
            jax.ShapeDtypeStruct((QUERY_HEADS * HALF, TOKENS), jnp.bfloat16),
        ),
        in_specs=[pl.BlockSpec(memory_space=pltpu.SMEM)] + [vmem] * 5,
        out_specs=(vmem, vmem, vmem),
        compiler_params=pltpu.CompilerParams(vmem_limit_bytes=VMEM_LIMIT),
        cost_estimate=pl.CostEstimate(
            flops=4 * QUERY_HEADS * TOKENS * 3 * TOKENS * HEAD_SIZE * 8,
            bytes_accessed=4 << 20,
            transcendentals=QUERY_HEADS * TOKENS * 3 * TOKENS,
        ),
    )(core, q, own, one, two, tags)


def outer_kernel(keep_ref, got_ref, own_ref, sib_ref, out_ref):
    total = lax.dot_general(keep_ref[...], own_ref[...], NT, preferred_element_type=jnp.float32)
    total += lax.dot_general(got_ref[...], sib_ref[...], NT, preferred_element_type=jnp.float32)
    out_ref[...] = total.astype(jnp.bfloat16)


def outer(keep, got, own, sib):
    rows, step = keep.shape[0], 256
    return pl.pallas_call(
        outer_kernel,
        out_shape=jax.ShapeDtypeStruct((rows, R), jnp.bfloat16),
        grid=(rows // step,),
        in_specs=[
            pl.BlockSpec((step, TOKENS), lambda i: (i, 0)),
            pl.BlockSpec((step, TOKENS), lambda i: (i, 0)),
            pl.BlockSpec((R, TOKENS), lambda i: (0, 0)),
            pl.BlockSpec((R, TOKENS), lambda i: (0, 0)),
        ],
        out_specs=pl.BlockSpec((step, R), lambda i: (i, 0)),
        compiler_params=pltpu.CompilerParams(vmem_limit_bytes=VMEM_LIMIT),
    )(keep, got, own, sib)


def local(queries, keys, values, doc_ids, coeffs, shard_dest, basis):
    seq = lax.axis_index("seq")
    rep = lax.axis_index("rep")
    bf16 = jnp.bfloat16

    own = jnp.concatenate([keys[0], values[0]], axis=1)
    two = shifted(own, 2)
    one = shifted(own, 1)

    gram_rows = R // REP
    basis_rows = lax.dynamic_slice_in_dim(basis, rep * gram_rows, gram_rows, 0)
    gram = lax.dot_general(basis_rows, basis, NT, preferred_element_type=jnp.float32)
    pieces = coeffs[0].T.reshape(SEQ, 4, TOKENS)
    extra = jnp.concatenate(
        [
            gram.astype(bf16).reshape(SEQ, 1, TOKENS),
            jnp.broadcast_to(shard_dest[0, 0].astype(bf16), (SEQ, 1, TOKENS)),
            jnp.broadcast_to(doc_ids[0].astype(bf16), (SEQ, 1, TOKENS)),
            jnp.zeros((SEQ, 1, TOKENS), bf16),
        ],
        axis=1,
    )
    first = lax.all_to_all(
        jnp.concatenate([pieces, extra], axis=2), "seq", split_axis=0, concat_axis=0, tiled=True
    )

    dest = first[:, 1, TOKENS].astype(jnp.int32)
    chosen = (dest[None, :] == jnp.arange(SEQ, dtype=jnp.int32)[:, None]).astype(bf16)
    sorted_own = jnp.einsum(
        "bj,jit->bit", chosen, first[:, :, :TOKENS], preferred_element_type=jnp.float32
    ).astype(bf16)
    chosen_sib = (dest[None, :] == (jnp.arange(SEQ, dtype=jnp.int32) ^ 1)[:, None]).astype(bf16)
    sorted_sib = jnp.einsum(
        "bj,jit->bit", chosen_sib, first[:, :, :TOKENS], preferred_element_type=jnp.float32
    ).astype(bf16)
    gram_piece = jnp.sum(first[:, 0, TOKENS:].astype(jnp.float32), axis=0).astype(bf16)
    second = lax.all_to_all(
        jnp.concatenate(
            [sorted_own, sorted_sib, jnp.broadcast_to(gram_piece, (SEQ, 4, TOKENS))], axis=2
        ),
        "seq",
        split_axis=0,
        concat_axis=0,
        tiled=True,
    )

    tag_rows = first[:, 2, TOKENS:].astype(jnp.float32)
    places = seq + jnp.arange(-2, 1, dtype=jnp.int32)
    tags = jnp.where(
        (places >= 0)[:, None], jnp.take(tag_rows, jnp.maximum(places, 0), axis=0), jnp.float32(-1)
    )
    core = (seq % 2).astype(jnp.int32).reshape(1)
    attended, keep, send = attention(core, queries[0], own, one, two, tags)
    got = other_core(send)

    coeffs_own = second[:, :, :TOKENS].reshape(R, TOKENS)
    coeffs_sib = second[:, :, TOKENS : 2 * TOKENS].reshape(R, TOKENS)
    partial = outer(keep, got, coeffs_own, coeffs_sib).reshape(CHIPS, HALF, R)
    arrived = lax.all_to_all(
        partial,
        "seq",
        split_axis=0,
        concat_axis=0,
        axis_index_groups=[list(range(0, SEQ, 2)), list(range(1, SEQ, 2))],
        tiled=True,
    )
    rows = jnp.sum(arrived.astype(jnp.float32), axis=0).astype(bf16)
    gram_share = second[:, 0, 2 * TOKENS :].reshape(gram_rows, R)
    last = lax.all_to_all(
        jnp.broadcast_to(jnp.concatenate([rows, gram_share], axis=0), (REP, HALF + gram_rows, R)),
        "rep",
        split_axis=0,
        concat_axis=0,
        tiled=True,
    )
    summed = jnp.sum(last[:, :HALF].astype(jnp.float32), axis=0)
    gram_all = last[:, HALF:].reshape(R, R).astype(jnp.float32)
    grad = jnp.dot(summed, gram_all, precision=lax.Precision.HIGHEST)
    grad = grad * (1.0 / math.sqrt(REP * SEQ * TOKENS))
    return attended[None], grad


def solution(mesh):
    in_specs = (
        P("rep", "seq", None),
        P("rep", "seq", None),
        P("rep", "seq", None),
        P("rep", "seq"),
        P("rep", "seq", None),
        P("rep", "seq"),
        P(None, "seq"),
    )
    out_specs = (P("rep", "seq", None), P("seq", None))
    return jax.shard_map(local, mesh=mesh, in_specs=in_specs, out_specs=out_specs, check_vma=False)
```

time: 629 us -> 125 us (0.20)
  the two profiles are of different devices: /device:TPU:8 before, /device:TPU:72 now
where the time goes in v1:
time: 125 us; the launch traced here: 124 us
  waiting for transfers between devices  39.3 us (31%)
  starting transfers between devices  35.4 us (28%)
  blocking collectives  25.9 us (21%)
  Pallas kernels  14.4 us (12%)
  other arithmetic  3.42 us (3%)
  local copies, waits for them, and re-layouts  3.1 us (2%)
  between operations  1.54 us (1%)
  matrix products  1.33 us (1%)
    all_to_all x1, waiting for transfers between devices, local(): lax.all_to_all(partial, 'seq', split_axis=0, concat_axis=0, axis_index_gr...  28.2 us
    all_to_all x1, blocking collectives, local(): lax.all_to_all(jnp.broadcast_to(jnp.concatenate([rows, gram_share], axis=...  25.9 us
    all_to_all x1, starting transfers between devices, local(): lax.all_to_all(jnp.concatenate([pieces, extra], axis=2), 'seq', split_axi...  12.2 us
    pallas_call x1, Pallas kernels, attention(): pl.pallas_call(attention_kernel, out_shape=(jax.ShapeDtypeStruct((TOKENS,...  10.6 us
    all_to_all x1, starting transfers between devices, local(): lax.all_to_all(partial, 'seq', split_axis=0, concat_axis=0, axis_index_gr...  10.3 us
    all_to_all x1, waiting for transfers between devices, local(): lax.all_to_all(jnp.concatenate([pieces, extra], axis=2), 'seq', split_axi...  9.47 us
    ppermute x2, starting transfers between devices, shifted(): lax.ppermute(block, 'seq', [(i, i + distance) for i in range(SEQ - distan...  5.41 us
    all_to_all x1, starting transfers between devices, local(): lax.all_to_all(jnp.concatenate([sorted_own, sorted_sib, jnp.broadcast_to(...  5.4 us
  transfers between devices with their start and end apart: 6, of which 3 were waited for; matrix products, arithmetic and copies ran while one was open for 4% of the time, Pallas kernels for 9%

profile of v1, /device:TPU:72, one launch (start us, length us, event | category | flops | bytes accessed | tf_op | source)
XLA Modules:
  0.0 124.4 jit_solution(13663421885410783757)
XLA Ops:
  0.6 0.0 copy-start
  0.6 1.0 pad_maximum_fusion.own_ref
  1.7 3.5 %collective-permute-start.1 = (bf16[128,1024]{1,0:T(8,128)(2,1)S(1)}, bf16[128,1024]{1,0:T(8,128)(2,1)S(1)}, u32[]{:S(2)}, u32[]{:S(2)}) collective-permute-start(bf16[128,1024]{1,0:T(8,128)(2,1)S(1)} %pad_maximum_fusion.own_ref), channel_id=1, source_target_pairs={{0,2},{1,3},{2,4},{3,5},{4,6},{5,7},{6,8},{7,9},{8,10},{9,11},{10,... | collective-permute-start | bytes 786440 | tf_op jit(solution)/shard_map/ppermute | solution.py:26
  5.2 1.9 %collective-permute-start = (bf16[128,1024]{1,0:T(8,128)(2,1)S(1)}, bf16[128,1024]{1,0:T(8,128)(2,1)S(1)}, u32[]{:S(2)}, u32[]{:S(2)}) collective-permute-start(bf16[128,1024]{1,0:T(8,128)(2,1)S(1)} %pad_maximum_fusion.own_ref), channel_id=1, source_target_pairs={{0,1},{1,2},{2,3},{3,4},{4,5},{5,6},{6,7},{7,8},{8,9},{9,10},{10,1... | collective-permute-start | bytes 786440 | tf_op jit(solution)/shard_map/ppermute | solution.py:26
  7.7 0.0 copy-start.3
  7.8 0.6 copy-done.3
  8.5 0.0 copy-done
  8.5 0.0 copy-start.2
  8.5 0.1 convolution_convert_fusion.2
  8.7 0.7 copy-done.2
  9.3 0.1 copy.25
  9.4 0.8 maximum_maximum_fusion.1
  10.2 0.0 copy-start.1
  10.2 12.2 %all-to-all-start = ((bf16[64,4,256]{2,1,0:T(4,128)(2,1)}), bf16[64,4,256]{2,1,0:T(4,128)(2,1)S(1)}, u32[]{:S(2)}, u32[]{:S(2)}) async-start(bf16[64,4,256]{2,1,0:T(4,128)(2,1)} %maximum_maximum_fusion.1), calls=%async_computation | async-start | bytes 262144 | tf_op jit(solution)/shard_map/all_to_all | solution.py:149
  22.5 9.5 %all-to-all-done = bf16[64,4,256]{2,1,0:T(4,128)(2,1)S(1)} async-done(((bf16[64,4,256]{2,1,0:T(4,128)(2,1)}), bf16[64,4,256]{2,1,0:T(4,128)(2,1)S(1)}, u32[]{:S(2)}, u32[]{:S(2)}) %all-to-all-start) | async-done | bytes 131104 | tf_op jit(solution)/shard_map/all_to_all | solution.py:149
  32.0 0.1 slice_reduce_fusion.1
  32.1 1.2 fusion.2
  33.3 0.1 convolution_convert_fusion.1
  33.5 0.2 convolution_convert_fusion
  33.8 0.8 copy.29
  34.6 5.4 %all-to-all-start.1 = ((bf16[64,4,384]{2,1,0:T(4,128)(2,1)}), bf16[64,4,384]{2,1,0:T(4,128)(2,1)S(1)}, u32[]{:S(2)}, u32[]{:S(2)}) async-start(bf16[64,4,384]{2,1,0:T(4,128)(2,1)} %copy.29), calls=%async_computation.1 | async-start | bytes 393216 | tf_op jit(solution)/shard_map/all_to_all | solution.py:163
  40.0 0.6 gather_fusion
  40.5 0.1 select_select_fusion.tags_ref
  40.6 0.0 collective-permute-done.1.two_ref
  40.6 0.0 collective-permute-done.one_ref
  40.6 0.0 copy-done.1
  40.6 10.6 %shard_map.86 = (bf16[128,4096]{1,0:T(8,128)(2,1)}, bf16[2048,128]{1,0:T(8,128)(2,1)S(1)}, bf16[2048,128]{1,0:T(8,128)(2,1)S(1)}) custom-call(s32[1]{0:T(128)} %bitcast.core_ref, bf16[128,4096]{1,0:T(8,128)(2,1)S(1)} %bitcast.34, bf16[128,1024]{1,0:T(8,128)(2,1)S(1)} %pad_maximum_fusion.own_ref, bf16[128,1024]{1,0:T(8,128)(2,1)S(1)} %collective-permute-done.one_ref, ...), custom_call_target="tpu_custom_call" | custom-call | flops 6442450944 | bytes 4194304 | tf_op jit(solution)/shard_map/pallas_call | solution.py:86
  51.2 2.0 %collective-permute-start.2 = (bf16[2048,128]{1,0:T(8,128)(2,1)S(1)}, bf16[2048,128]{1,0:T(8,128)(2,1)S(1)}, u32[]{:S(2)}, u32[]{:S(2)}) collective-permute-start(bf16[2048,128]{1,0:T(8,128)(2,1)S(1)} %get-tuple-element.7), channel_id=1, source_target_pairs={{0,1},{1,0},{2,3},{3,2},{4,5},{5,4},{6,7},{7,6},{8,9},{9,8},{10,11... | collective-permute-start | bytes 1572872 | tf_op jit(solution)/shard_map/ppermute | solution.py:30
  53.3 0.0 all-to-all-done.1
  53.4 1.7 %collective-permute-done.2.got_ref = bf16[2048,128]{1,0:T(8,128)(2,1)S(1)} collective-permute-done((bf16[2048,128]{1,0:T(8,128)(2,1)S(1)}, bf16[2048,128]{1,0:T(8,128)(2,1)S(1)}, u32[]{:S(2)}, u32[]{:S(2)}) %collective-permute-start.2) | collective-permute-done | bytes 524320 | tf_op jit(solution)/shard_map/ppermute | solution.py:30
  55.0 3.8 %shard_map.87 = bf16[2048,256]{1,0:T(8,128)(2,1)} custom-call(bf16[2048,128]{1,0:T(8,128)(2,1)S(1)} %get-tuple-element.6.keep_ref, bf16[2048,128]{1,0:T(8,128)(2,1)S(1)} %collective-permute-done.2.got_ref, bf16[256,128]{1,0:T(8,128)(2,1)S(1)} %bitcast.33, bf16[256,128]{1,0:T(8,128)(2,1)S(1)} %bitcast.32), custom_call_target="tpu_custom_call" | custom-call | tf_op jit(solution)/shard_map/pallas_call | solution.py:112
  58.8 10.3 %all-to-all-start.2 = ((bf16[32,64,256]{2,1,0:T(8,128)(2,1)}), bf16[32,64,256]{2,1,0:T(8,128)(2,1)S(1)}, u32[]{:S(2)}, u32[]{:S(2)}) async-start(bf16[32,64,256]{2,1,0:T(8,128)(2,1)} %bitcast.16), calls=%async_computation.2 | async-start | bytes 2097152 | tf_op jit(solution)/shard_map/all_to_all | solution.py:185
  69.1 0.1 slice_reduce_fusion
  69.2 28.2 %all-to-all-done.2 = bf16[32,64,256]{2,1,0:T(8,128)(2,1)S(1)} async-done(((bf16[32,64,256]{2,1,0:T(8,128)(2,1)}), bf16[32,64,256]{2,1,0:T(8,128)(2,1)S(1)}, u32[]{:S(2)}, u32[]{:S(2)}) %all-to-all-start.2) | async-done | bytes 1048608 | tf_op jit(solution)/shard_map/all_to_all | solution.py:185
  97.4 0.2 reduce_sum.34
  97.6 25.9 %all_to_all.20 = bf16[8,96,256]{2,1,0:T(8,128)(2,1)S(1)} all-to-all(bf16[8,96,256]{2,1,0:T(8,128)(2,1)S(1)} %broadcast_in_dim.54), channel_id=1, replica_groups=mesh['rep'=8,'seq'=64] {'rep'}, dimensions={0} | all-to-all | bytes 786432 | tf_op jit(solution)/shard_map/all_to_all | solution.py:195
  123.6 0.8 convolution_multiply_fusion
  (21 shorter events, 0.3 us)
Async XLA Ops:
  0.6 7.8 %copy-start = (bf16[256,128]{1,0:T(8,128)(2,1)S(1)}, bf16[256,128]{1,0:T(8,128)(2,1)}, u32[]{:S(2)}) copy-start(bf16[256,128]{1,0:T(8,128)(2,1)} %param.13) | copy-start | bytes 196612
  1.7 38.9 %collective-permute-start.1 = (bf16[128,1024]{1,0:T(8,128)(2,1)S(1)}, bf16[128,1024]{1,0:T(8,128)(2,1)S(1)}, u32[]{:S(2)}, u32[]{:S(2)}) collective-permute-start(bf16[128,1024]{1,0:T(8,128)(2,1)S(1)} %pad_maximum_fusion.own_ref), channel_id=1, source_target_pairs={{0,2},{1,3},{2,4},{3,5},{4,6},{5,7},{6,8},{7,9},{8,10},{9,11},{10,... | collective-permute-start | bytes 786440 | tf_op jit(solution)/shard_map/ppermute | solution.py:26
  5.2 35.4 %collective-permute-start = (bf16[128,1024]{1,0:T(8,128)(2,1)S(1)}, bf16[128,1024]{1,0:T(8,128)(2,1)S(1)}, u32[]{:S(2)}, u32[]{:S(2)}) collective-permute-start(bf16[128,1024]{1,0:T(8,128)(2,1)S(1)} %pad_maximum_fusion.own_ref), channel_id=1, source_target_pairs={{0,1},{1,2},{2,3},{3,4},{4,5},{5,6},{6,7},{7,8},{8,9},{9,10},{10,1... | collective-permute-start | bytes 786440 | tf_op jit(solution)/shard_map/ppermute | solution.py:26
  7.7 0.7 copy-start.3
  8.5 0.8 copy-start.2
  10.2 30.4 %copy-start.1 = (bf16[1,128,4096]{2,1,0:T(8,128)(2,1)S(1)}, bf16[1,128,4096]{2,1,0:T(8,128)(2,1)}, u32[]{:S(2)}) copy-start(bf16[1,128,4096]{2,1,0:T(8,128)(2,1)} %param.7) | copy-start | bytes 3145732
  10.2 21.8 %all-to-all-start = ((bf16[64,4,256]{2,1,0:T(4,128)(2,1)}), bf16[64,4,256]{2,1,0:T(4,128)(2,1)S(1)}, u32[]{:S(2)}, u32[]{:S(2)}) async-start(bf16[64,4,256]{2,1,0:T(4,128)(2,1)} %maximum_maximum_fusion.1), calls=%async_computation | async-start | bytes 262144 | tf_op jit(solution)/shard_map/all_to_all | solution.py:149
  34.6 18.7 %all-to-all-start.1 = ((bf16[64,4,384]{2,1,0:T(4,128)(2,1)}), bf16[64,4,384]{2,1,0:T(4,128)(2,1)S(1)}, u32[]{:S(2)}, u32[]{:S(2)}) async-start(bf16[64,4,384]{2,1,0:T(4,128)(2,1)} %copy.29), calls=%async_computation.1 | async-start | bytes 393216 | tf_op jit(solution)/shard_map/all_to_all | solution.py:163
  51.2 3.8 %collective-permute-start.2 = (bf16[2048,128]{1,0:T(8,128)(2,1)S(1)}, bf16[2048,128]{1,0:T(8,128)(2,1)S(1)}, u32[]{:S(2)}, u32[]{:S(2)}) collective-permute-start(bf16[2048,128]{1,0:T(8,128)(2,1)S(1)} %get-tuple-element.7), channel_id=1, source_target_pairs={{0,1},{1,0},{2,3},{3,2},{4,5},{5,4},{6,7},{7,6},{8,9},{9,8},{10,11... | collective-permute-start | bytes 1572872 | tf_op jit(solution)/shard_map/ppermute | solution.py:30
  58.8 38.6 %all-to-all-start.2 = ((bf16[32,64,256]{2,1,0:T(8,128)(2,1)}), bf16[32,64,256]{2,1,0:T(8,128)(2,1)S(1)}, u32[]{:S(2)}, u32[]{:S(2)}) async-start(bf16[32,64,256]{2,1,0:T(8,128)(2,1)} %bitcast.16), calls=%async_computation.2 | async-start | bytes 2097152 | tf_op jit(solution)/shard_map/all_to_all | solution.py:185

commit v2 on v0

v2 whole, which is shorter than its diff:
```python
import math

import jax
import jax.numpy as jnp
from jax import lax
from jax.experimental import pallas as pl
from jax.experimental.pallas import tpu as pltpu
from jax.sharding import PartitionSpec as P

QUERY_HEADS = 32
KEY_VALUE_HEADS = 4
HEAD_SIZE = 128
GROUP = QUERY_HEADS // KEY_VALUE_HEADS
KV = KEY_VALUE_HEADS * HEAD_SIZE
TOKENS = 128
R = 256
SEQ = 64
REP = 8
HALF = HEAD_SIZE // 2
LOG2E = math.log2(math.e)
VMEM_LIMIT = 48 * 1024 * 1024
NT = (((1,), (1,)), ((), ()))

MEMBERS = 4
SHARES = SEQ // MEMBERS
FOURS = [
    [z2 * 32 + zp * 16 + y * 2 + c for zp in range(2) for c in range(2)]
    for z2 in range(2)
    for y in range(8)
]
SIXTEENS = [list(column) for column in zip(*FOURS)]


def shifted(block, distance):
    return lax.ppermute(block, "seq", [(i, i + distance) for i in range(SEQ - distance)])


def exchange(block, axis, groups=None):
    return lax.all_to_all(
        block, axis, split_axis=0, concat_axis=0, axis_index_groups=groups, tiled=True
    )


def attention_kernel(q_ref, own_ref, one_ref, two_ref, tag_ref, out_ref, parts_ref):
    square = (TOKENS, TOKENS)
    query_tags = jnp.broadcast_to(tag_ref[...].astype(jnp.float32), square) + 1.0
    lower = lax.broadcasted_iota(jnp.int32, square, 0) <= lax.broadcasted_iota(jnp.int32, square, 1)
    tags = lambda block: block[:, 2 * KV :].astype(jnp.float32)
    wide = lambda mask: jnp.concatenate([mask] * GROUP, axis=1)
    seen_edge = wide(jnp.where(lower, tags(own_ref), tags(two_ref)) == query_tags)
    seen_one = wide(tags(one_ref) == query_tags)
    lower = wide(lower)
    hidden = jnp.float32(-1e30)
    factor = HEAD_SIZE ** (-0.5) * LOG2E
    for g in range(KEY_VALUE_HEADS):
        at = g * HEAD_SIZE
        turned = [
            b[:, KV + at : KV + at + HEAD_SIZE].astype(jnp.float32).T.astype(jnp.bfloat16)
            for b in (own_ref, one_ref, two_ref)
        ]
        q = jnp.concatenate(
            [
                q_ref[:, h * HEAD_SIZE : (h + 1) * HEAD_SIZE]
                for h in range(g * GROUP, (g + 1) * GROUP)
            ],
            axis=0,
        )
        score = lambda b: lax.dot_general(
            b[:, at : at + HEAD_SIZE], q, NT, preferred_element_type=jnp.float32
        )
        edge = jnp.where(seen_edge, jnp.where(lower, score(own_ref), score(two_ref)), hidden)
        one = jnp.where(seen_one, score(one_ref), hidden)
        highest = jnp.max(jnp.maximum(edge, one), axis=0, keepdims=True)
        edge = jnp.exp2((edge - highest) * factor)
        one = jnp.exp2((one - highest) * factor)
        inverse = 1.0 / jnp.sum(edge + one, axis=0, keepdims=True)
        edge = edge * inverse
        weights = jnp.concatenate(
            [
                jnp.where(lower, edge, 0.0).astype(jnp.bfloat16),
                (one * inverse).astype(jnp.bfloat16),
                jnp.where(lower, 0.0, edge).astype(jnp.bfloat16),
            ],
            axis=0,
        )
        mixed = jnp.dot(
            jnp.concatenate(turned, axis=1), weights, preferred_element_type=jnp.float32
        )
        for j in range(GROUP):
            h = g * GROUP + j
            head = mixed[:, j * HEAD_SIZE : (j + 1) * HEAD_SIZE]
            out_ref[:, h * HEAD_SIZE : (h + 1) * HEAD_SIZE] = head.T.astype(jnp.bfloat16)
            z, y = h // 8, h % 8
            row = ((z // 2) * 8 + y) * HALF
            parts_ref[(z % 2) * 2, row : row + HALF, :] = head[:HALF].astype(jnp.bfloat16)
            parts_ref[(z % 2) * 2 + 1, row : row + HALF, :] = head[HALF:].astype(jnp.bfloat16)


def attention(q, own, one, two, tag):
    vmem = pl.BlockSpec(memory_space=pltpu.VMEM)
    return pl.pallas_call(
        attention_kernel,
        out_shape=(
            jax.ShapeDtypeStruct((TOKENS, QUERY_HEADS * HEAD_SIZE), jnp.bfloat16),
            jax.ShapeDtypeStruct((MEMBERS, SHARES * HALF, TOKENS), jnp.bfloat16),
        ),
        in_specs=[vmem] * 5,
        out_specs=(vmem, vmem),
        compiler_params=pltpu.CompilerParams(vmem_limit_bytes=VMEM_LIMIT),
        cost_estimate=pl.CostEstimate(
            flops=4 * QUERY_HEADS * TOKENS * 3 * TOKENS * HEAD_SIZE * 6,
            bytes_accessed=4 << 20,
            transcendentals=QUERY_HEADS * TOKENS * 2 * TOKENS,
        ),
    )(q, own, one, two, tag)


def outer_kernel(parts_ref, coeffs_ref, out_ref):
    total = jnp.zeros(out_ref.shape, jnp.float32)
    for m in range(MEMBERS):
        total += lax.dot_general(
            parts_ref[m], coeffs_ref[m], NT, preferred_element_type=jnp.float32
        )
    out_ref[...] = total.astype(jnp.bfloat16)


def outer(parts, coeffs):
    rows = parts.shape[1]
    step = rows // 2
    return pl.pallas_call(
        outer_kernel,
        out_shape=jax.ShapeDtypeStruct((rows, R), jnp.bfloat16),
        grid=(rows // step,),
        in_specs=[
            pl.BlockSpec((MEMBERS, step, TOKENS), lambda i: (0, i, 0)),
            pl.BlockSpec((MEMBERS, R, TOKENS), lambda i: (0, 0, 0)),
        ],
        out_specs=pl.BlockSpec((step, R), lambda i: (i, 0)),
        compiler_params=pltpu.CompilerParams(vmem_limit_bytes=VMEM_LIMIT),
    )(parts, coeffs)


def local(queries, keys, values, doc_ids, coeffs, shard_dest, basis):
    rep = lax.axis_index("rep")
    bf16 = jnp.bfloat16

    numbers = jnp.broadcast_to((doc_ids[0] + 1).astype(bf16)[:, None], (TOKENS, TOKENS))
    own = jnp.concatenate([keys[0], values[0], numbers], axis=1)
    two = shifted(own, 2)
    one = shifted(own, 1)

    gram_rows = R // REP
    basis_rows = lax.dynamic_slice_in_dim(basis, rep * gram_rows, gram_rows, 0)
    gram = lax.dot_general(basis_rows, basis, NT, preferred_element_type=jnp.float32)
    extra = jnp.concatenate(
        [
            gram.astype(bf16).reshape(SEQ, 1, TOKENS),
            jnp.broadcast_to(shard_dest[0, 0].astype(bf16), (SEQ, 3, TOKENS)),
        ],
        axis=1,
    )
    first = exchange(jnp.concatenate([coeffs[0].T.reshape(SEQ, 4, TOKENS), extra], axis=2), "seq")

    attended, parts = attention(queries[0], own, one, two, doc_ids)
    parts, first = lax.optimization_barrier((parts, first))
    parts = exchange(parts, "seq", FOURS)

    dest = first[:, 1, TOKENS].astype(jnp.int32)
    device = lax.broadcasted_iota(jnp.int32, (SEQ, SEQ), 0)
    lowest = (device & 32) | (device & 14)
    sorted_pieces = [
        jnp.einsum(
            "bj,jit->bit",
            (dest[None, :] == lowest + (m // 2 * 16 + m % 2)).astype(bf16),
            first[:, :, :TOKENS],
            preferred_element_type=jnp.float32,
        ).astype(bf16)
        for m in range(MEMBERS)
    ]
    gram_piece = jnp.sum(first[:, 0, TOKENS:].astype(jnp.float32), axis=0).astype(bf16)
    second = exchange(
        jnp.concatenate(sorted_pieces + [jnp.broadcast_to(gram_piece, (SEQ, 4, TOKENS))], axis=2),
        "seq",
    )

    lined = jnp.stack(
        [second[:, :, m * TOKENS : (m + 1) * TOKENS].reshape(R, TOKENS) for m in range(MEMBERS)]
    )
    partial = outer(parts, lined).reshape(SHARES, HALF, R)
    arrived = exchange(partial, "seq", SIXTEENS)
    rows = jnp.sum(arrived.astype(jnp.float32), axis=0).astype(bf16)
    gram_share = second[:, 0, MEMBERS * TOKENS :].reshape(gram_rows, R)
    last = exchange(
        jnp.broadcast_to(jnp.concatenate([rows, gram_share], axis=0), (REP, HALF + gram_rows, R)),
        "rep",
    )
    summed = jnp.sum(last[:, :HALF].astype(jnp.float32), axis=0)
    gram_all = last[:, HALF:].reshape(R, R).astype(jnp.float32)
    grad = jnp.dot(summed, gram_all, precision=lax.Precision.HIGHEST)
    grad = grad * (1.0 / math.sqrt(REP * SEQ * TOKENS))
    return attended[None], grad


def solution(mesh):
    in_specs = (
        P("rep", "seq", None),
        P("rep", "seq", None),
        P("rep", "seq", None),
        P("rep", "seq"),
        P("rep", "seq", None),
        P("rep", "seq"),
        P(None, "seq"),
    )
    out_specs = (P("rep", "seq", None), P("seq", None))
    return jax.shard_map(local, mesh=mesh, in_specs=in_specs, out_specs=out_specs, check_vma=False)
```

time: 629 us -> 120 us (0.19)
  the two profiles are of different devices: /device:TPU:8 before, /device:TPU:136 now
where the time goes in v2:
time: 120 us; the launch traced here: 119 us
  blocking collectives  44.5 us (37%)
  waiting for transfers between devices  33.2 us (28%)
  starting transfers between devices  26.1 us (22%)
  Pallas kernels  5.91 us (5%)
  other arithmetic  3.96 us (3%)
  local copies, waits for them, and re-layouts  2.23 us (2%)
  matrix products  1.82 us (2%)
  between operations  1.51 us (1%)
    all_to_all x2, blocking collectives, exchange(): lax.all_to_all(block, axis, split_axis=0, concat_axis=0, axis_index_group...  44.5 us
    all_to_all x3, waiting for transfers between devices, exchange(): lax.all_to_all(block, axis, split_axis=0, concat_axis=0, axis_index_group...  33.2 us
    all_to_all x3, starting transfers between devices, exchange(): lax.all_to_all(block, axis, split_axis=0, concat_axis=0, axis_index_group...  20.7 us
    ppermute x2, starting transfers between devices, shifted(): lax.ppermute(block, 'seq', [(i, i + distance) for i in range(SEQ - distan...  5.41 us
    pallas_call x1, Pallas kernels, attention(): pl.pallas_call(attention_kernel, out_shape=(jax.ShapeDtypeStruct((TOKENS,...  4.24 us
  transfers between devices with their start and end apart: 5, of which 3 were waited for; matrix products, arithmetic and copies ran while one was open for 2% of the time, Pallas kernels for 4%

profile of v2, /device:TPU:136, one launch (start us, length us, event | category | flops | bytes accessed | tf_op | source)
XLA Modules:
  0.0 119.3 jit_solution(5345775369055450061)
XLA Ops:
  0.6 0.0 copy-start
  0.6 0.0 copy-start.1
  0.7 0.8 convert_bitcast_fusion
  1.4 0.1 broadcast_in_dim.8
  1.5 1.0 pad_maximum_fusion.own_ref
  2.5 3.5 %collective-permute-start.1 = (bf16[128,1152]{1,0:T(8,128)(2,1)S(1)}, bf16[128,1152]{1,0:T(8,128)(2,1)S(1)}, u32[]{:S(2)}, u32[]{:S(2)}) collective-permute-start(bf16[128,1152]{1,0:T(8,128)(2,1)S(1)} %pad_maximum_fusion.own_ref), channel_id=1, source_target_pairs={{0,2},{1,3},{2,4},{3,5},{4,6},{5,7},{6,8},{7,9},{8,10},{9,11},{10,... | collective-permute-start | bytes 884744 | tf_op jit(solution)/shard_map/ppermute | solution.py:35
  6.0 1.9 %collective-permute-start = (bf16[128,1152]{1,0:T(8,128)(2,1)S(1)}, bf16[128,1152]{1,0:T(8,128)(2,1)S(1)}, u32[]{:S(2)}, u32[]{:S(2)}) collective-permute-start(bf16[128,1152]{1,0:T(8,128)(2,1)S(1)} %pad_maximum_fusion.own_ref), channel_id=1, source_target_pairs={{0,1},{1,2},{2,3},{3,4},{4,5},{5,6},{6,7},{7,8},{8,9},{9,10},{10,1... | collective-permute-start | bytes 884744 | tf_op jit(solution)/shard_map/ppermute | solution.py:35
  8.6 0.0 copy-done
  8.6 0.1 convolution_convert_fusion.4
  8.7 1.0 copy.27
  9.7 0.7 fusion.5
  10.4 11.3 %all-to-all-start = ((bf16[64,4,256]{2,1,0:T(4,128)(2,1)}), bf16[64,4,256]{2,1,0:T(4,128)(2,1)S(1)}, u32[]{:S(2)}, u32[]{:S(2)}) async-start(bf16[64,4,256]{2,1,0:T(4,128)(2,1)} %fusion.5), calls=%async_computation | async-start | bytes 262144 | tf_op jit(solution)/shard_map/all_to_all | solution.py:39
  21.8 0.0 copy-start.2
  21.8 0.0 collective-permute-done.1.two_ref
  21.8 0.0 collective-permute-done.one_ref
  21.8 0.0 copy-done.1
  21.8 0.6 copy-done.2
  22.4 4.2 %shard_map.86 = (bf16[128,4096]{1,0:T(8,128)(2,1)}, bf16[4,1024,128]{2,1,0:T(8,128)(2,1)}) custom-call(bf16[128,4096]{1,0:T(8,128)(2,1)S(1)} %bitcast.33, bf16[128,1152]{1,0:T(8,128)(2,1)S(1)} %pad_maximum_fusion.own_ref, bf16[128,1152]{1,0:T(8,128)(2,1)S(1)} %collective-permute-done.one_ref, bf16[128,1152]{1,0:T(8,128)(2,1)S(1)} %collective-permute-done.1.two_ref, ...), custom_call_target="tpu_custom_call" | custom-call | flops 4831838208 | bytes 4194304 | tf_op jit(solution)/shard_map/pallas_call | solution.py:101
  26.7 4.0 %all-to-all-done = bf16[64,4,256]{2,1,0:T(4,128)(2,1)S(1)} async-done(((bf16[64,4,256]{2,1,0:T(4,128)(2,1)}), bf16[64,4,256]{2,1,0:T(4,128)(2,1)S(1)}, u32[]{:S(2)}, u32[]{:S(2)}) %all-to-all-start) | async-done | bytes 131104 | tf_op jit(solution)/shard_map/all_to_all | solution.py:39
  30.7 1.2 %convert_reduce_fusion.1 = s32[64]{0:T(128)S(1)} fusion(bf16[64,4,256]{2,1,0:T(4,128)(2,1)S(1)} %all-to-all-done), kind=kLoop, calls=%fused_computation.22 | loop fusion | flops 64 | bytes 384 | tf_op jit(solution)/shard_map/convert_element_type | solution.py:168
  31.9 0.1 slice_reduce_fusion.1
  32.0 0.2 fusion.3
  32.2 0.2 fusion.2
  32.4 0.2 fusion.1
  32.6 0.2 fusion
  32.9 0.3 copy.30
  33.2 19.2 %all_to_all.25 = bf16[64,4,640]{2,1,0:T(4,128)(2,1)S(1)} all-to-all(bf16[64,4,640]{2,1,0:T(4,128)(2,1)S(1)} %copy.30), channel_id=1, replica_groups=mesh['rep'=8,'seq'=64] {'seq'}, dimensions={0} | all-to-all | bytes 655360 | tf_op jit(solution)/shard_map/all_to_all | solution.py:39
  52.3 3.5 %all-to-all-start.1 = ((bf16[4,1024,128]{2,1,0:T(8,128)(2,1)}), bf16[4,1024,128]{2,1,0:T(8,128)(2,1)S(1)}, u32[]{:S(2)}, u32[]{:S(2)}) async-start(bf16[4,1024,128]{2,1,0:T(8,128)(2,1)} %get-tuple-element.8), calls=%async_computation.1 | async-start | bytes 2097152 | tf_op jit(solution)/shard_map/all_to_all | solution.py:39
  55.8 0.1 fusion.29
  56.0 14.3 %all-to-all-done.1.parts_ref = bf16[4,1024,128]{2,1,0:T(8,128)(2,1)S(1)} async-done(((bf16[4,1024,128]{2,1,0:T(8,128)(2,1)}), bf16[4,1024,128]{2,1,0:T(8,128)(2,1)S(1)}, u32[]{:S(2)}, u32[]{:S(2)}) %all-to-all-start.1) | async-done | bytes 1048608 | tf_op jit(solution)/shard_map/all_to_all | solution.py:39
  70.3 1.7 %shard_map.87 = bf16[1024,256]{1,0:T(8,128)(2,1)} custom-call(bf16[4,1024,128]{2,1,0:T(8,128)(2,1)S(1)} %all-to-all-done.1.parts_ref, bf16[4,256,128]{2,1,0:T(8,128)(2,1)S(1)} %pad_maximum_fusion.1.coeffs_ref), custom_call_target="tpu_custom_call" | custom-call | tf_op jit(solution)/shard_map/pallas_call | solution.py:130
  71.9 5.9 %all-to-all-start.3 = ((bf16[16,64,256]{2,1,0:T(8,128)(2,1)}), bf16[16,64,256]{2,1,0:T(8,128)(2,1)S(1)}, u32[]{:S(2)}, u32[]{:S(2)}) async-start(bf16[16,64,256]{2,1,0:T(8,128)(2,1)} %bitcast.17), calls=%async_computation.3 | async-start | bytes 1048576 | tf_op jit(solution)/shard_map/all_to_all | solution.py:39
  77.8 0.1 slice_reduce_fusion
  77.9 15.0 %all-to-all-done.3 = bf16[16,64,256]{2,1,0:T(8,128)(2,1)S(1)} async-done(((bf16[16,64,256]{2,1,0:T(8,128)(2,1)}), bf16[16,64,256]{2,1,0:T(8,128)(2,1)S(1)}, u32[]{:S(2)}, u32[]{:S(2)}) %all-to-all-start.3) | async-done | bytes 524320 | tf_op jit(solution)/shard_map/all_to_all | solution.py:39
  92.9 0.1 reduce_sum.34
  93.0 25.3 %all_to_all.26 = bf16[8,96,256]{2,1,0:T(8,128)(2,1)S(1)} all-to-all(bf16[8,96,256]{2,1,0:T(8,128)(2,1)S(1)} %broadcast_in_dim.11), channel_id=1, replica_groups=mesh['rep'=8,'seq'=64] {'rep'}, dimensions={0} | all-to-all | bytes 786432 | tf_op jit(solution)/shard_map/all_to_all | solution.py:39
  118.4 0.8 convolution_multiply_fusion
  (13 shorter events, 0.2 us)
Async XLA Ops:
  0.6 7.9 %copy-start = (bf16[256,128]{1,0:T(8,128)(2,1)S(1)}, bf16[256,128]{1,0:T(8,128)(2,1)}, u32[]{:S(2)}) copy-start(bf16[256,128]{1,0:T(8,128)(2,1)} %param.13) | copy-start | bytes 196612
  0.6 21.2 %copy-start.1 = (bf16[1,128,4096]{2,1,0:T(8,128)(2,1)S(1)}, bf16[1,128,4096]{2,1,0:T(8,128)(2,1)}, u32[]{:S(2)}) copy-start(bf16[1,128,4096]{2,1,0:T(8,128)(2,1)} %param.7) | copy-start | bytes 3145732
  2.5 19.3 %collective-permute-start.1 = (bf16[128,1152]{1,0:T(8,128)(2,1)S(1)}, bf16[128,1152]{1,0:T(8,128)(2,1)S(1)}, u32[]{:S(2)}, u32[]{:S(2)}) collective-permute-start(bf16[128,1152]{1,0:T(8,128)(2,1)S(1)} %pad_maximum_fusion.own_ref), channel_id=1, source_target_pairs={{0,2},{1,3},{2,4},{3,5},{4,6},{5,7},{6,8},{7,9},{8,10},{9,11},{10,... | collective-permute-start | bytes 884744 | tf_op jit(solution)/shard_map/ppermute | solution.py:35
  6.0 15.8 %collective-permute-start = (bf16[128,1152]{1,0:T(8,128)(2,1)S(1)}, bf16[128,1152]{1,0:T(8,128)(2,1)S(1)}, u32[]{:S(2)}, u32[]{:S(2)}) collective-permute-start(bf16[128,1152]{1,0:T(8,128)(2,1)S(1)} %pad_maximum_fusion.own_ref), channel_id=1, source_target_pairs={{0,1},{1,2},{2,3},{3,4},{4,5},{5,6},{6,7},{7,8},{8,9},{9,10},{10,1... | collective-permute-start | bytes 884744 | tf_op jit(solution)/shard_map/ppermute | solution.py:35
  10.4 20.2 %all-to-all-start = ((bf16[64,4,256]{2,1,0:T(4,128)(2,1)}), bf16[64,4,256]{2,1,0:T(4,128)(2,1)S(1)}, u32[]{:S(2)}, u32[]{:S(2)}) async-start(bf16[64,4,256]{2,1,0:T(4,128)(2,1)} %fusion.5), calls=%async_computation | async-start | bytes 262144 | tf_op jit(solution)/shard_map/all_to_all | solution.py:39
  21.8 0.7 copy-start.2
  52.3 18.0 %all-to-all-start.1 = ((bf16[4,1024,128]{2,1,0:T(8,128)(2,1)}), bf16[4,1024,128]{2,1,0:T(8,128)(2,1)S(1)}, u32[]{:S(2)}, u32[]{:S(2)}) async-start(bf16[4,1024,128]{2,1,0:T(8,128)(2,1)} %get-tuple-element.8), calls=%async_computation.1 | async-start | bytes 2097152 | tf_op jit(solution)/shard_map/all_to_all | solution.py:39
  71.9 21.0 %all-to-all-start.3 = ((bf16[16,64,256]{2,1,0:T(8,128)(2,1)}), bf16[16,64,256]{2,1,0:T(8,128)(2,1)S(1)}, u32[]{:S(2)}, u32[]{:S(2)}) async-start(bf16[16,64,256]{2,1,0:T(8,128)(2,1)} %bitcast.17), calls=%async_computation.3 | async-start | bytes 1048576 | tf_op jit(solution)/shard_map/all_to_all | solution.py:39

commit v3 on v2

--- a/solution.py
+++ b/solution.py
@@ -21,18 +21,22 @@
 VMEM_LIMIT = 48 * 1024 * 1024
 NT = (((1,), (1,)), ((), ()))
 
-MEMBERS = 4
+PARTNERS = (0, 1, 16, 17)
+MEMBERS = len(PARTNERS)
 SHARES = SEQ // MEMBERS
-FOURS = [
-    [z2 * 32 + zp * 16 + y * 2 + c for zp in range(2) for c in range(2)]
-    for z2 in range(2)
-    for y in range(8)
+SIXTEENS = [
+    [z2 * 32 + zp * 16 + y * 2 + c for z2 in range(2) for y in range(8)]
+    for zp in range(2)
+    for c in range(2)
 ]
-SIXTEENS = [list(column) for column in zip(*FOURS)]
 
 
 def shifted(block, distance):
     return lax.ppermute(block, "seq", [(i, i + distance) for i in range(SEQ - distance)])
+
+
+def swapped(block, partner):
+    return lax.ppermute(block, "seq", [(i, i ^ partner) for i in range(SEQ)])
 
 
 def exchange(block, axis, groups=None):
@@ -41,7 +45,10 @@
     )
 
 
-def attention_kernel(q_ref, own_ref, one_ref, two_ref, tag_ref, out_ref, parts_ref):
+def attention_kernel(
+    place_ref, q_ref, own_ref, one_ref, two_ref, tag_ref, out_ref, *part_refs
+):
+    core, odd = place_ref[0], place_ref[1]
     square = (TOKENS, TOKENS)
     query_tags = jnp.broadcast_to(tag_ref[...].astype(jnp.float32), square) + 1.0
     lower = lax.broadcasted_iota(jnp.int32, square, 0) <= lax.broadcasted_iota(jnp.int32, square, 1)
@@ -52,21 +59,19 @@
     lower = wide(lower)
     hidden = jnp.float32(-1e30)
     factor = HEAD_SIZE ** (-0.5) * LOG2E
-    for g in range(KEY_VALUE_HEADS):
-        at = g * HEAD_SIZE
+    column = lambda start: pl.ds(pl.multiple_of(start, HEAD_SIZE), HEAD_SIZE)
+    for step in range(KEY_VALUE_HEADS):
+        other, z2 = step // 2, step % 2
+        z = z2 * 2 + (odd if other == 0 else 1 - odd)
+        at = z * HEAD_SIZE
         turned = [
-            b[:, KV + at : KV + at + HEAD_SIZE].astype(jnp.float32).T.astype(jnp.bfloat16)
+            b[:, column(KV + at)].astype(jnp.float32).T.astype(jnp.bfloat16)
             for b in (own_ref, one_ref, two_ref)
         ]
-        q = jnp.concatenate(
-            [
-                q_ref[:, h * HEAD_SIZE : (h + 1) * HEAD_SIZE]
-                for h in range(g * GROUP, (g + 1) * GROUP)
-            ],
-            axis=0,
-        )
+        heads = [(z * GROUP + j) * HEAD_SIZE for j in range(GROUP)]
+        q = jnp.concatenate([q_ref[:, column(h)] for h in heads], axis=0)
         score = lambda b: lax.dot_general(
-            b[:, at : at + HEAD_SIZE], q, NT, preferred_element_type=jnp.float32
+            b[:, column(at)], q, NT, preferred_element_type=jnp.float32
         )
         edge = jnp.where(seen_edge, jnp.where(lower, score(own_ref), score(two_ref)), hidden)
         one = jnp.where(seen_one, score(one_ref), hidden)
@@ -87,57 +92,56 @@
             jnp.concatenate(turned, axis=1), weights, preferred_element_type=jnp.float32
         )
         for j in range(GROUP):
-            h = g * GROUP + j
             head = mixed[:, j * HEAD_SIZE : (j + 1) * HEAD_SIZE]
-            out_ref[:, h * HEAD_SIZE : (h + 1) * HEAD_SIZE] = head.T.astype(jnp.bfloat16)
-            z, y = h // 8, h % 8
-            row = ((z // 2) * 8 + y) * HALF
-            parts_ref[(z % 2) * 2, row : row + HALF, :] = head[:HALF].astype(jnp.bfloat16)
-            parts_ref[(z % 2) * 2 + 1, row : row + HALF, :] = head[HALF:].astype(jnp.bfloat16)
-
-
-def attention(q, own, one, two, tag):
+            out_ref[:, column(heads[j])] = head.T.astype(jnp.bfloat16)
+            low, high = head[:HALF], head[HALF:]
+            row = (z2 * 8 + j) * HALF
+            part_refs[other * 2][row : row + HALF, :] = jnp.where(core == 0, low, high).astype(
+                jnp.bfloat16
+            )
+            part_refs[other * 2 + 1][row : row + HALF, :] = jnp.where(core == 0, high, low).astype(
+                jnp.bfloat16
+            )
+
+
+def attention(place, q, own, one, two, tag):
     vmem = pl.BlockSpec(memory_space=pltpu.VMEM)
     return pl.pallas_call(
         attention_kernel,
-        out_shape=(
-            jax.ShapeDtypeStruct((TOKENS, QUERY_HEADS * HEAD_SIZE), jnp.bfloat16),
-            jax.ShapeDtypeStruct((MEMBERS, SHARES * HALF, TOKENS), jnp.bfloat16),
-        ),
-        in_specs=[vmem] * 5,
-        out_specs=(vmem, vmem),
+        out_shape=[jax.ShapeDtypeStruct((TOKENS, QUERY_HEADS * HEAD_SIZE), jnp.bfloat16)]
+        + [jax.ShapeDtypeStruct((SHARES * HALF, TOKENS), jnp.bfloat16)] * MEMBERS,
+        in_specs=[pl.BlockSpec(memory_space=pltpu.SMEM)] + [vmem] * 5,
+        out_specs=[vmem] * (1 + MEMBERS),
         compiler_params=pltpu.CompilerParams(vmem_limit_bytes=VMEM_LIMIT),
         cost_estimate=pl.CostEstimate(
             flops=4 * QUERY_HEADS * TOKENS * 3 * TOKENS * HEAD_SIZE * 6,
             bytes_accessed=4 << 20,
             transcendentals=QUERY_HEADS * TOKENS * 2 * TOKENS,
         ),
-    )(q, own, one, two, tag)
-
-
-def outer_kernel(parts_ref, coeffs_ref, out_ref):
-    total = jnp.zeros(out_ref.shape, jnp.float32)
+    )(place, q, own, one, two, tag)
+
+
+def outer_kernel(coeffs_ref, *refs):
+    total = jnp.zeros(refs[-1].shape, jnp.float32)
     for m in range(MEMBERS):
         total += lax.dot_general(
-            parts_ref[m], coeffs_ref[m], NT, preferred_element_type=jnp.float32
-        )
-    out_ref[...] = total.astype(jnp.bfloat16)
-
-
-def outer(parts, coeffs):
-    rows = parts.shape[1]
+            refs[m][...], coeffs_ref[m], NT, preferred_element_type=jnp.float32
+        )
+    refs[-1][...] = total.astype(jnp.bfloat16)
+
+
+def outer(coeffs, parts):
+    rows = parts[0].shape[0]
     step = rows // 2
     return pl.pallas_call(
         outer_kernel,
         out_shape=jax.ShapeDtypeStruct((rows, R), jnp.bfloat16),
         grid=(rows // step,),
-        in_specs=[
-            pl.BlockSpec((MEMBERS, step, TOKENS), lambda i: (0, i, 0)),
-            pl.BlockSpec((MEMBERS, R, TOKENS), lambda i: (0, 0, 0)),
-        ],
+        in_specs=[pl.BlockSpec((MEMBERS, R, TOKENS), lambda i: (0, 0, 0))]
+        + [pl.BlockSpec((step, TOKENS), lambda i: (i, 0))] * MEMBERS,
         out_specs=pl.BlockSpec((step, R), lambda i: (i, 0)),
         compiler_params=pltpu.CompilerParams(vmem_limit_bytes=VMEM_LIMIT),
-    )(parts, coeffs)
+    )(coeffs, *parts)
 
 
 def local(queries, keys, values, doc_ids, coeffs, shard_dest, basis):
@@ -161,21 +165,22 @@
     )
     first = exchange(jnp.concatenate([coeffs[0].T.reshape(SEQ, 4, TOKENS), extra], axis=2), "seq")
 
-    attended, parts = attention(queries[0], own, one, two, doc_ids)
-    parts, first = lax.optimization_barrier((parts, first))
-    parts = exchange(parts, "seq", FOURS)
+    seq = lax.axis_index("seq").astype(jnp.int32)
+    place = jnp.stack([seq % 2, seq // 16 % 2])
+    attended, *parts = attention(place, queries[0], own, one, two, doc_ids)
+    first, parts[0] = lax.optimization_barrier((first, parts[0]))
+    parts = parts[:1] + [swapped(part, partner) for part, partner in zip(parts[1:], PARTNERS[1:])]
 
     dest = first[:, 1, TOKENS].astype(jnp.int32)
     device = lax.broadcasted_iota(jnp.int32, (SEQ, SEQ), 0)
-    lowest = (device & 32) | (device & 14)
     sorted_pieces = [
         jnp.einsum(
             "bj,jit->bit",
-            (dest[None, :] == lowest + (m // 2 * 16 + m % 2)).astype(bf16),
+            (dest[None, :] == (device ^ partner)).astype(bf16),
             first[:, :, :TOKENS],
             preferred_element_type=jnp.float32,
         ).astype(bf16)
-        for m in range(MEMBERS)
+        for partner in PARTNERS
     ]
     gram_piece = jnp.sum(first[:, 0, TOKENS:].astype(jnp.float32), axis=0).astype(bf16)
     second = exchange(
@@ -186,7 +191,7 @@
     lined = jnp.stack(
         [second[:, :, m * TOKENS : (m + 1) * TOKENS].reshape(R, TOKENS) for m in range(MEMBERS)]
     )
-    partial = outer(parts, lined).reshape(SHARES, HALF, R)
+    partial = outer(lined, parts).reshape(SHARES, HALF, R)
     arrived = exchange(partial, "seq", SIXTEENS)
     rows = jnp.sum(arrived.astype(jnp.float32), axis=0).astype(bf16)
     gram_share = second[:, 0, MEMBERS * TOKENS :].reshape(gram_rows, R)

time: 120 us -> 114 us (0.950)
  blocking collectives: 44.5 us -> 25.3 us
  starting transfers between devices: 26.1 us -> 39.6 us
  waiting for transfers between devices: 33.2 us -> 31.7 us
    all_to_all x2 -> x1, blocking collectives: 44.5 us -> 25.3 us  [exchange(): lax.all_to_all(block, axis, split_axis=0, concat_axis=0, axis_index_group...]
    all_to_all x3, waiting for transfers between devices: 33.2 us -> 23.8 us  [exchange(): lax.all_to_all(block, axis, split_axis=0, concat_axis=0, axis_index_group...]
    ppermute x0 -> x3, waiting for transfers between devices: none -> 7.88 us  [swapped(): return lax.ppermute(block, 'seq', [(i, i ^ partner) for i in range(SEQ)])]
    ppermute x0 -> x3, starting transfers between devices: none -> 7.59 us  [swapped(): return lax.ppermute(block, 'seq', [(i, i ^ partner) for i in range(SEQ)])]
    all_to_all x3, starting transfers between devices: 20.7 us -> 26.6 us  [exchange(): lax.all_to_all(block, axis, split_axis=0, concat_axis=0, axis_index_group...]
  transfers between devices with their start and end apart: 5 -> 8, of which waited for: 3 -> 5; matrix products, arithmetic and copies ran while one was open for 2% -> 2% of each run, Pallas kernels for 4% -> 4%
where the time goes in v3:
time: 114 us; the launch traced here: 113 us
  starting transfers between devices  39.6 us (35%)
  waiting for transfers between devices  31.7 us (28%)
  blocking collectives  25.3 us (22%)
  Pallas kernels  6.32 us (6%)
  other arithmetic  4.02 us (4%)
  local copies, waits for them, and re-layouts  2.96 us (3%)
  matrix products  1.77 us (2%)
  between operations  1.56 us (1%)
    all_to_all x3, starting transfers between devices, exchange(): lax.all_to_all(block, axis, split_axis=0, concat_axis=0, axis_index_group...  26.6 us
    all_to_all x1, blocking collectives, exchange(): lax.all_to_all(block, axis, split_axis=0, concat_axis=0, axis_index_group...  25.3 us
    all_to_all x3, waiting for transfers between devices, exchange(): lax.all_to_all(block, axis, split_axis=0, concat_axis=0, axis_index_group...  23.8 us
    ppermute x3, waiting for transfers between devices, swapped(): return lax.ppermute(block, 'seq', [(i, i ^ partner) for i in range(SEQ)])  7.88 us
    ppermute x3, starting transfers between devices, swapped(): return lax.ppermute(block, 'seq', [(i, i ^ partner) for i in range(SEQ)])  7.59 us
    ppermute x2, starting transfers between devices, shifted(): lax.ppermute(block, 'seq', [(i, i + distance) for i in range(SEQ - distan...  5.41 us
    pallas_call x1, Pallas kernels, attention(): pl.pallas_call(attention_kernel, out_shape=[jax.ShapeDtypeStruct((TOKENS,...  4.75 us
  transfers between devices with their start and end apart: 8, of which 5 were waited for; matrix products, arithmetic and copies ran while one was open for 2% of the time, Pallas kernels for 4%

profile of v3, /device:TPU:136, one launch (start us, length us, event | category | flops | bytes accessed | tf_op | source)
XLA Modules:
  0.0 113.2 jit_solution(18203226315086351489)
XLA Ops:
  0.6 0.0 copy-start
  0.6 0.0 copy-start.1
  0.7 0.8 convert_bitcast_fusion
  1.4 0.1 broadcast_in_dim.8
  1.5 1.0 pad_maximum_fusion.own_ref
  2.5 1.9 %collective-permute-start = (bf16[128,1152]{1,0:T(8,128)(2,1)S(1)}, bf16[128,1152]{1,0:T(8,128)(2,1)S(1)}, u32[]{:S(2)}, u32[]{:S(2)}) collective-permute-start(bf16[128,1152]{1,0:T(8,128)(2,1)S(1)} %pad_maximum_fusion.own_ref), channel_id=1, source_target_pairs={{0,1},{1,2},{2,3},{3,4},{4,5},{5,6},{6,7},{7,8},{8,9},{9,10},{10,1... | collective-permute-start | bytes 884744 | tf_op jit(solution)/shard_map/ppermute | solution.py:35
  4.4 3.5 %collective-permute-start.1 = (bf16[128,1152]{1,0:T(8,128)(2,1)S(1)}, bf16[128,1152]{1,0:T(8,128)(2,1)S(1)}, u32[]{:S(2)}, u32[]{:S(2)}) collective-permute-start(bf16[128,1152]{1,0:T(8,128)(2,1)S(1)} %pad_maximum_fusion.own_ref), channel_id=1, source_target_pairs={{0,2},{1,3},{2,4},{3,5},{4,6},{5,7},{6,8},{7,9},{8,10},{9,11},{10,... | collective-permute-start | bytes 884744 | tf_op jit(solution)/shard_map/ppermute | solution.py:35
  7.9 0.0 copy-done
  7.9 0.1 convolution_convert_fusion.4
  8.8 1.0 copy.27
  9.7 0.7 fusion.5
  10.4 11.0 %all-to-all-start = ((bf16[64,4,256]{2,1,0:T(4,128)(2,1)}), bf16[64,4,256]{2,1,0:T(4,128)(2,1)S(1)}, u32[]{:S(2)}, u32[]{:S(2)}) async-start(bf16[64,4,256]{2,1,0:T(4,128)(2,1)} %fusion.5), calls=%async_computation | async-start | bytes 262144 | tf_op jit(solution)/shard_map/all_to_all | solution.py:43
  21.5 0.1 pad_add_fusion.place_ref
  21.6 0.0 copy-start.2
  21.6 0.0 collective-permute-done.one_ref
  21.6 0.0 collective-permute-done.1.two_ref
  21.6 0.0 copy-done.1
  21.6 0.6 copy-done.2
  22.3 4.7 %shard_map.86 = (bf16[128,4096]{1,0:T(8,128)(2,1)}, bf16[1024,128]{1,0:T(8,128)(2,1)S(1)}, bf16[1024,128]{1,0:T(8,128)(2,1)S(1)}, bf16[1024,128]{1,0:T(8,128)(2,1)S(1)}, bf16[1024,128]{1,0:T(8,128)(2,1)S(1)}) custom-call(s32[2]{0:T(128)S(1)} %pad_add_fusion.place_ref, bf16[128,4096]{1,0:T(8,128)(2,1)S(1)} %bitcast.35, ...), custom_call_target="tpu_custom_call" | custom-call | flops 4831838208 | bytes 4194304 | tf_op jit(solution)/shard_map/pallas_call | solution.py:109
  27.0 3.4 %all-to-all-done = bf16[64,4,256]{2,1,0:T(4,128)(2,1)S(1)} async-done(((bf16[64,4,256]{2,1,0:T(4,128)(2,1)}), bf16[64,4,256]{2,1,0:T(4,128)(2,1)S(1)}, u32[]{:S(2)}, u32[]{:S(2)}) %all-to-all-start) | async-done | bytes 131104 | tf_op jit(solution)/shard_map/all_to_all | solution.py:43
  30.4 1.2 %convert_reduce_fusion.1 = s32[64]{0:T(128)S(1)} fusion(bf16[64,4,256]{2,1,0:T(4,128)(2,1)S(1)} %all-to-all-done), kind=kLoop, calls=%fused_computation.22 | loop fusion | flops 64 | bytes 384 | tf_op jit(solution)/shard_map/convert_element_type | solution.py:174
  31.6 0.1 slice_reduce_fusion.1
  31.7 0.2 fusion.3
  31.9 0.2 fusion.2
  32.1 0.2 fusion.1
  32.3 0.2 fusion
  32.6 1.0 copy.30
  33.5 7.4 %all-to-all-start.1 = ((bf16[64,4,640]{2,1,0:T(4,128)(2,1)}), bf16[64,4,640]{2,1,0:T(4,128)(2,1)S(1)}, u32[]{:S(2)}, u32[]{:S(2)}) async-start(bf16[64,4,640]{2,1,0:T(4,128)(2,1)} %copy.30), calls=%async_computation.1 | async-start | bytes 655360 | tf_op jit(solution)/shard_map/all_to_all | solution.py:43
  40.9 2.1 %collective-permute-start.2 = (bf16[1024,128]{1,0:T(8,128)(2,1)S(1)}, bf16[1024,128]{1,0:T(8,128)(2,1)S(1)}, u32[]{:S(2)}, u32[]{:S(2)}) collective-permute-start(bf16[1024,128]{1,0:T(8,128)(2,1)S(1)} %get-tuple-element.13), channel_id=1, source_target_pairs={{0,1},{1,0},{2,3},{3,2},{4,5},{5,4},{6,7},{7,6},{8,9},{9,8},{10,11... | collective-permute-start | bytes 786440 | tf_op jit(solution)/shard_map/ppermute | solution.py:39
  43.0 3.5 %collective-permute-start.3 = (bf16[1024,128]{1,0:T(8,128)(2,1)S(1)}, bf16[1024,128]{1,0:T(8,128)(2,1)S(1)}, u32[]{:S(2)}, u32[]{:S(2)}) collective-permute-start(bf16[1024,128]{1,0:T(8,128)(2,1)S(1)} %get-tuple-element.14), channel_id=1, source_target_pairs={{0,16},{1,17},{2,18},{3,19},{4,20},{5,21},{6,22},{7,23},{8,24},{9,... | collective-permute-start | bytes 786440 | tf_op jit(solution)/shard_map/ppermute | solution.py:39
  46.5 2.0 %collective-permute-start.4 = (bf16[1024,128]{1,0:T(8,128)(2,1)S(1)}, bf16[1024,128]{1,0:T(8,128)(2,1)S(1)}, u32[]{:S(2)}, u32[]{:S(2)}) collective-permute-start(bf16[1024,128]{1,0:T(8,128)(2,1)S(1)} %get-tuple-element.15), channel_id=1, source_target_pairs={{0,17},{1,16},{2,19},{3,18},{4,21},{5,20},{6,23},{7,22},{8,25},{9,... | collective-permute-start | bytes 786440 | tf_op jit(solution)/shard_map/ppermute | solution.py:39
  48.5 5.0 %all-to-all-done.1 = bf16[64,4,640]{2,1,0:T(4,128)(2,1)S(1)} async-done(((bf16[64,4,640]{2,1,0:T(4,128)(2,1)}), bf16[64,4,640]{2,1,0:T(4,128)(2,1)S(1)}, u32[]{:S(2)}, u32[]{:S(2)}) %all-to-all-start.1) | async-done | bytes 327712 | tf_op jit(solution)/shard_map/all_to_all | solution.py:43
  53.5 0.1 fusion.27
  53.7 0.0 collective-permute-done.2.refs_1_
  53.7 2.5 %collective-permute-done.3.refs_2_ = bf16[1024,128]{1,0:T(8,128)(2,1)S(1)} collective-permute-done((bf16[1024,128]{1,0:T(8,128)(2,1)S(1)}, bf16[1024,128]{1,0:T(8,128)(2,1)S(1)}, u32[]{:S(2)}, u32[]{:S(2)}) %collective-permute-start.3) | collective-permute-done | bytes 262176 | tf_op jit(solution)/shard_map/ppermute | solution.py:39
  56.2 5.3 %collective-permute-done.4.refs_3_ = bf16[1024,128]{1,0:T(8,128)(2,1)S(1)} collective-permute-done((bf16[1024,128]{1,0:T(8,128)(2,1)S(1)}, bf16[1024,128]{1,0:T(8,128)(2,1)S(1)}, u32[]{:S(2)}, u32[]{:S(2)}) %collective-permute-start.4) | collective-permute-done | bytes 262176 | tf_op jit(solution)/shard_map/ppermute | solution.py:39
  61.5 1.6 %shard_map.87 = bf16[1024,256]{1,0:T(8,128)(2,1)} custom-call(bf16[4,256,128]{2,1,0:T(8,128)(2,1)S(1)} %pad_maximum_fusion.1.coeffs_ref, bf16[1024,128]{1,0:T(8,128)(2,1)S(1)} %get-tuple-element.12.refs_0_, bf16[1024,128]{1,0:T(8,128)(2,1)S(1)} %collective-permute-done.2.refs_1_, bf16[1024,128]{1,0:T(8,128)(2,1)S(1)} %collective-permute-done.3.refs_2_, ...), custom_call_target="tpu_custom_call" | custom-call | tf_op jit(solution)/shard_map/pallas_call | solution.py:136
  63.1 8.2 %all-to-all-start.2 = ((bf16[16,64,256]{2,1,0:T(8,128)(2,1)}), bf16[16,64,256]{2,1,0:T(8,128)(2,1)S(1)}, u32[]{:S(2)}, u32[]{:S(2)}) async-start(bf16[16,64,256]{2,1,0:T(8,128)(2,1)} %bitcast.19), calls=%async_computation.2 | async-start | bytes 1048576 | tf_op jit(solution)/shard_map/all_to_all | solution.py:43
  71.3 0.1 slice_reduce_fusion
  71.4 15.5 %all-to-all-done.2 = bf16[16,64,256]{2,1,0:T(8,128)(2,1)S(1)} async-done(((bf16[16,64,256]{2,1,0:T(8,128)(2,1)}), bf16[16,64,256]{2,1,0:T(8,128)(2,1)S(1)}, u32[]{:S(2)}, u32[]{:S(2)}) %all-to-all-start.2) | async-done | bytes 524320 | tf_op jit(solution)/shard_map/all_to_all | solution.py:43
  86.9 0.1 reduce_sum.34
  87.0 25.3 %all_to_all.20 = bf16[8,96,256]{2,1,0:T(8,128)(2,1)S(1)} all-to-all(bf16[8,96,256]{2,1,0:T(8,128)(2,1)S(1)} %broadcast_in_dim.11), channel_id=1, replica_groups=mesh['rep'=8,'seq'=64] {'rep'}, dimensions={0} | all-to-all | bytes 786432 | tf_op jit(solution)/shard_map/all_to_all | solution.py:43
  112.4 0.8 convolution_multiply_fusion
  (12 shorter events, 0.2 us)
Async XLA Ops:
  0.6 7.3 %copy-start = (bf16[256,128]{1,0:T(8,128)(2,1)S(1)}, bf16[256,128]{1,0:T(8,128)(2,1)}, u32[]{:S(2)}) copy-start(bf16[256,128]{1,0:T(8,128)(2,1)} %param.13) | copy-start | bytes 196612
  0.6 21.0 %copy-start.1 = (bf16[1,128,4096]{2,1,0:T(8,128)(2,1)S(1)}, bf16[1,128,4096]{2,1,0:T(8,128)(2,1)}, u32[]{:S(2)}) copy-start(bf16[1,128,4096]{2,1,0:T(8,128)(2,1)} %param.7) | copy-start | bytes 3145732
  2.5 19.1 %collective-permute-start = (bf16[128,1152]{1,0:T(8,128)(2,1)S(1)}, bf16[128,1152]{1,0:T(8,128)(2,1)S(1)}, u32[]{:S(2)}, u32[]{:S(2)}) collective-permute-start(bf16[128,1152]{1,0:T(8,128)(2,1)S(1)} %pad_maximum_fusion.own_ref), channel_id=1, source_target_pairs={{0,1},{1,2},{2,3},{3,4},{4,5},{5,6},{6,7},{7,8},{8,9},{9,10},{10,1... | collective-permute-start | bytes 884744 | tf_op jit(solution)/shard_map/ppermute | solution.py:35
  4.4 17.2 %collective-permute-start.1 = (bf16[128,1152]{1,0:T(8,128)(2,1)S(1)}, bf16[128,1152]{1,0:T(8,128)(2,1)S(1)}, u32[]{:S(2)}, u32[]{:S(2)}) collective-permute-start(bf16[128,1152]{1,0:T(8,128)(2,1)S(1)} %pad_maximum_fusion.own_ref), channel_id=1, source_target_pairs={{0,2},{1,3},{2,4},{3,5},{4,6},{5,7},{6,8},{7,9},{8,10},{9,11},{10,... | collective-permute-start | bytes 884744 | tf_op jit(solution)/shard_map/ppermute | solution.py:35
  10.4 20.0 %all-to-all-start = ((bf16[64,4,256]{2,1,0:T(4,128)(2,1)}), bf16[64,4,256]{2,1,0:T(4,128)(2,1)S(1)}, u32[]{:S(2)}, u32[]{:S(2)}) async-start(bf16[64,4,256]{2,1,0:T(4,128)(2,1)} %fusion.5), calls=%async_computation | async-start | bytes 262144 | tf_op jit(solution)/shard_map/all_to_all | solution.py:43
  21.6 0.7 copy-start.2
  33.5 20.0 %all-to-all-start.1 = ((bf16[64,4,640]{2,1,0:T(4,128)(2,1)}), bf16[64,4,640]{2,1,0:T(4,128)(2,1)S(1)}, u32[]{:S(2)}, u32[]{:S(2)}) async-start(bf16[64,4,640]{2,1,0:T(4,128)(2,1)} %copy.30), calls=%async_computation.1 | async-start | bytes 655360 | tf_op jit(solution)/shard_map/all_to_all | solution.py:43
  40.9 12.7 %collective-permute-start.2 = (bf16[1024,128]{1,0:T(8,128)(2,1)S(1)}, bf16[1024,128]{1,0:T(8,128)(2,1)S(1)}, u32[]{:S(2)}, u32[]{:S(2)}) collective-permute-start(bf16[1024,128]{1,0:T(8,128)(2,1)S(1)} %get-tuple-element.13), channel_id=1, source_target_pairs={{0,1},{1,0},{2,3},{3,2},{4,5},{5,4},{6,7},{7,6},{8,9},{9,8},{10,11... | collective-permute-start | bytes 786440 | tf_op jit(solution)/shard_map/ppermute | solution.py:39
  43.0 13.2 %collective-permute-start.3 = (bf16[1024,128]{1,0:T(8,128)(2,1)S(1)}, bf16[1024,128]{1,0:T(8,128)(2,1)S(1)}, u32[]{:S(2)}, u32[]{:S(2)}) collective-permute-start(bf16[1024,128]{1,0:T(8,128)(2,1)S(1)} %get-tuple-element.14), channel_id=1, source_target_pairs={{0,16},{1,17},{2,18},{3,19},{4,20},{5,21},{6,22},{7,23},{8,24},{9,... | collective-permute-start | bytes 786440 | tf_op jit(solution)/shard_map/ppermute | solution.py:39
  46.5 15.1 %collective-permute-start.4 = (bf16[1024,128]{1,0:T(8,128)(2,1)S(1)}, bf16[1024,128]{1,0:T(8,128)(2,1)S(1)}, u32[]{:S(2)}, u32[]{:S(2)}) collective-permute-start(bf16[1024,128]{1,0:T(8,128)(2,1)S(1)} %get-tuple-element.15), channel_id=1, source_target_pairs={{0,17},{1,16},{2,19},{3,18},{4,21},{5,20},{6,23},{7,22},{8,25},{9,... | collective-permute-start | bytes 786440 | tf_op jit(solution)/shard_map/ppermute | solution.py:39
  63.1 23.8 %all-to-all-start.2 = ((bf16[16,64,256]{2,1,0:T(8,128)(2,1)}), bf16[16,64,256]{2,1,0:T(8,128)(2,1)S(1)}, u32[]{:S(2)}, u32[]{:S(2)}) async-start(bf16[16,64,256]{2,1,0:T(8,128)(2,1)} %bitcast.19), calls=%async_computation.2 | async-start | bytes 1048576 | tf_op jit(solution)/shard_map/all_to_all | solution.py:43

commit v4 on v3

--- a/solution.py
+++ b/solution.py
@@ -19,11 +19,13 @@
 HALF = HEAD_SIZE // 2
 LOG2E = math.log2(math.e)
 VMEM_LIMIT = 48 * 1024 * 1024
+PACK_VMEM_LIMIT = 66000000
 NT = (((1,), (1,)), ((), ()))
 
 PARTNERS = (0, 1, 16, 17)
 MEMBERS = len(PARTNERS)
 SHARES = SEQ // MEMBERS
+ROWS = SHARES * HALF
 SIXTEENS = [
     [z2 * 32 + zp * 16 + y * 2 + c for z2 in range(2) for y in range(8)]
     for zp in range(2)
@@ -46,13 +48,13 @@
 
 
 def attention_kernel(
-    place_ref, q_ref, own_ref, one_ref, two_ref, tag_ref, out_ref, *part_refs
+    place_ref, q_ref, own_ref, one_ref, two_ref, out_ref, keep_ref, near_ref, far_ref
 ):
     core, odd = place_ref[0], place_ref[1]
     square = (TOKENS, TOKENS)
-    query_tags = jnp.broadcast_to(tag_ref[...].astype(jnp.float32), square) + 1.0
     lower = lax.broadcasted_iota(jnp.int32, square, 0) <= lax.broadcasted_iota(jnp.int32, square, 1)
     tags = lambda block: block[:, 2 * KV :].astype(jnp.float32)
+    query_tags = tags(own_ref).T
     wide = lambda mask: jnp.concatenate([mask] * GROUP, axis=1)
     seen_edge = wide(jnp.where(lower, tags(own_ref), tags(two_ref)) == query_tags)
     seen_one = wide(tags(one_ref) == query_tags)
@@ -96,29 +98,31 @@
             out_ref[:, column(heads[j])] = head.T.astype(jnp.bfloat16)
             low, high = head[:HALF], head[HALF:]
             row = (z2 * 8 + j) * HALF
-            part_refs[other * 2][row : row + HALF, :] = jnp.where(core == 0, low, high).astype(
-                jnp.bfloat16
-            )
-            part_refs[other * 2 + 1][row : row + HALF, :] = jnp.where(core == 0, high, low).astype(
-                jnp.bfloat16
-            )
-
-
-def attention(place, q, own, one, two, tag):
+            mine = jnp.where(core == 0, low, high).astype(jnp.bfloat16)
+            theirs = jnp.where(core == 0, high, low).astype(jnp.bfloat16)
+            if other == 0:
+                keep_ref[row : row + HALF, :] = mine
+                near_ref[row : row + HALF, :] = theirs
+            else:
+                far_ref[row : row + HALF, :] = mine
+                far_ref[ROWS + row : ROWS + row + HALF, :] = theirs
+
+
+def attention(place, q, own, one, two):
     vmem = pl.BlockSpec(memory_space=pltpu.VMEM)
     return pl.pallas_call(
         attention_kernel,
         out_shape=[jax.ShapeDtypeStruct((TOKENS, QUERY_HEADS * HEAD_SIZE), jnp.bfloat16)]
-        + [jax.ShapeDtypeStruct((SHARES * HALF, TOKENS), jnp.bfloat16)] * MEMBERS,
-        in_specs=[pl.BlockSpec(memory_space=pltpu.SMEM)] + [vmem] * 5,
-        out_specs=[vmem] * (1 + MEMBERS),
+        + [jax.ShapeDtypeStruct((n * ROWS, TOKENS), jnp.bfloat16) for n in (1, 1, 2)],
+        in_specs=[pl.BlockSpec(memory_space=pltpu.SMEM)] + [vmem] * 4,
+        out_specs=[vmem] * 4,
         compiler_params=pltpu.CompilerParams(vmem_limit_bytes=VMEM_LIMIT),
         cost_estimate=pl.CostEstimate(
             flops=4 * QUERY_HEADS * TOKENS * 3 * TOKENS * HEAD_SIZE * 6,
             bytes_accessed=4 << 20,
             transcendentals=QUERY_HEADS * TOKENS * 2 * TOKENS,
         ),
-    )(place, q, own, one, two, tag)
+    )(place, q, own, one, two)
 
 
 def outer_kernel(coeffs_ref, *refs):
@@ -130,71 +134,157 @@
     refs[-1][...] = total.astype(jnp.bfloat16)
 
 
-def outer(coeffs, parts):
-    rows = parts[0].shape[0]
-    step = rows // 2
+def outer(coeffs, keep, near, far, farthest):
+    step = ROWS // 2
+    block = lambda first: pl.BlockSpec((step, TOKENS), lambda i: (i + first, 0))
     return pl.pallas_call(
         outer_kernel,
-        out_shape=jax.ShapeDtypeStruct((rows, R), jnp.bfloat16),
-        grid=(rows // step,),
-        in_specs=[pl.BlockSpec((MEMBERS, R, TOKENS), lambda i: (0, 0, 0))]
-        + [pl.BlockSpec((step, TOKENS), lambda i: (i, 0))] * MEMBERS,
+        out_shape=jax.ShapeDtypeStruct((ROWS, R), jnp.bfloat16),
+        grid=(ROWS // step,),
+        in_specs=[
+            pl.BlockSpec((MEMBERS, R, TOKENS), lambda i: (0, 0, 0)),
+            block(0),
+            block(0),
+            block(0),
+            block(ROWS // step),
+        ],
         out_specs=pl.BlockSpec((step, R), lambda i: (i, 0)),
         compiler_params=pltpu.CompilerParams(vmem_limit_bytes=VMEM_LIMIT),
-    )(coeffs, *parts)
+    )(coeffs, keep, near, far, farthest)
+
+
+PIECES = (SEQ, 4, TOKENS)
+
+
+def pack_kernel(
+    rep_ref,
+    dest_ref,
+    keys_hbm,
+    values_hbm,
+    tag_hbm,
+    coeffs_hbm,
+    basis_hbm,
+    own_ref,
+    out_ref,
+    tag_ref,
+    coeffs_ref,
+    basis_ref,
+    sems,
+):
+    f32, bf16 = jnp.float32, jnp.bfloat16
+    pairs = (
+        (tag_hbm, tag_ref),
+        (coeffs_hbm, coeffs_ref),
+        (basis_hbm, basis_ref),
+        (keys_hbm, own_ref.at[:, :KV]),
+        (values_hbm, own_ref.at[:, KV : 2 * KV]),
+    )
+    copies = [pltpu.make_async_copy(a, b, sems.at[i]) for i, (a, b) in enumerate(pairs)]
+    for copy in copies:
+        copy.start()
+    copies[0].wait()
+    tags = jnp.broadcast_to(tag_ref[...].astype(f32), (TOKENS, TOKENS)).T + 1.0
+    own_ref[:, 2 * KV :] = tags.astype(bf16)
+    copies[1].wait()
+    out_ref[:, :, :TOKENS] = coeffs_ref[...].astype(f32).T.reshape(PIECES).astype(bf16)
+    copies[2].wait()
+    count = R // REP
+    mine = basis_ref[pl.ds(pl.multiple_of(rep_ref[0] * count, count), count), :]
+    gram = lax.dot_general(mine, basis_ref[...], NT, preferred_element_type=f32)
+    gram = jnp.concatenate([gram[:, :TOKENS], gram[:, TOKENS:]], axis=0).astype(bf16)
+    row = lax.broadcasted_iota(jnp.int32, (R, SEQ), 0)
+    column = lax.broadcasted_iota(jnp.int32, (R, SEQ), 1)
+    spread = jnp.where(row == column * 4, 1.0, 0.0).astype(bf16)
+    extra = jnp.dot(spread, gram, preferred_element_type=f32)
+    row = lax.broadcasted_iota(jnp.int32, (R, TOKENS), 0)
+    extra = jnp.where(row % 4 == 0, extra, dest_ref[0, 0].astype(f32))
+    out_ref[:, :, TOKENS:] = extra.reshape(PIECES).astype(bf16)
+    copies[3].wait()
+    copies[4].wait()
+
+
+def pack(rep, dest, keys, values, tag, coeffs, basis):
+    vmem = pl.BlockSpec(memory_space=pltpu.VMEM)
+    smem = pl.BlockSpec(memory_space=pltpu.SMEM)
+    hbm = pl.BlockSpec(memory_space=pltpu.HBM)
+    return pl.pallas_call(
+        pack_kernel,
+        out_shape=(
+            jax.ShapeDtypeStruct((TOKENS, 2 * KV + TOKENS), jnp.bfloat16),
+            jax.ShapeDtypeStruct((SEQ, 4, 2 * TOKENS), jnp.bfloat16),
+        ),
+        in_specs=[smem, smem] + [hbm] * 5,
+        out_specs=(vmem, vmem),
+        scratch_shapes=[
+            pltpu.VMEM(tag.shape, tag.dtype),
+            pltpu.VMEM(coeffs.shape, coeffs.dtype),
+            pltpu.VMEM(basis.shape, basis.dtype),
+            pltpu.SemaphoreType.DMA((5,)),
+        ],
+        compiler_params=pltpu.CompilerParams(vmem_limit_bytes=PACK_VMEM_LIMIT),
+    )(rep, dest, keys, values, tag, coeffs, basis)
+
+
+def sort_kernel(first_ref, out_ref):
+    f32, bf16 = jnp.float32, jnp.bfloat16
+    pieces = first_ref[:, :, :TOKENS].astype(f32).reshape(R, TOKENS).astype(bf16)
+    extra = first_ref[:, :, TOKENS:].astype(f32).reshape(R, TOKENS)
+    row = lax.broadcasted_iota(jnp.int32, (R, TOKENS), 0)
+    gram = jnp.sum(jnp.where(row % 4 == 0, extra, 0.0), axis=0, keepdims=True)
+    dest = jnp.where(row % 4 == 0, pltpu.roll(extra, R - 1, 0), extra)
+    dest = jnp.concatenate([dest.T] * 2, axis=0)
+    row = lax.broadcasted_iota(jnp.int32, (R, R), 0)
+    column = lax.broadcasted_iota(jnp.int32, (R, R), 1)
+    same = row % 4 == column % 4
+    for m, partner in enumerate(PARTNERS):
+        holder = ((row // 4) ^ partner).astype(f32)
+        chosen = jnp.where(same & (dest == holder), 1.0, 0.0).astype(bf16)
+        sorted_pieces = jnp.dot(chosen, pieces, preferred_element_type=f32)
+        out_ref[:, :, m * TOKENS : (m + 1) * TOKENS] = sorted_pieces.reshape(PIECES).astype(bf16)
+    out_ref[:, :, MEMBERS * TOKENS :] = jnp.broadcast_to(gram.reshape(1, 1, TOKENS), PIECES).astype(
+        bf16
+    )
+
+
+def sort(first):
+    vmem = pl.BlockSpec(memory_space=pltpu.VMEM)
+    return pl.pallas_call(
+        sort_kernel,
+        out_shape=jax.ShapeDtypeStruct((SEQ, 4, (MEMBERS + 1) * TOKENS), jnp.bfloat16),
+        in_specs=[vmem],
+        out_specs=vmem,
+        compiler_params=pltpu.CompilerParams(vmem_limit_bytes=VMEM_LIMIT),
+    )(first)
 
 
 def local(queries, keys, values, doc_ids, coeffs, shard_dest, basis):
-    rep = lax.axis_index("rep")
+    rep = lax.axis_index("rep").astype(jnp.int32)
+    seq = lax.axis_index("seq").astype(jnp.int32)
     bf16 = jnp.bfloat16
 
-    numbers = jnp.broadcast_to((doc_ids[0] + 1).astype(bf16)[:, None], (TOKENS, TOKENS))
-    own = jnp.concatenate([keys[0], values[0], numbers], axis=1)
+    own, packed = pack(rep[None], shard_dest, keys[0], values[0], doc_ids, coeffs[0], basis)
     two = shifted(own, 2)
     one = shifted(own, 1)
-
-    gram_rows = R // REP
-    basis_rows = lax.dynamic_slice_in_dim(basis, rep * gram_rows, gram_rows, 0)
-    gram = lax.dot_general(basis_rows, basis, NT, preferred_element_type=jnp.float32)
-    extra = jnp.concatenate(
-        [
-            gram.astype(bf16).reshape(SEQ, 1, TOKENS),
-            jnp.broadcast_to(shard_dest[0, 0].astype(bf16), (SEQ, 3, TOKENS)),
-        ],
-        axis=1,
-    )
-    first = exchange(jnp.concatenate([coeffs[0].T.reshape(SEQ, 4, TOKENS), extra], axis=2), "seq")
-
-    seq = lax.axis_index("seq").astype(jnp.int32)
-    place = jnp.stack([seq % 2, seq // 16 % 2])
-    attended, *parts = attention(place, queries[0], own, one, two, doc_ids)
-    first, parts[0] = lax.optimization_barrier((first, parts[0]))
-    parts = parts[:1] + [swapped(part, partner) for part, partner in zip(parts[1:], PARTNERS[1:])]
-
-    dest = first[:, 1, TOKENS].astype(jnp.int32)
-    device = lax.broadcasted_iota(jnp.int32, (SEQ, SEQ), 0)
-    sorted_pieces = [
-        jnp.einsum(
-            "bj,jit->bit",
-            (dest[None, :] == (device ^ partner)).astype(bf16),
-            first[:, :, :TOKENS],
-            preferred_element_type=jnp.float32,
-        ).astype(bf16)
-        for partner in PARTNERS
-    ]
-    gram_piece = jnp.sum(first[:, 0, TOKENS:].astype(jnp.float32), axis=0).astype(bf16)
-    second = exchange(
-        jnp.concatenate(sorted_pieces + [jnp.broadcast_to(gram_piece, (SEQ, 4, TOKENS))], axis=2),
-        "seq",
-    )
+    first = exchange(packed, "seq")
+
+    place = jnp.stack([seq & 1, (seq >> 4) & 1])
+    attended, keep, near, far = attention(place, queries[0], own, one, two)
+    first, keep = lax.optimization_barrier((first, keep))
+    near = swapped(near, 1)
+    far = swapped(far, 16)
+    farthest = swapped(far, 1)
+
+    second = exchange(sort(first), "seq")
 
     lined = jnp.stack(
         [second[:, :, m * TOKENS : (m + 1) * TOKENS].reshape(R, TOKENS) for m in range(MEMBERS)]
     )
-    partial = outer(lined, parts).reshape(SHARES, HALF, R)
+    partial = outer(lined, keep, near, far, farthest).reshape(SHARES, HALF, R)
     arrived = exchange(partial, "seq", SIXTEENS)
     rows = jnp.sum(arrived.astype(jnp.float32), axis=0).astype(bf16)
-    gram_share = second[:, 0, MEMBERS * TOKENS :].reshape(gram_rows, R)
+    gram_rows = R // REP
+    gram_share = second[:, 0, MEMBERS * TOKENS :]
+    gram_share = jnp.concatenate([gram_share[:gram_rows], gram_share[gram_rows:]], axis=1)
     last = exchange(
         jnp.broadcast_to(jnp.concatenate([rows, gram_share], axis=0), (REP, HALF + gram_rows, R)),
         "rep",

time: 114 us -> 104 us (0.912)
  waiting for transfers between devices: 31.7 us -> 23.6 us
  other arithmetic: 4.02 us -> 0.23 us
  Pallas kernels: 6.32 us -> 9.54 us
    ppermute x3, waiting for transfers between devices: 7.88 us -> 1.55 us  [swapped(): return lax.ppermute(block, 'seq', [(i, i ^ partner) for i in range(SEQ)])]
    pallas_call x1 -> x3, Pallas kernels: 1.57 us -> 4.79 us  [the longest x1 2.07 us: pack(): pl.pallas_call(pack_kernel, out_shape=(jax.ShapeDtypeStruct((TOKENS, 2 *...]
    convert_element_type x2 -> x0, other arithmetic: 1.98 us -> none  [the longest x1 1.23 us: local(): dest = first[:, 1, TOKENS].astype(jnp.int32)]
    all_to_all x3, waiting for transfers between devices: 23.8 us -> 22 us  [exchange(): lax.all_to_all(block, axis, split_axis=0, concat_axis=0, axis_index_group...]
    concatenate x2 -> x0, other arithmetic: 1.7 us -> none  [the longest x1 0.99 us: local(): own = jnp.concatenate([keys[0], values[0], numbers], axis=1)]
  transfers between devices with their start and end apart: 8 -> 8, of which waited for: 5 -> 3; matrix products, arithmetic and copies ran while one was open for 2% -> 0% of each run, Pallas kernels for 4% -> 6%
where the time goes in v4:
time: 104 us
  starting transfers between devices  40.1 us (39%)
  blocking collectives  25.5 us (25%)
  waiting for transfers between devices  23.6 us (23%)
  Pallas kernels  9.54 us (9%)
  local copies, waits for them, and re-layouts  2.35 us (2%)
  between operations  1.44 us (1%)
    all_to_all x3, starting transfers between devices, exchange(): lax.all_to_all(block, axis, split_axis=0, concat_axis=0, axis_index_group...  26.9 us
    all_to_all x1, blocking collectives, exchange(): lax.all_to_all(block, axis, split_axis=0, concat_axis=0, axis_index_group...  25.5 us
    all_to_all x3, waiting for transfers between devices, exchange(): lax.all_to_all(block, axis, split_axis=0, concat_axis=0, axis_index_group...  22 us
    ppermute x3, starting transfers between devices, swapped(): return lax.ppermute(block, 'seq', [(i, i ^ partner) for i in range(SEQ)])  7.8 us
    ppermute x2, starting transfers between devices, shifted(): lax.ppermute(block, 'seq', [(i, i + distance) for i in range(SEQ - distan...  5.4 us
    pallas_call x1, Pallas kernels, attention(): pl.pallas_call(attention_kernel, out_shape=[jax.ShapeDtypeStruct((TOKENS,...  4.75 us
    unnamed x5, local copies, waits for them, and re-layouts  2.19 us
  transfers between devices with their start and end apart: 8, of which 3 were waited for; matrix products, arithmetic and copies ran while one was open for 0% of the time, Pallas kernels for 6%

profile of v4, /device:TPU:136, one launch (start us, length us, event | category | flops | bytes accessed | tf_op | source)
XLA Modules:
  0.0 103.6 jit_solution(8275663337885025204)
XLA Ops:
  1.3 2.1 %shard_map.86 = (bf16[128,1152]{1,0:T(8,128)(2,1)}, bf16[64,4,256]{2,1,0:T(4,128)(2,1)}) custom-call(s32[1]{0:T(128)} %bitcast.3.rep_ref, s32[1,1]{1,0:T(1,128)S(6)} %copy.14.dest_ref, bf16[128,512]{1,0:T(8,128)(2,1)} %bitcast.26, bf16[128,512]{1,0:T(8,128)(2,1)} %bitcast.27, s32[1,128]{1,0:T(1,128)} %tag_hbm.1, bf16[128,256]{1,0:T(8,128)(2,1)} %bitcast.28, ...), custom_call_target="tpu_custom_call" | custom-call | tf_op jit(solution)/shard_map/pallas_call | solution.py:210
  3.4 3.5 %collective-permute-start.1 = (bf16[128,1152]{1,0:T(8,128)(2,1)}, bf16[128,1152]{1,0:T(8,128)(2,1)S(1)}, u32[]{:S(2)}, u32[]{:S(2)}) collective-permute-start(bf16[128,1152]{1,0:T(8,128)(2,1)} %get-tuple-element.10.own_ref), channel_id=1, source_target_pairs={{0,2},{1,3},{2,4},{3,5},{4,6},{5,7},{6,8},{7,9},{8,10},{9,11},{10,... | collective-permute-start | bytes 884744 | tf_op jit(solution)/shard_map/ppermute | solution.py:37
  6.8 1.9 %collective-permute-start = (bf16[128,1152]{1,0:T(8,128)(2,1)}, bf16[128,1152]{1,0:T(8,128)(2,1)S(1)}, u32[]{:S(2)}, u32[]{:S(2)}) collective-permute-start(bf16[128,1152]{1,0:T(8,128)(2,1)} %get-tuple-element.10.own_ref), channel_id=1, source_target_pairs={{0,1},{1,2},{2,3},{3,4},{4,5},{5,6},{6,7},{7,8},{8,9},{9,10},{10,1... | collective-permute-start | bytes 884744 | tf_op jit(solution)/shard_map/ppermute | solution.py:37
  8.8 11.3 %all-to-all-start = ((bf16[64,4,256]{2,1,0:T(4,128)(2,1)}), bf16[64,4,256]{2,1,0:T(4,128)(2,1)S(1)}, u32[]{:S(2)}, u32[]{:S(2)}) async-start(bf16[64,4,256]{2,1,0:T(4,128)(2,1)} %get-tuple-element.12), calls=%async_computation | async-start | bytes 262144 | tf_op jit(solution)/shard_map/all_to_all | solution.py:45
  20.1 0.1 pad_add_fusion.place_ref
  20.2 0.0 collective-permute-done.1.two_ref
  20.2 0.0 collective-permute-done.one_ref
  20.2 0.0 copy-start
  20.2 1.2 %copy-done = bf16[1,128,4096]{2,1,0:T(8,128)(2,1)S(1)} copy-done((bf16[1,128,4096]{2,1,0:T(8,128)(2,1)S(1)}, bf16[1,128,4096]{2,1,0:T(8,128)(2,1)}, u32[]{:S(2)}) %copy-start) | copy-done | bytes 1048600
  21.4 0.0 copy-start.1
  21.4 1.0 copy-done.1
  22.4 4.7 %shard_map.87 = (bf16[128,4096]{1,0:T(8,128)(2,1)}, bf16[1024,128]{1,0:T(8,128)(2,1)S(1)}, bf16[1024,128]{1,0:T(8,128)(2,1)S(1)}, bf16[2048,128]{1,0:T(8,128)(2,1)S(1)}) custom-call(s32[2]{0:T(128)S(1)} %pad_add_fusion.place_ref, bf16[128,4096]{1,0:T(8,128)(2,1)S(1)} %bitcast.20, bf16[128,1152]{1,0:T(8,128)(2,1)S(1)} %copy-done.1, ...), custom_call_target="tpu_custom_call" | custom-call | flops 4831838208 | bytes 4194304 | tf_op jit(solution)/shard_map/pallas_call | solution.py:113
  27.1 3.5 %collective-permute-start.3 = (bf16[2048,128]{1,0:T(8,128)(2,1)S(1)}, bf16[2048,128]{1,0:T(8,128)(2,1)S(1)}, u32[]{:S(2)}, u32[]{:S(2)}) collective-permute-start(bf16[2048,128]{1,0:T(8,128)(2,1)S(1)} %get-tuple-element.17), channel_id=1, source_target_pairs={{0,16},{1,17},{2,18},{3,19},{4,20},{5,21},{6,22},{7,23},{8,24},{9,... | collective-permute-start | bytes 1572872 | tf_op jit(solution)/shard_map/ppermute | solution.py:41
  30.6 0.0 all-to-all-done.first_ref
  30.6 1.1 %shard_map.88 = bf16[64,4,640]{2,1,0:T(4,128)(2,1)} custom-call(bf16[64,4,256]{2,1,0:T(4,128)(2,1)S(1)} %all-to-all-done.first_ref), custom_call_target="tpu_custom_call" | custom-call | tf_op jit(solution)/shard_map/pallas_call | solution.py:251
  31.7 9.7 %all-to-all-start.1 = ((bf16[64,4,640]{2,1,0:T(4,128)(2,1)}), bf16[64,4,640]{2,1,0:T(4,128)(2,1)S(1)}, u32[]{:S(2)}, u32[]{:S(2)}) async-start(bf16[64,4,640]{2,1,0:T(4,128)(2,1)} %shard_map.88), calls=%async_computation.1 | async-start | bytes 655360 | tf_op jit(solution)/shard_map/all_to_all | solution.py:45
  41.4 1.5 %collective-permute-done.3.refs_2_ = bf16[2048,128]{1,0:T(8,128)(2,1)S(1)} collective-permute-done((bf16[2048,128]{1,0:T(8,128)(2,1)S(1)}, bf16[2048,128]{1,0:T(8,128)(2,1)S(1)}, u32[]{:S(2)}, u32[]{:S(2)}) %collective-permute-start.3) | collective-permute-done | bytes 524320 | tf_op jit(solution)/shard_map/ppermute | solution.py:41
  43.0 1.9 %collective-permute-start.4 = (bf16[2048,128]{1,0:T(8,128)(2,1)S(1)}, bf16[2048,128]{1,0:T(8,128)(2,1)S(1)}, u32[]{:S(2)}, u32[]{:S(2)}) collective-permute-start(bf16[2048,128]{1,0:T(8,128)(2,1)S(1)} %collective-permute-done.3.refs_2_), channel_id=1, source_target_pairs={{0,1},{1,0},{2,3},{3,2},{4,5},{5,4},{6,7},{7,6},{8,9},{9,8},{10,11... | collective-permute-start | bytes 1572872 | tf_op jit(solution)/shard_map/ppermute | solution.py:41
  44.9 2.4 %collective-permute-start.2 = (bf16[1024,128]{1,0:T(8,128)(2,1)S(1)}, bf16[1024,128]{1,0:T(8,128)(2,1)S(1)}, u32[]{:S(2)}, u32[]{:S(2)}) collective-permute-start(bf16[1024,128]{1,0:T(8,128)(2,1)S(1)} %get-tuple-element.16), channel_id=1, source_target_pairs={{0,1},{1,0},{2,3},{3,2},{4,5},{5,4},{6,7},{7,6},{8,9},{9,8},{10,11... | collective-permute-start | bytes 786440 | tf_op jit(solution)/shard_map/ppermute | solution.py:41
  47.3 6.7 %all-to-all-done.1 = bf16[64,4,640]{2,1,0:T(4,128)(2,1)S(1)} async-done(((bf16[64,4,640]{2,1,0:T(4,128)(2,1)}), bf16[64,4,640]{2,1,0:T(4,128)(2,1)S(1)}, u32[]{:S(2)}, u32[]{:S(2)}) %all-to-all-start.1) | async-done | bytes 327712 | tf_op jit(solution)/shard_map/all_to_all | solution.py:45
  54.0 0.1 fusion
  54.2 0.0 collective-permute-done.2.refs_1_
  54.2 0.0 collective-permute-done.4.refs_3_
  54.2 1.6 %shard_map.89 = bf16[1024,256]{1,0:T(8,128)(2,1)} custom-call(bf16[4,256,128]{2,1,0:T(8,128)(2,1)S(1)} %pad_maximum_fusion.coeffs_ref, bf16[1024,128]{1,0:T(8,128)(2,1)S(1)} %get-tuple-element.15.refs_0_, bf16[1024,128]{1,0:T(8,128)(2,1)S(1)} %collective-permute-done.2.refs_1_, bf16[2048,128]{1,0:T(8,128)(2,1)S(1)} %collective-permute-done.3.refs_2_, ...), custom_call_target="tpu_custom_call" | custom-call | tf_op jit(solution)/shard_map/pallas_call | solution.py:140
  55.8 5.9 %all-to-all-start.2 = ((bf16[16,64,256]{2,1,0:T(8,128)(2,1)}), bf16[16,64,256]{2,1,0:T(8,128)(2,1)S(1)}, u32[]{:S(2)}, u32[]{:S(2)}) async-start(bf16[16,64,256]{2,1,0:T(8,128)(2,1)} %bitcast.12), calls=%async_computation.2 | async-start | bytes 1048576 | tf_op jit(solution)/shard_map/all_to_all | solution.py:45
  61.7 15.3 %all-to-all-done.2 = bf16[16,64,256]{2,1,0:T(8,128)(2,1)S(1)} async-done(((bf16[16,64,256]{2,1,0:T(8,128)(2,1)}), bf16[16,64,256]{2,1,0:T(8,128)(2,1)S(1)}, u32[]{:S(2)}, u32[]{:S(2)}) %all-to-all-start.2) | async-done | bytes 524320 | tf_op jit(solution)/shard_map/all_to_all | solution.py:45
  77.0 0.1 reduce_sum.21
  77.1 25.5 %all_to_all.20 = bf16[8,96,256]{2,1,0:T(8,128)(2,1)S(1)} all-to-all(bf16[8,96,256]{2,1,0:T(8,128)(2,1)S(1)} %broadcast_in_dim.11), channel_id=1, replica_groups=mesh['rep'=8,'seq'=64] {'rep'}, dimensions={0} | all-to-all | bytes 786432 | tf_op jit(solution)/shard_map/all_to_all | solution.py:45
  102.7 0.8 convolution_multiply_fusion
  (7 shorter events, 0.1 us)
Async XLA Ops:
  3.4 16.8 %collective-permute-start.1 = (bf16[128,1152]{1,0:T(8,128)(2,1)}, bf16[128,1152]{1,0:T(8,128)(2,1)S(1)}, u32[]{:S(2)}, u32[]{:S(2)}) collective-permute-start(bf16[128,1152]{1,0:T(8,128)(2,1)} %get-tuple-element.10.own_ref), channel_id=1, source_target_pairs={{0,2},{1,3},{2,4},{3,5},{4,6},{5,7},{6,8},{7,9},{8,10},{9,11},{10,... | collective-permute-start | bytes 884744 | tf_op jit(solution)/shard_map/ppermute | solution.py:37
  6.8 13.3 %collective-permute-start = (bf16[128,1152]{1,0:T(8,128)(2,1)}, bf16[128,1152]{1,0:T(8,128)(2,1)S(1)}, u32[]{:S(2)}, u32[]{:S(2)}) collective-permute-start(bf16[128,1152]{1,0:T(8,128)(2,1)} %get-tuple-element.10.own_ref), channel_id=1, source_target_pairs={{0,1},{1,2},{2,3},{3,4},{4,5},{5,6},{6,7},{7,8},{8,9},{9,10},{10,1... | collective-permute-start | bytes 884744 | tf_op jit(solution)/shard_map/ppermute | solution.py:37
  8.8 21.8 %all-to-all-start = ((bf16[64,4,256]{2,1,0:T(4,128)(2,1)}), bf16[64,4,256]{2,1,0:T(4,128)(2,1)S(1)}, u32[]{:S(2)}, u32[]{:S(2)}) async-start(bf16[64,4,256]{2,1,0:T(4,128)(2,1)} %get-tuple-element.12), calls=%async_computation | async-start | bytes 262144 | tf_op jit(solution)/shard_map/all_to_all | solution.py:45
  20.2 1.2 %copy-start = (bf16[1,128,4096]{2,1,0:T(8,128)(2,1)S(1)}, bf16[1,128,4096]{2,1,0:T(8,128)(2,1)}, u32[]{:S(2)}) copy-start(bf16[1,128,4096]{2,1,0:T(8,128)(2,1)} %param.7) | copy-start | bytes 3145732
  21.4 1.0 copy-start.1
  27.1 15.9 %collective-permute-start.3 = (bf16[2048,128]{1,0:T(8,128)(2,1)S(1)}, bf16[2048,128]{1,0:T(8,128)(2,1)S(1)}, u32[]{:S(2)}, u32[]{:S(2)}) collective-permute-start(bf16[2048,128]{1,0:T(8,128)(2,1)S(1)} %get-tuple-element.17), channel_id=1, source_target_pairs={{0,16},{1,17},{2,18},{3,19},{4,20},{5,21},{6,22},{7,23},{8,24},{9,... | collective-permute-start | bytes 1572872 | tf_op jit(solution)/shard_map/ppermute | solution.py:41
  31.7 22.3 %all-to-all-start.1 = ((bf16[64,4,640]{2,1,0:T(4,128)(2,1)}), bf16[64,4,640]{2,1,0:T(4,128)(2,1)S(1)}, u32[]{:S(2)}, u32[]{:S(2)}) async-start(bf16[64,4,640]{2,1,0:T(4,128)(2,1)} %shard_map.88), calls=%async_computation.1 | async-start | bytes 655360 | tf_op jit(solution)/shard_map/all_to_all | solution.py:45
  43.0 11.2 %collective-permute-start.4 = (bf16[2048,128]{1,0:T(8,128)(2,1)S(1)}, bf16[2048,128]{1,0:T(8,128)(2,1)S(1)}, u32[]{:S(2)}, u32[]{:S(2)}) collective-permute-start(bf16[2048,128]{1,0:T(8,128)(2,1)S(1)} %collective-permute-done.3.refs_2_), channel_id=1, source_target_pairs={{0,1},{1,0},{2,3},{3,2},{4,5},{5,4},{6,7},{7,6},{8,9},{9,8},{10,11... | collective-permute-start | bytes 1572872 | tf_op jit(solution)/shard_map/ppermute | solution.py:41
  44.9 9.3 %collective-permute-start.2 = (bf16[1024,128]{1,0:T(8,128)(2,1)S(1)}, bf16[1024,128]{1,0:T(8,128)(2,1)S(1)}, u32[]{:S(2)}, u32[]{:S(2)}) collective-permute-start(bf16[1024,128]{1,0:T(8,128)(2,1)S(1)} %get-tuple-element.16), channel_id=1, source_target_pairs={{0,1},{1,0},{2,3},{3,2},{4,5},{5,4},{6,7},{7,6},{8,9},{9,8},{10,11... | collective-permute-start | bytes 786440 | tf_op jit(solution)/shard_map/ppermute | solution.py:41
  55.8 21.2 %all-to-all-start.2 = ((bf16[16,64,256]{2,1,0:T(8,128)(2,1)}), bf16[16,64,256]{2,1,0:T(8,128)(2,1)S(1)}, u32[]{:S(2)}, u32[]{:S(2)}) async-start(bf16[16,64,256]{2,1,0:T(8,128)(2,1)} %bitcast.12), calls=%async_computation.2 | async-start | bytes 1048576 | tf_op jit(solution)/shard_map/all_to_all | solution.py:45

commit v5 on v4

--- a/solution.py
+++ b/solution.py
@@ -1,3 +1,4 @@
+import functools
 import math
 
 import jax
@@ -19,7 +20,7 @@
 HALF = HEAD_SIZE // 2
 LOG2E = math.log2(math.e)
 VMEM_LIMIT = 48 * 1024 * 1024
-PACK_VMEM_LIMIT = 66000000
+OWN_COPIES_VMEM_LIMIT = 66000000
 NT = (((1,), (1,)), ((), ()))
 
 PARTNERS = (0, 1, 16, 17)
@@ -47,36 +48,70 @@
     )
 
 
-def attention_kernel(
-    place_ref, q_ref, own_ref, one_ref, two_ref, out_ref, keep_ref, near_ref, far_ref
-):
+def attention_kernel(other, place_ref, q_hbm, own_hbm, one_hbm, two_hbm, *refs):
+    if other == 0:
+        _, out_hbm, mine_ref, theirs_ref = refs[:4]
+    else:
+        out_hbm, mine_ref = refs[:2]
+        theirs_ref = mine_ref
+    q_ref, block_ref, tag_ref, out_ref, sems = refs[-5:]
     core, odd = place_ref[0], place_ref[1]
+    blocks = (own_hbm, one_hbm, two_hbm)
+    span = GROUP * HEAD_SIZE
+    columns = lambda start, size: pl.ds(pl.multiple_of(start, size), size)
+    zs = [z2 * 2 + (odd if other == 0 else 1 - odd) for z2 in range(2)]
+    tag_copies = [
+        pltpu.make_async_copy(b.at[:, 2 * KV :], tag_ref.at[i], sems.at[i])
+        for i, b in enumerate(blocks)
+    ]
+    steps = []
+    for z2, z in enumerate(zs):
+        at = 3 + z2 * 7
+        copies = [
+            pltpu.make_async_copy(q_hbm.at[:, columns(z * span, span)], q_ref.at[z2], sems.at[at])
+        ]
+        for i, b in enumerate(blocks):
+            for part in range(2):
+                copies.append(
+                    pltpu.make_async_copy(
+                        b.at[:, columns(part * KV + z * HEAD_SIZE, HEAD_SIZE)],
+                        block_ref.at[z2, part, i],
+                        sems.at[at + 1 + i * 2 + part],
+                    )
+                )
+        steps.append(copies)
+    for copy in tag_copies + steps[0] + steps[1]:
+        copy.start()
+    outs = [
+        pltpu.make_async_copy(
+            out_ref.at[z2], out_hbm.at[:, columns(z * span, span)], sems.at[17 + z2]
+        )
+        for z2, z in enumerate(zs)
+    ]
     square = (TOKENS, TOKENS)
     lower = lax.broadcasted_iota(jnp.int32, square, 0) <= lax.broadcasted_iota(jnp.int32, square, 1)
-    tags = lambda block: block[:, 2 * KV :].astype(jnp.float32)
-    query_tags = tags(own_ref).T
+    for copy in tag_copies:
+        copy.wait()
+    own_tags, one_tags, two_tags = [tag_ref[i].astype(jnp.float32) for i in range(3)]
+    query_tags = own_tags.T
     wide = lambda mask: jnp.concatenate([mask] * GROUP, axis=1)
-    seen_edge = wide(jnp.where(lower, tags(own_ref), tags(two_ref)) == query_tags)
-    seen_one = wide(tags(one_ref) == query_tags)
+    seen_edge = wide(jnp.where(lower, own_tags, two_tags) == query_tags)
+    seen_one = wide(one_tags == query_tags)
     lower = wide(lower)
     hidden = jnp.float32(-1e30)
     factor = HEAD_SIZE ** (-0.5) * LOG2E
-    column = lambda start: pl.ds(pl.multiple_of(start, HEAD_SIZE), HEAD_SIZE)
-    for step in range(KEY_VALUE_HEADS):
-        other, z2 = step // 2, step % 2
-        z = z2 * 2 + (odd if other == 0 else 1 - odd)
-        at = z * HEAD_SIZE
-        turned = [
-            b[:, column(KV + at)].astype(jnp.float32).T.astype(jnp.bfloat16)
-            for b in (own_ref, one_ref, two_ref)
-        ]
-        heads = [(z * GROUP + j) * HEAD_SIZE for j in range(GROUP)]
-        q = jnp.concatenate([q_ref[:, column(h)] for h in heads], axis=0)
-        score = lambda b: lax.dot_general(
-            b[:, column(at)], q, NT, preferred_element_type=jnp.float32
-        )
-        edge = jnp.where(seen_edge, jnp.where(lower, score(own_ref), score(two_ref)), hidden)
-        one = jnp.where(seen_one, score(one_ref), hidden)
+    for z2 in range(2):
+        for copy in steps[z2]:
+            copy.wait()
+        turned = [block_ref[z2, 1, i].astype(jnp.float32).T.astype(jnp.bfloat16) for i in range(3)]
+        q = jnp.concatenate(
+            [q_ref[z2, :, j * HEAD_SIZE : (j + 1) * HEAD_SIZE] for j in range(GROUP)], axis=0
+        )
+        score = lambda i: lax.dot_general(
+            block_ref[z2, 0, i], q, NT, preferred_element_type=jnp.float32
+        )
+        edge = jnp.where(seen_edge, jnp.where(lower, score(0), score(2)), hidden)
+        one = jnp.where(seen_one, score(1), hidden)
         highest = jnp.max(jnp.maximum(edge, one), axis=0, keepdims=True)
         edge = jnp.exp2((edge - highest) * factor)
         one = jnp.exp2((one - highest) * factor)
@@ -95,34 +130,46 @@
         )
         for j in range(GROUP):
             head = mixed[:, j * HEAD_SIZE : (j + 1) * HEAD_SIZE]
-            out_ref[:, column(heads[j])] = head.T.astype(jnp.bfloat16)
+            out_ref[z2, :, j * HEAD_SIZE : (j + 1) * HEAD_SIZE] = head.T.astype(jnp.bfloat16)
             low, high = head[:HALF], head[HALF:]
             row = (z2 * 8 + j) * HALF
-            mine = jnp.where(core == 0, low, high).astype(jnp.bfloat16)
-            theirs = jnp.where(core == 0, high, low).astype(jnp.bfloat16)
-            if other == 0:
-                keep_ref[row : row + HALF, :] = mine
-                near_ref[row : row + HALF, :] = theirs
-            else:
-                far_ref[row : row + HALF, :] = mine
-                far_ref[ROWS + row : ROWS + row + HALF, :] = theirs
-
-
-def attention(place, q, own, one, two):
+            shift = other * ROWS
+            mine_ref[row : row + HALF, :] = jnp.where(core == 0, low, high).astype(jnp.bfloat16)
+            theirs_ref[shift + row : shift + row + HALF, :] = jnp.where(
+                core == 0, high, low
+            ).astype(jnp.bfloat16)
+        outs[z2].start()
+    for copy in outs:
+        copy.wait()
+
+
+def attention(other, place, q, own, one, two, attended=None):
     vmem = pl.BlockSpec(memory_space=pltpu.VMEM)
+    hbm = pl.BlockSpec(memory_space=pltpu.HBM)
+    operands = (place, q, own, one, two) + (() if attended is None else (attended,))
+    sizes = (2,) if other else (1, 1)
+    square = (TOKENS, TOKENS)
     return pl.pallas_call(
-        attention_kernel,
+        functools.partial(attention_kernel, other),
         out_shape=[jax.ShapeDtypeStruct((TOKENS, QUERY_HEADS * HEAD_SIZE), jnp.bfloat16)]
-        + [jax.ShapeDtypeStruct((n * ROWS, TOKENS), jnp.bfloat16) for n in (1, 1, 2)],
-        in_specs=[pl.BlockSpec(memory_space=pltpu.SMEM)] + [vmem] * 4,
-        out_specs=[vmem] * 4,
-        compiler_params=pltpu.CompilerParams(vmem_limit_bytes=VMEM_LIMIT),
+        + [jax.ShapeDtypeStruct((n * ROWS, TOKENS), jnp.bfloat16) for n in sizes],
+        in_specs=[pl.BlockSpec(memory_space=pltpu.SMEM)] + [hbm] * (len(operands) - 1),
+        out_specs=[hbm] + [vmem] * len(sizes),
+        scratch_shapes=[
+            pltpu.VMEM((2, TOKENS, GROUP * HEAD_SIZE), jnp.bfloat16),
+            pltpu.VMEM((2, 2, 3) + square, jnp.bfloat16),
+            pltpu.VMEM((3,) + square, jnp.bfloat16),
+            pltpu.VMEM((2, TOKENS, GROUP * HEAD_SIZE), jnp.bfloat16),
+            pltpu.SemaphoreType.DMA((19,)),
+        ],
+        input_output_aliases={} if attended is None else {5: 0},
+        compiler_params=pltpu.CompilerParams(vmem_limit_bytes=OWN_COPIES_VMEM_LIMIT),
         cost_estimate=pl.CostEstimate(
-            flops=4 * QUERY_HEADS * TOKENS * 3 * TOKENS * HEAD_SIZE * 6,
-            bytes_accessed=4 << 20,
-            transcendentals=QUERY_HEADS * TOKENS * 2 * TOKENS,
+            flops=4 * QUERY_HEADS * TOKENS * 3 * TOKENS * HEAD_SIZE * 3,
+            bytes_accessed=2 << 20,
+            transcendentals=QUERY_HEADS * TOKENS * TOKENS,
         ),
-    )(place, q, own, one, two)
+    )(*operands)
 
 
 def outer_kernel(coeffs_ref, *refs):
@@ -221,7 +268,7 @@
             pltpu.VMEM(basis.shape, basis.dtype),
             pltpu.SemaphoreType.DMA((5,)),
         ],
-        compiler_params=pltpu.CompilerParams(vmem_limit_bytes=PACK_VMEM_LIMIT),
+        compiler_params=pltpu.CompilerParams(vmem_limit_bytes=OWN_COPIES_VMEM_LIMIT),
     )(rep, dest, keys, values, tag, coeffs, basis)
 
 
@@ -268,13 +315,15 @@
     first = exchange(packed, "seq")
 
     place = jnp.stack([seq & 1, (seq >> 4) & 1])
-    attended, keep, near, far = attention(place, queries[0], own, one, two)
-    first, keep = lax.optimization_barrier((first, keep))
+    attended, far = attention(1, place, queries[0], own, one, two)
+    first, far = lax.optimization_barrier((first, far))
+    far = swapped(far, 16)
+
+    second = exchange(sort(first), "seq")
+    attended, keep, near = attention(0, place, queries[0], own, one, two, attended)
+    near, far = lax.optimization_barrier((near, far))
     near = swapped(near, 1)
-    far = swapped(far, 16)
     farthest = swapped(far, 1)
-
-    second = exchange(sort(first), "seq")
 
     lined = jnp.stack(
         [second[:, :, m * TOKENS : (m + 1) * TOKENS].reshape(R, TOKENS) for m in range(MEMBERS)]

time: 104 us -> 107 us (1.029)
  the two profiles are of different devices: /device:TPU:136 before, /device:TPU:72 now
where the time goes in v5:
time: 107 us; the launch traced here: 106 us
  starting transfers between devices  38.3 us (36%)
  blocking collectives  25.6 us (24%)
  waiting for transfers between devices  23.1 us (22%)
  Pallas kernels  15.3 us (14%)
  between operations  1.46 us (1%)
    all_to_all x3, starting transfers between devices, exchange(): lax.all_to_all(block, axis, split_axis=0, concat_axis=0, axis_index_group...  26 us
    all_to_all x1, blocking collectives, exchange(): lax.all_to_all(block, axis, split_axis=0, concat_axis=0, axis_index_group...  25.6 us
    all_to_all x3, waiting for transfers between devices, exchange(): lax.all_to_all(block, axis, split_axis=0, concat_axis=0, axis_index_group...  18.6 us
    pallas_call x2, Pallas kernels, attention(): pl.pallas_call(functools.partial(attention_kernel, other), out_shape=[jax...  10.5 us
    ppermute x3, starting transfers between devices, swapped(): return lax.ppermute(block, 'seq', [(i, i ^ partner) for i in range(SEQ)])  6.94 us
    ppermute x2, starting transfers between devices, shifted(): lax.ppermute(block, 'seq', [(i, i + distance) for i in range(SEQ - distan...  5.4 us
    ppermute x3, waiting for transfers between devices, swapped(): return lax.ppermute(block, 'seq', [(i, i ^ partner) for i in range(SEQ)])  4.48 us
  transfers between devices with their start and end apart: 8, of which 4 were waited for; matrix products, arithmetic and copies ran while one was open for 1% of the time, Pallas kernels for 11%

profile of v5, /device:TPU:72, one launch (start us, length us, event | category | flops | bytes accessed | tf_op | source)
XLA Modules:
  0.0 106.4 jit_solution(4640032344500878700)
XLA Ops:
  1.3 2.1 %shard_map.86 = (bf16[128,1152]{1,0:T(8,128)(2,1)}, bf16[64,4,256]{2,1,0:T(4,128)(2,1)}) custom-call(s32[1]{0:T(128)} %bitcast.3.rep_ref, s32[1,1]{1,0:T(1,128)S(6)} %copy.16.dest_ref, bf16[128,512]{1,0:T(8,128)(2,1)} %bitcast.25, bf16[128,512]{1,0:T(8,128)(2,1)} %bitcast.26, s32[1,128]{1,0:T(1,128)} %tag_hbm.1, bf16[128,256]{1,0:T(8,128)(2,1)} %bitcast.27, ...), custom_call_target="tpu_custom_call" | custom-call | tf_op jit(solution)/shard_map/pallas_call | solution.py:257
  3.4 3.5 %collective-permute-start.1 = (bf16[128,1152]{1,0:T(8,128)(2,1)}, bf16[128,1152]{1,0:T(8,128)(2,1)S(1)}, u32[]{:S(2)}, u32[]{:S(2)}) collective-permute-start(bf16[128,1152]{1,0:T(8,128)(2,1)} %get-tuple-element.13.own_hbm), channel_id=1, source_target_pairs={{0,2},{1,3},{2,4},{3,5},{4,6},{5,7},{6,8},{7,9},{8,10},{9,11},{10,... | collective-permute-start | bytes 884744 | tf_op jit(solution)/shard_map/ppermute | solution.py:38
  6.9 1.9 %collective-permute-start = (bf16[128,1152]{1,0:T(8,128)(2,1)}, bf16[128,1152]{1,0:T(8,128)(2,1)S(1)}, u32[]{:S(2)}, u32[]{:S(2)}) collective-permute-start(bf16[128,1152]{1,0:T(8,128)(2,1)} %get-tuple-element.13.own_hbm), channel_id=1, source_target_pairs={{0,1},{1,2},{2,3},{3,4},{4,5},{5,6},{6,7},{7,8},{8,9},{9,10},{10,1... | collective-permute-start | bytes 884744 | tf_op jit(solution)/shard_map/ppermute | solution.py:38
  8.8 12.1 %all-to-all-start = ((bf16[64,4,256]{2,1,0:T(4,128)(2,1)}), bf16[64,4,256]{2,1,0:T(4,128)(2,1)S(1)}, u32[]{:S(2)}, u32[]{:S(2)}) async-start(bf16[64,4,256]{2,1,0:T(4,128)(2,1)} %get-tuple-element.16), calls=%async_computation | async-start | bytes 262144 | tf_op jit(solution)/shard_map/all_to_all | solution.py:46
  20.9 0.7 pad_add_fusion.place_ref
  21.6 0.0 collective-permute-done.1.two_hbm
  21.6 0.0 copy-start.1
  21.6 0.0 collective-permute-done.one_hbm
  21.6 0.0 copy-start.2
  21.6 0.7 copy-done.1
  22.3 0.1 copy-done.2
  22.4 5.2 %shard_map.87 = (bf16[128,4096]{1,0:T(8,128)(2,1)}, bf16[2048,128]{1,0:T(8,128)(2,1)}) custom-call(s32[2]{0:T(128)} %pad_add_fusion.place_ref, bf16[128,4096]{1,0:T(8,128)(2,1)} %bitcast.28, bf16[128,1152]{1,0:T(8,128)(2,1)} %get-tuple-element.13.own_hbm, bf16[128,1152]{1,0:T(8,128)(2,1)} %copy-done.2, bf16[128,1152]{1,0:T(8,128)(2,1)} %copy-done.1), custom_call_target="tpu_custom_call" | custom-call | flops 2415919104 | bytes 2097152 | tf_op jit(solution)/shard_map/pallas_call | solution.py:152
  27.7 2.8 %all-to-all-done.first_ref = bf16[64,4,256]{2,1,0:T(4,128)(2,1)S(1)} async-done(((bf16[64,4,256]{2,1,0:T(4,128)(2,1)}), bf16[64,4,256]{2,1,0:T(4,128)(2,1)S(1)}, u32[]{:S(2)}, u32[]{:S(2)}) %all-to-all-start) | async-done | bytes 131104 | tf_op jit(solution)/shard_map/all_to_all | solution.py:46
  30.5 2.6 %collective-permute-start.2 = (bf16[2048,128]{1,0:T(8,128)(2,1)}, bf16[2048,128]{1,0:T(8,128)(2,1)S(1)}, u32[]{:S(2)}, u32[]{:S(2)}) collective-permute-start(bf16[2048,128]{1,0:T(8,128)(2,1)} %get-tuple-element.21), channel_id=1, source_target_pairs={{0,16},{1,17},{2,18},{3,19},{4,20},{5,21},{6,22},{7,23},{8,24},{9,... | collective-permute-start | bytes 1572872 | tf_op jit(solution)/shard_map/ppermute | solution.py:42
  33.1 1.1 %shard_map.89 = bf16[64,4,640]{2,1,0:T(4,128)(2,1)} custom-call(bf16[64,4,256]{2,1,0:T(4,128)(2,1)S(1)} %all-to-all-done.first_ref), custom_call_target="tpu_custom_call" | custom-call | tf_op jit(solution)/shard_map/pallas_call | solution.py:298
  34.2 7.8 %all-to-all-start.1 = ((bf16[64,4,640]{2,1,0:T(4,128)(2,1)}), bf16[64,4,640]{2,1,0:T(4,128)(2,1)S(1)}, u32[]{:S(2)}, u32[]{:S(2)}) async-start(bf16[64,4,640]{2,1,0:T(4,128)(2,1)} %shard_map.89), calls=%async_computation.1 | async-start | bytes 655360 | tf_op jit(solution)/shard_map/all_to_all | solution.py:46
  42.0 5.3 %shard_map.88 = (bf16[128,4096]{1,0:T(8,128)(2,1)}, bf16[1024,128]{1,0:T(8,128)(2,1)}, bf16[1024,128]{1,0:T(8,128)(2,1)}) custom-call(s32[2]{0:T(128)} %pad_add_fusion.place_ref, bf16[128,4096]{1,0:T(8,128)(2,1)} %bitcast.29, bf16[128,1152]{1,0:T(8,128)(2,1)} %get-tuple-element.13.own_hbm, ...), custom_call_target="tpu_custom_call", output_to_operand_aliasing={{0}: (5, {})} | custom-call | flops 2415919104 | bytes 2097152 | tf_op jit(solution)/shard_map/pallas_call | solution.py:152
  47.3 3.3 %collective-permute-done.2.refs_2_ = bf16[2048,128]{1,0:T(8,128)(2,1)S(1)} collective-permute-done((bf16[2048,128]{1,0:T(8,128)(2,1)}, bf16[2048,128]{1,0:T(8,128)(2,1)S(1)}, u32[]{:S(2)}, u32[]{:S(2)}) %collective-permute-start.2) | collective-permute-done | bytes 524320 | tf_op jit(solution)/shard_map/ppermute | solution.py:42
  50.6 1.9 %collective-permute-start.4 = (bf16[2048,128]{1,0:T(8,128)(2,1)S(1)}, bf16[2048,128]{1,0:T(8,128)(2,1)S(1)}, u32[]{:S(2)}, u32[]{:S(2)}) collective-permute-start(bf16[2048,128]{1,0:T(8,128)(2,1)S(1)} %collective-permute-done.2.refs_2_), channel_id=1, source_target_pairs={{0,1},{1,0},{2,3},{3,2},{4,5},{5,4},{6,7},{7,6},{8,9},{9,8},{10,11... | collective-permute-start | bytes 1572872 | tf_op jit(solution)/shard_map/ppermute | solution.py:42
  52.5 2.4 %collective-permute-start.3 = (bf16[1024,128]{1,0:T(8,128)(2,1)}, bf16[1024,128]{1,0:T(8,128)(2,1)S(1)}, u32[]{:S(2)}, u32[]{:S(2)}) collective-permute-start(bf16[1024,128]{1,0:T(8,128)(2,1)} %get-tuple-element.22), channel_id=1, source_target_pairs={{0,1},{1,0},{2,3},{3,2},{4,5},{5,4},{6,7},{7,6},{8,9},{9,8},{10,11... | collective-permute-start | bytes 786440 | tf_op jit(solution)/shard_map/ppermute | solution.py:42
  54.9 0.0 all-to-all-done.1
  54.9 0.1 fusion
  55.0 0.0 copy-start
  55.1 1.2 %collective-permute-done.3.refs_1_ = bf16[1024,128]{1,0:T(8,128)(2,1)S(1)} collective-permute-done((bf16[1024,128]{1,0:T(8,128)(2,1)}, bf16[1024,128]{1,0:T(8,128)(2,1)S(1)}, u32[]{:S(2)}, u32[]{:S(2)}) %collective-permute-start.3) | collective-permute-done | bytes 262176 | tf_op jit(solution)/shard_map/ppermute | solution.py:42
  56.2 0.0 collective-permute-done.4.refs_3_
  56.2 0.0 copy-done
  56.2 1.6 %shard_map.90 = bf16[1024,256]{1,0:T(8,128)(2,1)} custom-call(bf16[4,256,128]{2,1,0:T(8,128)(2,1)S(1)} %pad_maximum_fusion.coeffs_ref, bf16[1024,128]{1,0:T(8,128)(2,1)S(1)} %copy-done, bf16[1024,128]{1,0:T(8,128)(2,1)S(1)} %collective-permute-done.3.refs_1_, bf16[2048,128]{1,0:T(8,128)(2,1)S(1)} %collective-permute-done.2.refs_2_, ...), custom_call_target="tpu_custom_call" | custom-call | tf_op jit(solution)/shard_map/pallas_call | solution.py:187
  57.8 6.0 %all-to-all-start.2 = ((bf16[16,64,256]{2,1,0:T(8,128)(2,1)}), bf16[16,64,256]{2,1,0:T(8,128)(2,1)S(1)}, u32[]{:S(2)}, u32[]{:S(2)}) async-start(bf16[16,64,256]{2,1,0:T(8,128)(2,1)} %bitcast.12), calls=%async_computation.2 | async-start | bytes 1048576 | tf_op jit(solution)/shard_map/all_to_all | solution.py:46
  63.9 15.8 %all-to-all-done.2 = bf16[16,64,256]{2,1,0:T(8,128)(2,1)S(1)} async-done(((bf16[16,64,256]{2,1,0:T(8,128)(2,1)}), bf16[16,64,256]{2,1,0:T(8,128)(2,1)S(1)}, u32[]{:S(2)}, u32[]{:S(2)}) %all-to-all-start.2) | async-done | bytes 524320 | tf_op jit(solution)/shard_map/all_to_all | solution.py:46
  79.7 0.1 reduce_sum.21
  79.9 25.6 %all_to_all.20 = bf16[8,96,256]{2,1,0:T(8,128)(2,1)S(1)} all-to-all(bf16[8,96,256]{2,1,0:T(8,128)(2,1)S(1)} %broadcast_in_dim.11), channel_id=1, replica_groups=mesh['rep'=8,'seq'=64] {'rep'}, dimensions={0} | all-to-all | bytes 786432 | tf_op jit(solution)/shard_map/all_to_all | solution.py:46
  105.6 0.8 convolution_multiply_fusion
  (7 shorter events, 0.1 us)
Async XLA Ops:
  3.4 18.2 %collective-permute-start.1 = (bf16[128,1152]{1,0:T(8,128)(2,1)}, bf16[128,1152]{1,0:T(8,128)(2,1)S(1)}, u32[]{:S(2)}, u32[]{:S(2)}) collective-permute-start(bf16[128,1152]{1,0:T(8,128)(2,1)} %get-tuple-element.13.own_hbm), channel_id=1, source_target_pairs={{0,2},{1,3},{2,4},{3,5},{4,6},{5,7},{6,8},{7,9},{8,10},{9,11},{10,... | collective-permute-start | bytes 884744 | tf_op jit(solution)/shard_map/ppermute | solution.py:38
  6.9 14.7 %collective-permute-start = (bf16[128,1152]{1,0:T(8,128)(2,1)}, bf16[128,1152]{1,0:T(8,128)(2,1)S(1)}, u32[]{:S(2)}, u32[]{:S(2)}) collective-permute-start(bf16[128,1152]{1,0:T(8,128)(2,1)} %get-tuple-element.13.own_hbm), channel_id=1, source_target_pairs={{0,1},{1,2},{2,3},{3,4},{4,5},{5,6},{6,7},{7,8},{8,9},{9,10},{10,1... | collective-permute-start | bytes 884744 | tf_op jit(solution)/shard_map/ppermute | solution.py:38
  8.8 21.7 %all-to-all-start = ((bf16[64,4,256]{2,1,0:T(4,128)(2,1)}), bf16[64,4,256]{2,1,0:T(4,128)(2,1)S(1)}, u32[]{:S(2)}, u32[]{:S(2)}) async-start(bf16[64,4,256]{2,1,0:T(4,128)(2,1)} %get-tuple-element.16), calls=%async_computation | async-start | bytes 262144 | tf_op jit(solution)/shard_map/all_to_all | solution.py:46
  21.6 0.7 copy-start.1
  21.6 0.8 copy-start.2
  30.5 20.1 %collective-permute-start.2 = (bf16[2048,128]{1,0:T(8,128)(2,1)}, bf16[2048,128]{1,0:T(8,128)(2,1)S(1)}, u32[]{:S(2)}, u32[]{:S(2)}) collective-permute-start(bf16[2048,128]{1,0:T(8,128)(2,1)} %get-tuple-element.21), channel_id=1, source_target_pairs={{0,16},{1,17},{2,18},{3,19},{4,20},{5,21},{6,22},{7,23},{8,24},{9,... | collective-permute-start | bytes 1572872 | tf_op jit(solution)/shard_map/ppermute | solution.py:42
  34.2 20.7 %all-to-all-start.1 = ((bf16[64,4,640]{2,1,0:T(4,128)(2,1)}), bf16[64,4,640]{2,1,0:T(4,128)(2,1)S(1)}, u32[]{:S(2)}, u32[]{:S(2)}) async-start(bf16[64,4,640]{2,1,0:T(4,128)(2,1)} %shard_map.89), calls=%async_computation.1 | async-start | bytes 655360 | tf_op jit(solution)/shard_map/all_to_all | solution.py:46
  50.6 5.7 %collective-permute-start.4 = (bf16[2048,128]{1,0:T(8,128)(2,1)S(1)}, bf16[2048,128]{1,0:T(8,128)(2,1)S(1)}, u32[]{:S(2)}, u32[]{:S(2)}) collective-permute-start(bf16[2048,128]{1,0:T(8,128)(2,1)S(1)} %collective-permute-done.2.refs_2_), channel_id=1, source_target_pairs={{0,1},{1,0},{2,3},{3,2},{4,5},{5,4},{6,7},{7,6},{8,9},{9,8},{10,11... | collective-permute-start | bytes 1572872 | tf_op jit(solution)/shard_map/ppermute | solution.py:42
  52.5 3.8 %collective-permute-start.3 = (bf16[1024,128]{1,0:T(8,128)(2,1)}, bf16[1024,128]{1,0:T(8,128)(2,1)S(1)}, u32[]{:S(2)}, u32[]{:S(2)}) collective-permute-start(bf16[1024,128]{1,0:T(8,128)(2,1)} %get-tuple-element.22), channel_id=1, source_target_pairs={{0,1},{1,0},{2,3},{3,2},{4,5},{5,4},{6,7},{7,6},{8,9},{9,8},{10,11... | collective-permute-start | bytes 786440 | tf_op jit(solution)/shard_map/ppermute | solution.py:42
  55.0 1.2 %copy-start = (bf16[1024,128]{1,0:T(8,128)(2,1)S(1)}, bf16[1024,128]{1,0:T(8,128)(2,1)}, u32[]{:S(2)}) copy-start(bf16[1024,128]{1,0:T(8,128)(2,1)} %get-tuple-element.19.refs_0_) | copy-start | bytes 786436
  57.8 21.9 %all-to-all-start.2 = ((bf16[16,64,256]{2,1,0:T(8,128)(2,1)}), bf16[16,64,256]{2,1,0:T(8,128)(2,1)S(1)}, u32[]{:S(2)}, u32[]{:S(2)}) async-start(bf16[16,64,256]{2,1,0:T(8,128)(2,1)} %bitcast.12), calls=%async_computation.2 | async-start | bytes 1048576 | tf_op jit(solution)/shard_map/all_to_all | solution.py:46

commit v6 on v4

--- a/solution.py
+++ b/solution.py
@@ -1,3 +1,4 @@
+import functools
 import math
 
 import jax
@@ -47,10 +48,14 @@
     )
 
 
-def attention_kernel(
-    place_ref, q_ref, own_ref, one_ref, two_ref, out_ref, keep_ref, near_ref, far_ref
-):
-    core, odd = place_ref[0], place_ref[1]
+def attention_kernel(other, q_ref, own_ref, one_ref, two_ref, *refs):
+    if other == 0:
+        half_ref, out_ref, mine_ref, theirs_ref = refs
+    else:
+        half_ref, mine_ref = refs
+        theirs_ref = mine_ref
+    seq = lax.axis_index("seq")
+    core, odd = seq & 1, (seq >> 4) & 1
     square = (TOKENS, TOKENS)
     lower = lax.broadcasted_iota(jnp.int32, square, 0) <= lax.broadcasted_iota(jnp.int32, square, 1)
     tags = lambda block: block[:, 2 * KV :].astype(jnp.float32)
@@ -62,8 +67,8 @@
     hidden = jnp.float32(-1e30)
     factor = HEAD_SIZE ** (-0.5) * LOG2E
     column = lambda start: pl.ds(pl.multiple_of(start, HEAD_SIZE), HEAD_SIZE)
-    for step in range(KEY_VALUE_HEADS):
-        other, z2 = step // 2, step % 2
+    span = GROUP * HEAD_SIZE
+    for z2 in range(2):
         z = z2 * 2 + (odd if other == 0 else 1 - odd)
         at = z * HEAD_SIZE
         turned = [
@@ -95,34 +100,42 @@
         )
         for j in range(GROUP):
             head = mixed[:, j * HEAD_SIZE : (j + 1) * HEAD_SIZE]
-            out_ref[:, column(heads[j])] = head.T.astype(jnp.bfloat16)
+            turned = head.T.astype(jnp.bfloat16)
+            if other == 0:
+                out_ref[:, column(heads[j])] = turned
+            else:
+                at = z2 * span + j * HEAD_SIZE
+                half_ref[:, at : at + HEAD_SIZE] = turned
             low, high = head[:HALF], head[HALF:]
             row = (z2 * 8 + j) * HALF
-            mine = jnp.where(core == 0, low, high).astype(jnp.bfloat16)
-            theirs = jnp.where(core == 0, high, low).astype(jnp.bfloat16)
-            if other == 0:
-                keep_ref[row : row + HALF, :] = mine
-                near_ref[row : row + HALF, :] = theirs
-            else:
-                far_ref[row : row + HALF, :] = mine
-                far_ref[ROWS + row : ROWS + row + HALF, :] = theirs
-
-
-def attention(place, q, own, one, two):
+            shift = other * ROWS
+            mine_ref[row : row + HALF, :] = jnp.where(core == 0, low, high).astype(jnp.bfloat16)
+            theirs_ref[shift + row : shift + row + HALF, :] = jnp.where(
+                core == 0, high, low
+            ).astype(jnp.bfloat16)
+        if other == 0:
+            away = pl.ds(pl.multiple_of((z2 * 2 + 1 - odd) * span, span), span)
+            out_ref[:, away] = half_ref[:, z2 * span : (z2 + 1) * span]
+
+
+def attention(other, q, own, one, two, *half):
     vmem = pl.BlockSpec(memory_space=pltpu.VMEM)
+    width = QUERY_HEADS * HEAD_SIZE
+    shapes = [(TOKENS, width // 2), (2 * ROWS, TOKENS)]
+    if other == 0:
+        shapes = [(TOKENS, width), (ROWS, TOKENS), (ROWS, TOKENS)]
     return pl.pallas_call(
-        attention_kernel,
-        out_shape=[jax.ShapeDtypeStruct((TOKENS, QUERY_HEADS * HEAD_SIZE), jnp.bfloat16)]
-        + [jax.ShapeDtypeStruct((n * ROWS, TOKENS), jnp.bfloat16) for n in (1, 1, 2)],
-        in_specs=[pl.BlockSpec(memory_space=pltpu.SMEM)] + [vmem] * 4,
-        out_specs=[vmem] * 4,
+        functools.partial(attention_kernel, other),
+        out_shape=[jax.ShapeDtypeStruct(shape, jnp.bfloat16) for shape in shapes],
+        in_specs=[vmem] * (4 + len(half)),
+        out_specs=[vmem] * len(shapes),
         compiler_params=pltpu.CompilerParams(vmem_limit_bytes=VMEM_LIMIT),
         cost_estimate=pl.CostEstimate(
-            flops=4 * QUERY_HEADS * TOKENS * 3 * TOKENS * HEAD_SIZE * 6,
-            bytes_accessed=4 << 20,
-            transcendentals=QUERY_HEADS * TOKENS * 2 * TOKENS,
-        ),
-    )(place, q, own, one, two)
+            flops=1 << 20, bytes_accessed=1 << 18, transcendentals=1 << 10
+        )
+        if other
+        else pl.CostEstimate(flops=3 << 30, bytes_accessed=2 << 20, transcendentals=1 << 19),
+    )(q, own, one, two, *half)
 
 
 def outer_kernel(coeffs_ref, *refs):
@@ -157,8 +170,7 @@
 
 
 def pack_kernel(
-    rep_ref,
-    dest_ref,
+    dest_hbm,
     keys_hbm,
     values_hbm,
     tag_hbm,
@@ -166,6 +178,7 @@
     basis_hbm,
     own_ref,
     out_ref,
+    dest_ref,
     tag_ref,
     coeffs_ref,
     basis_ref,
@@ -178,6 +191,7 @@
         (basis_hbm, basis_ref),
         (keys_hbm, own_ref.at[:, :KV]),
         (values_hbm, own_ref.at[:, KV : 2 * KV]),
+        (dest_hbm, dest_ref),
     )
     copies = [pltpu.make_async_copy(a, b, sems.at[i]) for i, (a, b) in enumerate(pairs)]
     for copy in copies:
@@ -189,7 +203,7 @@
     out_ref[:, :, :TOKENS] = coeffs_ref[...].astype(f32).T.reshape(PIECES).astype(bf16)
     copies[2].wait()
     count = R // REP
-    mine = basis_ref[pl.ds(pl.multiple_of(rep_ref[0] * count, count), count), :]
+    mine = basis_ref[pl.ds(pl.multiple_of(lax.axis_index("rep") * count, count), count), :]
     gram = lax.dot_general(mine, basis_ref[...], NT, preferred_element_type=f32)
     gram = jnp.concatenate([gram[:, :TOKENS], gram[:, TOKENS:]], axis=0).astype(bf16)
     row = lax.broadcasted_iota(jnp.int32, (R, SEQ), 0)
@@ -197,15 +211,15 @@
     spread = jnp.where(row == column * 4, 1.0, 0.0).astype(bf16)
     extra = jnp.dot(spread, gram, preferred_element_type=f32)
     row = lax.broadcasted_iota(jnp.int32, (R, TOKENS), 0)
+    copies[5].wait()
     extra = jnp.where(row % 4 == 0, extra, dest_ref[0, 0].astype(f32))
     out_ref[:, :, TOKENS:] = extra.reshape(PIECES).astype(bf16)
     copies[3].wait()
     copies[4].wait()
 
 
-def pack(rep, dest, keys, values, tag, coeffs, basis):
+def pack(dest, keys, values, tag, coeffs, basis):
     vmem = pl.BlockSpec(memory_space=pltpu.VMEM)
-    smem = pl.BlockSpec(memory_space=pltpu.SMEM)
     hbm = pl.BlockSpec(memory_space=pltpu.HBM)
     return pl.pallas_call(
         pack_kernel,
@@ -213,16 +227,17 @@
             jax.ShapeDtypeStruct((TOKENS, 2 * KV + TOKENS), jnp.bfloat16),
             jax.ShapeDtypeStruct((SEQ, 4, 2 * TOKENS), jnp.bfloat16),
         ),
-        in_specs=[smem, smem] + [hbm] * 5,
+        in_specs=[hbm] * 6,
         out_specs=(vmem, vmem),
         scratch_shapes=[
+            pltpu.SMEM(dest.shape, dest.dtype),
             pltpu.VMEM(tag.shape, tag.dtype),
             pltpu.VMEM(coeffs.shape, coeffs.dtype),
             pltpu.VMEM(basis.shape, basis.dtype),
-            pltpu.SemaphoreType.DMA((5,)),
+            pltpu.SemaphoreType.DMA((6,)),
         ],
         compiler_params=pltpu.CompilerParams(vmem_limit_bytes=PACK_VMEM_LIMIT),
-    )(rep, dest, keys, values, tag, coeffs, basis)
+    )(dest, keys, values, tag, coeffs, basis)
 
 
 def sort_kernel(first_ref, out_ref):
@@ -258,23 +273,22 @@
 
 
 def local(queries, keys, values, doc_ids, coeffs, shard_dest, basis):
-    rep = lax.axis_index("rep").astype(jnp.int32)
-    seq = lax.axis_index("seq").astype(jnp.int32)
     bf16 = jnp.bfloat16
 
-    own, packed = pack(rep[None], shard_dest, keys[0], values[0], doc_ids, coeffs[0], basis)
+    own, packed = pack(shard_dest, keys[0], values[0], doc_ids, coeffs[0], basis)
     two = shifted(own, 2)
     one = shifted(own, 1)
     first = exchange(packed, "seq")
 
-    place = jnp.stack([seq & 1, (seq >> 4) & 1])
-    attended, keep, near, far = attention(place, queries[0], own, one, two)
-    first, keep = lax.optimization_barrier((first, keep))
+    half, far = attention(1, queries[0], own, one, two)
+    first, half = lax.optimization_barrier((first, half))
+    far = swapped(far, 16)
+
+    second = exchange(sort(first), "seq")
+    attended, keep, near = attention(0, queries[0], own, one, two, half)
+    near, far = lax.optimization_barrier((near, far))
     near = swapped(near, 1)
-    far = swapped(far, 16)
     farthest = swapped(far, 1)
-
-    second = exchange(sort(first), "seq")
 
     lined = jnp.stack(
         [second[:, :, m * TOKENS : (m + 1) * TOKENS].reshape(R, TOKENS) for m in range(MEMBERS)]

time: 104 us -> 103 us (level)
  waiting for transfers between devices: 23.6 us -> 20.8 us
  local copies, waits for them, and re-layouts: 2.35 us -> 4.06 us
    ppermute x3, waiting for transfers between devices: 1.55 us -> 0.01 us  [swapped(): return lax.ppermute(block, 'seq', [(i, i ^ partner) for i in range(SEQ)])]
    all_to_all x3, waiting for transfers between devices: 22 us -> 20.8 us  [exchange(): lax.all_to_all(block, axis, split_axis=0, concat_axis=0, axis_index_group...]
    pallas_call x1 -> x2, Pallas kernels: 4.75 us -> 5.13 us  [attention(): pl.pallas_call(functools.partial(attention_kernel, other), out_shape=[jax...]
    unnamed x5 -> x9, local copies, waits for them, and re-layouts: 2.19 us -> 2.19 us
  transfers between devices with their start and end apart: 8 -> 8, of which waited for: 3 -> 3; matrix products, arithmetic and copies ran while one was open for 0% -> 2% of each run, Pallas kernels for 6% -> 6%
where the time goes in v6:
time: 103 us; the launch traced here: 102 us
  starting transfers between devices  39.6 us (38%)
  blocking collectives  25.5 us (25%)
  waiting for transfers between devices  20.8 us (20%)
  Pallas kernels  9.95 us (10%)
  local copies, waits for them, and re-layouts  4.06 us (4%)
  between operations  1.45 us (1%)
    all_to_all x3, starting transfers between devices, exchange(): lax.all_to_all(block, axis, split_axis=0, concat_axis=0, axis_index_group...  26.4 us
    all_to_all x1, blocking collectives, exchange(): lax.all_to_all(block, axis, split_axis=0, concat_axis=0, axis_index_group...  25.5 us
    all_to_all x3, waiting for transfers between devices, exchange(): lax.all_to_all(block, axis, split_axis=0, concat_axis=0, axis_index_group...  20.8 us
    ppermute x3, starting transfers between devices, swapped(): return lax.ppermute(block, 'seq', [(i, i ^ partner) for i in range(SEQ)])  7.77 us
    ppermute x2, starting transfers between devices, shifted(): lax.ppermute(block, 'seq', [(i, i + distance) for i in range(SEQ - distan...  5.4 us
    pallas_call x2, Pallas kernels, attention(): pl.pallas_call(functools.partial(attention_kernel, other), out_shape=[jax...  5.13 us
    unnamed x9, local copies, waits for them, and re-layouts  2.19 us
    pallas_call x1, Pallas kernels, pack(): pl.pallas_call(pack_kernel, out_shape=(jax.ShapeDtypeStruct((TOKENS, 2 *...  2.11 us
  transfers between devices with their start and end apart: 8, of which 3 were waited for; matrix products, arithmetic and copies ran while one was open for 2% of the time, Pallas kernels for 6%

profile of v6, /device:TPU:136, one launch (start us, length us, event | category | flops | bytes accessed | tf_op | source)
XLA Modules:
  0.0 102.4 jit_solution(14962509271391640247)
XLA Ops:
  1.3 2.1 %shard_map.86 = (bf16[128,1152]{1,0:T(8,128)(2,1)}, bf16[64,4,256]{2,1,0:T(4,128)(2,1)}) custom-call(s32[1,1]{1,0:T(1,128)S(6)} %copy.14.dest_hbm, bf16[128,512]{1,0:T(8,128)(2,1)} %bitcast.24, bf16[128,512]{1,0:T(8,128)(2,1)} %bitcast.25, s32[1,128]{1,0:T(1,128)} %tag_hbm.1, bf16[128,256]{1,0:T(8,128)(2,1)} %bitcast.26, bf16[256,128]{1,0:T(8,128)(2,1)} %basis_hbm.1), custom_call_target="tpu_custom_call" | custom-call | tf_op jit(solution)/shard_map/pallas_call | solution.py:224
  3.4 3.5 %collective-permute-start.1 = (bf16[128,1152]{1,0:T(8,128)(2,1)}, bf16[128,1152]{1,0:T(8,128)(2,1)S(1)}, u32[]{:S(2)}, u32[]{:S(2)}) collective-permute-start(bf16[128,1152]{1,0:T(8,128)(2,1)} %get-tuple-element.13.own_ref), channel_id=1, source_target_pairs={{0,2},{1,3},{2,4},{3,5},{4,6},{5,7},{6,8},{7,9},{8,10},{9,11},{10,... | collective-permute-start | bytes 884744 | tf_op jit(solution)/shard_map/ppermute | solution.py:38
  6.9 1.9 %collective-permute-start = (bf16[128,1152]{1,0:T(8,128)(2,1)}, bf16[128,1152]{1,0:T(8,128)(2,1)S(1)}, u32[]{:S(2)}, u32[]{:S(2)}) collective-permute-start(bf16[128,1152]{1,0:T(8,128)(2,1)} %get-tuple-element.13.own_ref), channel_id=1, source_target_pairs={{0,1},{1,2},{2,3},{3,4},{4,5},{5,6},{6,7},{7,8},{8,9},{9,10},{10,1... | collective-permute-start | bytes 884744 | tf_op jit(solution)/shard_map/ppermute | solution.py:38
  8.8 11.3 %all-to-all-start = ((bf16[64,4,256]{2,1,0:T(4,128)(2,1)}), bf16[64,4,256]{2,1,0:T(4,128)(2,1)S(1)}, u32[]{:S(2)}, u32[]{:S(2)}) async-start(bf16[64,4,256]{2,1,0:T(4,128)(2,1)} %get-tuple-element.14), calls=%async_computation | async-start | bytes 262144 | tf_op jit(solution)/shard_map/all_to_all | solution.py:46
  20.1 0.0 collective-permute-done.1.two_ref
  20.2 0.0 collective-permute-done.one_ref
  20.2 0.0 copy-start
  20.2 1.2 %copy-done = bf16[1,128,4096]{2,1,0:T(8,128)(2,1)S(1)} copy-done((bf16[1,128,4096]{2,1,0:T(8,128)(2,1)S(1)}, bf16[1,128,4096]{2,1,0:T(8,128)(2,1)}, u32[]{:S(2)}) %copy-start) | copy-done | bytes 1048600
  21.4 0.0 copy-start.2
  21.4 1.0 copy-done.2
  22.4 0.0 copy-start.1
  22.4 2.4 %shard_map.87 = (bf16[128,2048]{1,0:T(8,128)(2,1)S(1)}, bf16[2048,128]{1,0:T(8,128)(2,1)}) custom-call(bf16[128,4096]{1,0:T(8,128)(2,1)S(1)} %bitcast.17, bf16[128,1152]{1,0:T(8,128)(2,1)S(1)} %copy-done.2, bf16[128,1152]{1,0:T(8,128)(2,1)S(1)} %collective-permute-done.one_ref, bf16[128,1152]{1,0:T(8,128)(2,1)S(1)} %collective-permute-done.1.two_ref), custom_call_target="tpu_custom_call" | custom-call | flops 1048576 | bytes 262144 | tf_op jit(solution)/shard_map/pallas_call | solution.py:127
  24.8 3.5 %collective-permute-start.2 = (bf16[2048,128]{1,0:T(8,128)(2,1)}, bf16[2048,128]{1,0:T(8,128)(2,1)S(1)}, u32[]{:S(2)}, u32[]{:S(2)}) collective-permute-start(bf16[2048,128]{1,0:T(8,128)(2,1)} %get-tuple-element.21), channel_id=1, source_target_pairs={{0,16},{1,17},{2,18},{3,19},{4,20},{5,21},{6,22},{7,23},{8,24},{9,... | collective-permute-start | bytes 1572872 | tf_op jit(solution)/shard_map/ppermute | solution.py:42
  28.2 0.8 all-to-all-done.first_ref
  29.1 1.1 %shard_map.89 = bf16[64,4,640]{2,1,0:T(4,128)(2,1)} custom-call(bf16[64,4,256]{2,1,0:T(4,128)(2,1)S(1)} %all-to-all-done.first_ref), custom_call_target="tpu_custom_call" | custom-call | tf_op jit(solution)/shard_map/pallas_call | solution.py:266
  30.2 0.0 copy-start.3
  30.2 9.2 %all-to-all-start.1 = ((bf16[64,4,640]{2,1,0:T(4,128)(2,1)}), bf16[64,4,640]{2,1,0:T(4,128)(2,1)}, u32[]{:S(2)}, u32[]{:S(2)}) async-start(bf16[64,4,640]{2,1,0:T(4,128)(2,1)} %shard_map.89), calls=%async_computation.1 | async-start | bytes 655360 | tf_op jit(solution)/shard_map/all_to_all | solution.py:46
  39.4 0.0 copy-done.1
  39.4 0.0 copy-done.3
  39.4 2.7 %shard_map.88 = (bf16[128,4096]{1,0:T(8,128)(2,1)}, bf16[1024,128]{1,0:T(8,128)(2,1)S(1)}, bf16[1024,128]{1,0:T(8,128)(2,1)}) custom-call(bf16[128,4096]{1,0:T(8,128)(2,1)S(1)} %bitcast.18, bf16[128,1152]{1,0:T(8,128)(2,1)S(1)} %copy-done.3, bf16[128,1152]{1,0:T(8,128)(2,1)S(1)} %collective-permute-done.one_ref, ...), custom_call_target="tpu_custom_call" | custom-call | flops 3221225472 | bytes 2097152 | tf_op jit(solution)/shard_map/pallas_call | solution.py:127
  42.1 0.0 collective-permute-done.2.refs_2_
  42.1 2.0 %collective-permute-start.4 = (bf16[2048,128]{1,0:T(8,128)(2,1)S(1)}, bf16[2048,128]{1,0:T(8,128)(2,1)S(1)}, u32[]{:S(2)}, u32[]{:S(2)}) collective-permute-start(bf16[2048,128]{1,0:T(8,128)(2,1)S(1)} %collective-permute-done.2.refs_2_), channel_id=1, source_target_pairs={{0,1},{1,0},{2,3},{3,2},{4,5},{5,4},{6,7},{7,6},{8,9},{9,8},{10,11... | collective-permute-start | bytes 1572872 | tf_op jit(solution)/shard_map/ppermute | solution.py:42
  44.2 2.3 %collective-permute-start.3 = (bf16[1024,128]{1,0:T(8,128)(2,1)}, bf16[1024,128]{1,0:T(8,128)(2,1)S(1)}, u32[]{:S(2)}, u32[]{:S(2)}) collective-permute-start(bf16[1024,128]{1,0:T(8,128)(2,1)} %get-tuple-element.22), channel_id=1, source_target_pairs={{0,1},{1,0},{2,3},{3,2},{4,5},{5,4},{6,7},{7,6},{8,9},{9,8},{10,11... | collective-permute-start | bytes 786440 | tf_op jit(solution)/shard_map/ppermute | solution.py:42
  46.5 5.5 %all-to-all-done.1 = bf16[64,4,640]{2,1,0:T(4,128)(2,1)} async-done(((bf16[64,4,640]{2,1,0:T(4,128)(2,1)}), bf16[64,4,640]{2,1,0:T(4,128)(2,1)}, u32[]{:S(2)}, u32[]{:S(2)}) %all-to-all-start.1) | async-done | bytes 327712 | tf_op jit(solution)/shard_map/all_to_all | solution.py:46
  51.9 1.0 %fusion = (bf16[64,4,128]{2,1,0:T(4,128)(2,1)S(1)}, bf16[64,4,128]{2,1,0:T(4,128)(2,1)S(1)}, bf16[64,4,128]{2,1,0:T(4,128)(2,1)S(1)}, bf16[64,4,128]{2,1,0:T(4,128)(2,1)S(1)}) fusion(bf16[64,4,640]{2,1,0:T(4,128)(2,1)} %all-to-all-done.1), kind=kLoop, calls=%fused_computation.6 | loop fusion | bytes 524288 | tf_op jit(solution)/shard_map/slice | solution.py:294
  53.0 0.0 collective-permute-done.3.refs_1_
  53.0 0.0 collective-permute-done.4.refs_3_
  53.0 1.6 %shard_map.90 = bf16[1024,256]{1,0:T(8,128)(2,1)} custom-call(bf16[4,256,128]{2,1,0:T(8,128)(2,1)S(1)} %pad_maximum_fusion.coeffs_ref, bf16[1024,128]{1,0:T(8,128)(2,1)S(1)} %get-tuple-element.19.refs_0_, bf16[1024,128]{1,0:T(8,128)(2,1)S(1)} %collective-permute-done.3.refs_1_, bf16[2048,128]{1,0:T(8,128)(2,1)S(1)} %collective-permute-done.2.refs_2_, ...), custom_call_target="tpu_custom_call" | custom-call | tf_op jit(solution)/shard_map/pallas_call | solution.py:153
  54.6 5.9 %all-to-all-start.2 = ((bf16[16,64,256]{2,1,0:T(8,128)(2,1)}), bf16[16,64,256]{2,1,0:T(8,128)(2,1)S(1)}, u32[]{:S(2)}, u32[]{:S(2)}) async-start(bf16[16,64,256]{2,1,0:T(8,128)(2,1)} %bitcast.9), calls=%async_computation.2 | async-start | bytes 1048576 | tf_op jit(solution)/shard_map/all_to_all | solution.py:46
  60.5 0.8 fusion.1
  61.3 14.5 %all-to-all-done.2 = bf16[16,64,256]{2,1,0:T(8,128)(2,1)S(1)} async-done(((bf16[16,64,256]{2,1,0:T(8,128)(2,1)}), bf16[16,64,256]{2,1,0:T(8,128)(2,1)S(1)}, u32[]{:S(2)}, u32[]{:S(2)}) %all-to-all-start.2) | async-done | bytes 524320 | tf_op jit(solution)/shard_map/all_to_all | solution.py:46
  75.8 0.1 reduce_sum.21
  75.9 25.5 %all_to_all.20 = bf16[8,96,256]{2,1,0:T(8,128)(2,1)S(1)} all-to-all(bf16[8,96,256]{2,1,0:T(8,128)(2,1)S(1)} %broadcast_in_dim.7), channel_id=1, replica_groups=mesh['rep'=8,'seq'=64] {'rep'}, dimensions={0} | all-to-all | bytes 786432 | tf_op jit(solution)/shard_map/all_to_all | solution.py:46
  101.5 0.8 convolution_multiply_fusion
  (6 shorter events, 0.1 us)
Async XLA Ops:
  3.4 16.8 %collective-permute-start.1 = (bf16[128,1152]{1,0:T(8,128)(2,1)}, bf16[128,1152]{1,0:T(8,128)(2,1)S(1)}, u32[]{:S(2)}, u32[]{:S(2)}) collective-permute-start(bf16[128,1152]{1,0:T(8,128)(2,1)} %get-tuple-element.13.own_ref), channel_id=1, source_target_pairs={{0,2},{1,3},{2,4},{3,5},{4,6},{5,7},{6,8},{7,9},{8,10},{9,11},{10,... | collective-permute-start | bytes 884744 | tf_op jit(solution)/shard_map/ppermute | solution.py:38
  6.9 13.3 %collective-permute-start = (bf16[128,1152]{1,0:T(8,128)(2,1)}, bf16[128,1152]{1,0:T(8,128)(2,1)S(1)}, u32[]{:S(2)}, u32[]{:S(2)}) collective-permute-start(bf16[128,1152]{1,0:T(8,128)(2,1)} %get-tuple-element.13.own_ref), channel_id=1, source_target_pairs={{0,1},{1,2},{2,3},{3,4},{4,5},{5,6},{6,7},{7,8},{8,9},{9,10},{10,1... | collective-permute-start | bytes 884744 | tf_op jit(solution)/shard_map/ppermute | solution.py:38
  8.8 20.2 %all-to-all-start = ((bf16[64,4,256]{2,1,0:T(4,128)(2,1)}), bf16[64,4,256]{2,1,0:T(4,128)(2,1)S(1)}, u32[]{:S(2)}, u32[]{:S(2)}) async-start(bf16[64,4,256]{2,1,0:T(4,128)(2,1)} %get-tuple-element.14), calls=%async_computation | async-start | bytes 262144 | tf_op jit(solution)/shard_map/all_to_all | solution.py:46
  20.2 1.2 %copy-start = (bf16[1,128,4096]{2,1,0:T(8,128)(2,1)S(1)}, bf16[1,128,4096]{2,1,0:T(8,128)(2,1)}, u32[]{:S(2)}) copy-start(bf16[1,128,4096]{2,1,0:T(8,128)(2,1)} %param.7) | copy-start | bytes 3145732
  21.4 1.0 copy-start.2
  22.4 17.0 %copy-start.1 = (bf16[1,128,4096]{2,1,0:T(8,128)(2,1)S(1)}, bf16[1,128,4096]{2,1,0:T(8,128)(2,1)}, u32[]{:S(2)}) copy-start(bf16[1,128,4096]{2,1,0:T(8,128)(2,1)} %param.7) | copy-start | bytes 3145732
  24.8 17.3 %collective-permute-start.2 = (bf16[2048,128]{1,0:T(8,128)(2,1)}, bf16[2048,128]{1,0:T(8,128)(2,1)S(1)}, u32[]{:S(2)}, u32[]{:S(2)}) collective-permute-start(bf16[2048,128]{1,0:T(8,128)(2,1)} %get-tuple-element.21), channel_id=1, source_target_pairs={{0,16},{1,17},{2,18},{3,19},{4,20},{5,21},{6,22},{7,23},{8,24},{9,... | collective-permute-start | bytes 1572872 | tf_op jit(solution)/shard_map/ppermute | solution.py:42
  30.2 9.2 %copy-start.3 = (bf16[128,1152]{1,0:T(8,128)(2,1)S(1)}, bf16[128,1152]{1,0:T(8,128)(2,1)}, u32[]{:S(2)}) copy-start(bf16[128,1152]{1,0:T(8,128)(2,1)} %get-tuple-element.13.own_ref) | copy-start | bytes 884740
  30.2 21.7 %all-to-all-start.1 = ((bf16[64,4,640]{2,1,0:T(4,128)(2,1)}), bf16[64,4,640]{2,1,0:T(4,128)(2,1)}, u32[]{:S(2)}, u32[]{:S(2)}) async-start(bf16[64,4,640]{2,1,0:T(4,128)(2,1)} %shard_map.89), calls=%async_computation.1 | async-start | bytes 655360 | tf_op jit(solution)/shard_map/all_to_all | solution.py:46
  42.1 10.9 %collective-permute-start.4 = (bf16[2048,128]{1,0:T(8,128)(2,1)S(1)}, bf16[2048,128]{1,0:T(8,128)(2,1)S(1)}, u32[]{:S(2)}, u32[]{:S(2)}) collective-permute-start(bf16[2048,128]{1,0:T(8,128)(2,1)S(1)} %collective-permute-done.2.refs_2_), channel_id=1, source_target_pairs={{0,1},{1,0},{2,3},{3,2},{4,5},{5,4},{6,7},{7,6},{8,9},{9,8},{10,11... | collective-permute-start | bytes 1572872 | tf_op jit(solution)/shard_map/ppermute | solution.py:42
  44.2 8.8 %collective-permute-start.3 = (bf16[1024,128]{1,0:T(8,128)(2,1)}, bf16[1024,128]{1,0:T(8,128)(2,1)S(1)}, u32[]{:S(2)}, u32[]{:S(2)}) collective-permute-start(bf16[1024,128]{1,0:T(8,128)(2,1)} %get-tuple-element.22), channel_id=1, source_target_pairs={{0,1},{1,0},{2,3},{3,2},{4,5},{5,4},{6,7},{7,6},{8,9},{9,8},{10,11... | collective-permute-start | bytes 786440 | tf_op jit(solution)/shard_map/ppermute | solution.py:42
  54.6 21.2 %all-to-all-start.2 = ((bf16[16,64,256]{2,1,0:T(8,128)(2,1)}), bf16[16,64,256]{2,1,0:T(8,128)(2,1)S(1)}, u32[]{:S(2)}, u32[]{:S(2)}) async-start(bf16[16,64,256]{2,1,0:T(8,128)(2,1)} %bitcast.9), calls=%async_computation.2 | async-start | bytes 1048576 | tf_op jit(solution)/shard_map/all_to_all | solution.py:46

commit v7 on v6

--- a/solution.py
+++ b/solution.py
@@ -138,16 +138,27 @@
     )(q, own, one, two, *half)
 
 
-def outer_kernel(coeffs_ref, *refs):
-    total = jnp.zeros(refs[-1].shape, jnp.float32)
-    for m in range(MEMBERS):
+def outer_kernel(second_ref, keep_ref, near_ref, far_ref, farthest_ref, out_ref, coeffs_ref):
+    pair = 2 * TOKENS
+
+    @pl.when(pl.program_id(0) == 0)
+    def _():
+        for p in range(MEMBERS // 2):
+            part = second_ref[:, :, p * pair : (p + 1) * pair].astype(jnp.float32)
+            coeffs_ref[p] = part.reshape(R, pair).astype(jnp.bfloat16)
+
+    total = jnp.zeros(out_ref.shape, jnp.float32)
+    for p, refs in enumerate(((keep_ref, near_ref), (far_ref, farthest_ref))):
         total += lax.dot_general(
-            refs[m][...], coeffs_ref[m], NT, preferred_element_type=jnp.float32
-        )
-    refs[-1][...] = total.astype(jnp.bfloat16)
-
-
-def outer(coeffs, keep, near, far, farthest):
+            jnp.concatenate([ref[...] for ref in refs], axis=1),
+            coeffs_ref[p],
+            NT,
+            preferred_element_type=jnp.float32,
+        )
+    out_ref[...] = total.astype(jnp.bfloat16)
+
+
+def outer(second, keep, near, far, farthest):
     step = ROWS // 2
     block = lambda first: pl.BlockSpec((step, TOKENS), lambda i: (i + first, 0))
     return pl.pallas_call(
@@ -155,15 +166,16 @@
         out_shape=jax.ShapeDtypeStruct((ROWS, R), jnp.bfloat16),
         grid=(ROWS // step,),
         in_specs=[
-            pl.BlockSpec((MEMBERS, R, TOKENS), lambda i: (0, 0, 0)),
+            pl.BlockSpec(second.shape, lambda i: (0, 0, 0)),
             block(0),
             block(0),
             block(0),
             block(ROWS // step),
         ],
         out_specs=pl.BlockSpec((step, R), lambda i: (i, 0)),
+        scratch_shapes=[pltpu.VMEM((MEMBERS // 2, R, 2 * TOKENS), jnp.bfloat16)],
         compiler_params=pltpu.CompilerParams(vmem_limit_bytes=VMEM_LIMIT),
-    )(coeffs, keep, near, far, farthest)
+    )(second, keep, near, far, farthest)
 
 
 PIECES = (SEQ, 4, TOKENS)
@@ -290,10 +302,7 @@
     near = swapped(near, 1)
     farthest = swapped(far, 1)
 
-    lined = jnp.stack(
-        [second[:, :, m * TOKENS : (m + 1) * TOKENS].reshape(R, TOKENS) for m in range(MEMBERS)]
-    )
-    partial = outer(lined, keep, near, far, farthest).reshape(SHARES, HALF, R)
+    partial = outer(second, keep, near, far, farthest).reshape(SHARES, HALF, R)
     arrived = exchange(partial, "seq", SIXTEENS)
     rows = jnp.sum(arrived.astype(jnp.float32), axis=0).astype(bf16)
     gram_rows = R // REP

time: 103 us -> 104 us (level)
  the two profiles are of different devices: /device:TPU:136 before, /device:TPU:72 now
where the time goes in v7:
time: 104 us; the launch traced here: 103 us
  starting transfers between devices  39.5 us (38%)
  blocking collectives  25.6 us (25%)
  waiting for transfers between devices  22 us (21%)
  Pallas kernels  9.79 us (9%)
  local copies, waits for them, and re-layouts  4.09 us (4%)
  between operations  1.44 us (1%)
    all_to_all x3, starting transfers between devices, exchange(): lax.all_to_all(block, axis, split_axis=0, concat_axis=0, axis_index_group...  27.3 us
    all_to_all x1, blocking collectives, exchange(): lax.all_to_all(block, axis, split_axis=0, concat_axis=0, axis_index_group...  25.6 us
    all_to_all x3, waiting for transfers between devices, exchange(): lax.all_to_all(block, axis, split_axis=0, concat_axis=0, axis_index_group...  22 us
    ppermute x3, starting transfers between devices, swapped(): return lax.ppermute(block, 'seq', [(i, i ^ partner) for i in range(SEQ)])  6.77 us
    ppermute x2, starting transfers between devices, shifted(): lax.ppermute(block, 'seq', [(i, i + distance) for i in range(SEQ - distan...  5.41 us
    pallas_call x2, Pallas kernels, attention(): pl.pallas_call(functools.partial(attention_kernel, other), out_shape=[jax...  5.1 us
    unnamed x13, local copies, waits for them, and re-layouts  4.02 us
    pallas_call x1, Pallas kernels, pack(): pl.pallas_call(pack_kernel, out_shape=(jax.ShapeDtypeStruct((TOKENS, 2 *...  2.15 us
  transfers between devices with their start and end apart: 8, of which 3 were waited for; matrix products, arithmetic and copies ran while one was open for 0% of the time, Pallas kernels for 6%

profile of v7, /device:TPU:72, one launch (start us, length us, event | category | flops | bytes accessed | tf_op | source)
XLA Modules:
  0.0 103.3 jit_solution(15142462328886585295)
XLA Ops:
  1.3 2.1 %shard_map.86 = (bf16[128,1152]{1,0:T(8,128)(2,1)}, bf16[64,4,256]{2,1,0:T(4,128)(2,1)}) custom-call(s32[1,1]{1,0:T(1,128)S(6)} %copy.14.dest_hbm, bf16[128,512]{1,0:T(8,128)(2,1)} %bitcast.16, bf16[128,512]{1,0:T(8,128)(2,1)} %bitcast.17, s32[1,128]{1,0:T(1,128)} %tag_hbm.1, bf16[128,256]{1,0:T(8,128)(2,1)} %bitcast.18, bf16[256,128]{1,0:T(8,128)(2,1)} %basis_hbm.1), custom_call_target="tpu_custom_call" | custom-call | tf_op jit(solution)/shard_map/pallas_call | solution.py:236
  3.4 3.5 %collective-permute-start.1 = (bf16[128,1152]{1,0:T(8,128)(2,1)}, bf16[128,1152]{1,0:T(8,128)(2,1)S(1)}, u32[]{:S(2)}, u32[]{:S(2)}) collective-permute-start(bf16[128,1152]{1,0:T(8,128)(2,1)} %get-tuple-element.13.own_ref), channel_id=1, source_target_pairs={{0,2},{1,3},{2,4},{3,5},{4,6},{5,7},{6,8},{7,9},{8,10},{9,11},{10,... | collective-permute-start | bytes 884744 | tf_op jit(solution)/shard_map/ppermute | solution.py:38
  6.9 1.9 %collective-permute-start = (bf16[128,1152]{1,0:T(8,128)(2,1)}, bf16[128,1152]{1,0:T(8,128)(2,1)S(1)}, u32[]{:S(2)}, u32[]{:S(2)}) collective-permute-start(bf16[128,1152]{1,0:T(8,128)(2,1)} %get-tuple-element.13.own_ref), channel_id=1, source_target_pairs={{0,1},{1,2},{2,3},{3,4},{4,5},{5,6},{6,7},{7,8},{8,9},{9,10},{10,1... | collective-permute-start | bytes 884744 | tf_op jit(solution)/shard_map/ppermute | solution.py:38
  8.9 12.1 %all-to-all-start = ((bf16[64,4,256]{2,1,0:T(4,128)(2,1)}), bf16[64,4,256]{2,1,0:T(4,128)(2,1)S(1)}, u32[]{:S(2)}, u32[]{:S(2)}) async-start(bf16[64,4,256]{2,1,0:T(4,128)(2,1)} %get-tuple-element.14), calls=%async_computation | async-start | bytes 262144 | tf_op jit(solution)/shard_map/all_to_all | solution.py:46
  21.0 0.0 collective-permute-done.1.two_ref
  21.0 0.0 collective-permute-done.one_ref
  21.0 0.0 copy-start
  21.0 1.2 %copy-done = bf16[1,128,4096]{2,1,0:T(8,128)(2,1)S(1)} copy-done((bf16[1,128,4096]{2,1,0:T(8,128)(2,1)S(1)}, bf16[1,128,4096]{2,1,0:T(8,128)(2,1)}, u32[]{:S(2)}) %copy-start) | copy-done | bytes 1048600
  22.2 0.0 copy-start.2
  22.2 1.0 copy-done.2
  23.2 0.0 copy-start.1
  23.2 2.4 %shard_map.87 = (bf16[128,2048]{1,0:T(8,128)(2,1)S(1)}, bf16[2048,128]{1,0:T(8,128)(2,1)}) custom-call(bf16[128,4096]{1,0:T(8,128)(2,1)S(1)} %bitcast.13, bf16[128,1152]{1,0:T(8,128)(2,1)S(1)} %copy-done.2, bf16[128,1152]{1,0:T(8,128)(2,1)S(1)} %collective-permute-done.one_ref, bf16[128,1152]{1,0:T(8,128)(2,1)S(1)} %collective-permute-done.1.two_ref), custom_call_target="tpu_custom_call" | custom-call | flops 1048576 | bytes 262144 | tf_op jit(solution)/shard_map/pallas_call | solution.py:127
  25.6 0.0 copy-start.4
  25.6 0.8 copy-done.4
  26.4 2.5 %collective-permute-start.2 = (bf16[2048,128]{1,0:T(8,128)(2,1)}, bf16[2048,128]{1,0:T(8,128)(2,1)S(1)}, u32[]{:S(2)}, u32[]{:S(2)}) collective-permute-start(bf16[2048,128]{1,0:T(8,128)(2,1)} %get-tuple-element.21), channel_id=1, source_target_pairs={{0,16},{1,17},{2,18},{3,19},{4,20},{5,21},{6,22},{7,23},{8,24},{9,... | collective-permute-start | bytes 1572872 | tf_op jit(solution)/shard_map/ppermute | solution.py:42
  28.9 1.6 %all-to-all-done.first_ref = bf16[64,4,256]{2,1,0:T(4,128)(2,1)S(1)} async-done(((bf16[64,4,256]{2,1,0:T(4,128)(2,1)}), bf16[64,4,256]{2,1,0:T(4,128)(2,1)S(1)}, u32[]{:S(2)}, u32[]{:S(2)}) %all-to-all-start) | async-done | bytes 131104 | tf_op jit(solution)/shard_map/all_to_all | solution.py:46
  30.5 1.1 %shard_map.89 = bf16[64,4,640]{2,1,0:T(4,128)(2,1)} custom-call(bf16[64,4,256]{2,1,0:T(4,128)(2,1)S(1)} %all-to-all-done.first_ref), custom_call_target="tpu_custom_call" | custom-call | tf_op jit(solution)/shard_map/pallas_call | solution.py:278
  31.6 0.0 copy-start.3
  31.6 9.2 %all-to-all-start.1 = ((bf16[64,4,640]{2,1,0:T(4,128)(2,1)}), bf16[64,4,640]{2,1,0:T(4,128)(2,1)S(1)}, u32[]{:S(2)}, u32[]{:S(2)}) async-start(bf16[64,4,640]{2,1,0:T(4,128)(2,1)} %shard_map.89), calls=%async_computation.1 | async-start | bytes 655360 | tf_op jit(solution)/shard_map/all_to_all | solution.py:46
  40.9 0.0 copy-done.1
  40.9 0.0 copy-done.3
  40.9 0.0 copy-start.5
  40.9 1.0 copy-done.5
  41.9 2.7 %shard_map.88 = (bf16[128,4096]{1,0:T(8,128)(2,1)}, bf16[1024,128]{1,0:T(8,128)(2,1)S(1)}, bf16[1024,128]{1,0:T(8,128)(2,1)S(1)}) custom-call(bf16[128,4096]{1,0:T(8,128)(2,1)S(1)} %bitcast.14, bf16[128,1152]{1,0:T(8,128)(2,1)S(1)} %copy-done.3, bf16[128,1152]{1,0:T(8,128)(2,1)S(1)} %collective-permute-done.one_ref, ...), custom_call_target="tpu_custom_call" | custom-call | flops 3221225472 | bytes 2097152 | tf_op jit(solution)/shard_map/pallas_call | solution.py:127
  44.6 0.0 collective-permute-done.2.far_ref
  44.6 2.0 %collective-permute-start.4 = (bf16[2048,128]{1,0:T(8,128)(2,1)S(1)}, bf16[2048,128]{1,0:T(8,128)(2,1)S(1)}, u32[]{:S(2)}, u32[]{:S(2)}) collective-permute-start(bf16[2048,128]{1,0:T(8,128)(2,1)S(1)} %collective-permute-done.2.far_ref), channel_id=1, source_target_pairs={{0,1},{1,0},{2,3},{3,2},{4,5},{5,4},{6,7},{7,6},{8,9},{9,8},{10,11... | collective-permute-start | bytes 1572872 | tf_op jit(solution)/shard_map/ppermute | solution.py:42
  46.7 2.3 %collective-permute-start.3 = (bf16[1024,128]{1,0:T(8,128)(2,1)S(1)}, bf16[1024,128]{1,0:T(8,128)(2,1)S(1)}, u32[]{:S(2)}, u32[]{:S(2)}) collective-permute-start(bf16[1024,128]{1,0:T(8,128)(2,1)S(1)} %get-tuple-element.22), channel_id=1, source_target_pairs={{0,1},{1,0},{2,3},{3,2},{4,5},{5,4},{6,7},{7,6},{8,9},{9,8},{10,11... | collective-permute-start | bytes 786440 | tf_op jit(solution)/shard_map/ppermute | solution.py:42
  48.9 4.5 %all-to-all-done.1.second_ref = bf16[64,4,640]{2,1,0:T(4,128)(2,1)S(1)} async-done(((bf16[64,4,640]{2,1,0:T(4,128)(2,1)}), bf16[64,4,640]{2,1,0:T(4,128)(2,1)S(1)}, u32[]{:S(2)}, u32[]{:S(2)}) %all-to-all-start.1) | async-done | bytes 327712 | tf_op jit(solution)/shard_map/all_to_all | solution.py:46
  53.4 0.0 collective-permute-done.3.near_ref
  53.4 0.0 collective-permute-done.4.farthest_ref
  53.4 1.4 %shard_map.90 = bf16[1024,256]{1,0:T(8,128)(2,1)} custom-call(bf16[64,4,640]{2,1,0:T(4,128)(2,1)S(1)} %all-to-all-done.1.second_ref, bf16[1024,128]{1,0:T(8,128)(2,1)S(1)} %get-tuple-element.19.keep_ref, bf16[1024,128]{1,0:T(8,128)(2,1)S(1)} %collective-permute-done.3.near_ref, bf16[2048,128]{1,0:T(8,128)(2,1)S(1)} %collective-permute-done.2.far_ref, ...), custom_call_target="tpu_custom_call" | custom-call | tf_op jit(solution)/shard_map/pallas_call | solution.py:164
  54.9 5.9 %all-to-all-start.2 = ((bf16[16,64,256]{2,1,0:T(8,128)(2,1)}), bf16[16,64,256]{2,1,0:T(8,128)(2,1)S(1)}, u32[]{:S(2)}, u32[]{:S(2)}) async-start(bf16[16,64,256]{2,1,0:T(8,128)(2,1)} %bitcast.5), calls=%async_computation.2 | async-start | bytes 1048576 | tf_op jit(solution)/shard_map/all_to_all | solution.py:46
  60.8 15.8 %all-to-all-done.2 = bf16[16,64,256]{2,1,0:T(8,128)(2,1)S(1)} async-done(((bf16[16,64,256]{2,1,0:T(8,128)(2,1)}), bf16[16,64,256]{2,1,0:T(8,128)(2,1)S(1)}, u32[]{:S(2)}, u32[]{:S(2)}) %all-to-all-start.2) | async-done | bytes 524320 | tf_op jit(solution)/shard_map/all_to_all | solution.py:46
  76.7 0.1 reduce_sum.21
  76.8 25.6 %all_to_all.20 = bf16[8,96,256]{2,1,0:T(8,128)(2,1)S(1)} all-to-all(bf16[8,96,256]{2,1,0:T(8,128)(2,1)S(1)} %broadcast_in_dim.7), channel_id=1, replica_groups=mesh['rep'=8,'seq'=64] {'rep'}, dimensions={0} | all-to-all | bytes 786432 | tf_op jit(solution)/shard_map/all_to_all | solution.py:46
  102.5 0.8 convolution_multiply_fusion
  (6 shorter events, 0.1 us)
Async XLA Ops:
  3.4 17.6 %collective-permute-start.1 = (bf16[128,1152]{1,0:T(8,128)(2,1)}, bf16[128,1152]{1,0:T(8,128)(2,1)S(1)}, u32[]{:S(2)}, u32[]{:S(2)}) collective-permute-start(bf16[128,1152]{1,0:T(8,128)(2,1)} %get-tuple-element.13.own_ref), channel_id=1, source_target_pairs={{0,2},{1,3},{2,4},{3,5},{4,6},{5,7},{6,8},{7,9},{8,10},{9,11},{10,... | collective-permute-start | bytes 884744 | tf_op jit(solution)/shard_map/ppermute | solution.py:38
  6.9 14.1 %collective-permute-start = (bf16[128,1152]{1,0:T(8,128)(2,1)}, bf16[128,1152]{1,0:T(8,128)(2,1)S(1)}, u32[]{:S(2)}, u32[]{:S(2)}) collective-permute-start(bf16[128,1152]{1,0:T(8,128)(2,1)} %get-tuple-element.13.own_ref), channel_id=1, source_target_pairs={{0,1},{1,2},{2,3},{3,4},{4,5},{5,6},{6,7},{7,8},{8,9},{9,10},{10,1... | collective-permute-start | bytes 884744 | tf_op jit(solution)/shard_map/ppermute | solution.py:38
  8.9 21.7 %all-to-all-start = ((bf16[64,4,256]{2,1,0:T(4,128)(2,1)}), bf16[64,4,256]{2,1,0:T(4,128)(2,1)S(1)}, u32[]{:S(2)}, u32[]{:S(2)}) async-start(bf16[64,4,256]{2,1,0:T(4,128)(2,1)} %get-tuple-element.14), calls=%async_computation | async-start | bytes 262144 | tf_op jit(solution)/shard_map/all_to_all | solution.py:46
  21.0 1.2 %copy-start = (bf16[1,128,4096]{2,1,0:T(8,128)(2,1)S(1)}, bf16[1,128,4096]{2,1,0:T(8,128)(2,1)}, u32[]{:S(2)}) copy-start(bf16[1,128,4096]{2,1,0:T(8,128)(2,1)} %param.7) | copy-start | bytes 3145732
  22.2 1.0 copy-start.2
  23.2 17.7 %copy-start.1 = (bf16[1,128,4096]{2,1,0:T(8,128)(2,1)S(1)}, bf16[1,128,4096]{2,1,0:T(8,128)(2,1)}, u32[]{:S(2)}) copy-start(bf16[1,128,4096]{2,1,0:T(8,128)(2,1)} %param.7) | copy-start | bytes 3145732
  25.6 0.8 copy-start.4
  26.4 18.2 %collective-permute-start.2 = (bf16[2048,128]{1,0:T(8,128)(2,1)}, bf16[2048,128]{1,0:T(8,128)(2,1)S(1)}, u32[]{:S(2)}, u32[]{:S(2)}) collective-permute-start(bf16[2048,128]{1,0:T(8,128)(2,1)} %get-tuple-element.21), channel_id=1, source_target_pairs={{0,16},{1,17},{2,18},{3,19},{4,20},{5,21},{6,22},{7,23},{8,24},{9,... | collective-permute-start | bytes 1572872 | tf_op jit(solution)/shard_map/ppermute | solution.py:42
  31.6 9.2 %copy-start.3 = (bf16[128,1152]{1,0:T(8,128)(2,1)S(1)}, bf16[128,1152]{1,0:T(8,128)(2,1)}, u32[]{:S(2)}) copy-start(bf16[128,1152]{1,0:T(8,128)(2,1)} %get-tuple-element.13.own_ref) | copy-start | bytes 884740
  31.6 21.8 %all-to-all-start.1 = ((bf16[64,4,640]{2,1,0:T(4,128)(2,1)}), bf16[64,4,640]{2,1,0:T(4,128)(2,1)S(1)}, u32[]{:S(2)}, u32[]{:S(2)}) async-start(bf16[64,4,640]{2,1,0:T(4,128)(2,1)} %shard_map.89), calls=%async_computation.1 | async-start | bytes 655360 | tf_op jit(solution)/shard_map/all_to_all | solution.py:46
  40.9 1.0 %copy-start.5 = (bf16[128,2048]{1,0:T(8,128)(2,1)S(1)}, bf16[128,2048]{1,0:T(8,128)(2,1)}, u32[]{:S(2)}) copy-start(bf16[128,2048]{1,0:T(8,128)(2,1)} %copy-done.4) | copy-start | bytes 1572868
  44.6 8.8 %collective-permute-start.4 = (bf16[2048,128]{1,0:T(8,128)(2,1)S(1)}, bf16[2048,128]{1,0:T(8,128)(2,1)S(1)}, u32[]{:S(2)}, u32[]{:S(2)}) collective-permute-start(bf16[2048,128]{1,0:T(8,128)(2,1)S(1)} %collective-permute-done.2.far_ref), channel_id=1, source_target_pairs={{0,1},{1,0},{2,3},{3,2},{4,5},{5,4},{6,7},{7,6},{8,9},{9,8},{10,11... | collective-permute-start | bytes 1572872 | tf_op jit(solution)/shard_map/ppermute | solution.py:42
  46.7 6.8 %collective-permute-start.3 = (bf16[1024,128]{1,0:T(8,128)(2,1)S(1)}, bf16[1024,128]{1,0:T(8,128)(2,1)S(1)}, u32[]{:S(2)}, u32[]{:S(2)}) collective-permute-start(bf16[1024,128]{1,0:T(8,128)(2,1)S(1)} %get-tuple-element.22), channel_id=1, source_target_pairs={{0,1},{1,0},{2,3},{3,2},{4,5},{5,4},{6,7},{7,6},{8,9},{9,8},{10,11... | collective-permute-start | bytes 786440 | tf_op jit(solution)/shard_map/ppermute | solution.py:42
  54.9 21.8 %all-to-all-start.2 = ((bf16[16,64,256]{2,1,0:T(8,128)(2,1)}), bf16[16,64,256]{2,1,0:T(8,128)(2,1)S(1)}, u32[]{:S(2)}, u32[]{:S(2)}) async-start(bf16[16,64,256]{2,1,0:T(8,128)(2,1)} %bitcast.5), calls=%async_computation.2 | async-start | bytes 1048576 | tf_op jit(solution)/shard_map/all_to_all | solution.py:46

commit v8 on v7

--- a/solution.py
+++ b/solution.py
@@ -49,11 +49,14 @@
 
 
 def attention_kernel(other, q_ref, own_ref, one_ref, two_ref, *refs):
+    slab_ref, sems = refs[-2:]
     if other == 0:
-        half_ref, out_ref, mine_ref, theirs_ref = refs
+        _, out_hbm, mine_ref, theirs_ref = refs[:-2]
     else:
-        half_ref, mine_ref = refs
+        out_hbm, mine_ref, mark_ref = refs[:-2]
         theirs_ref = mine_ref
+        mark_ref[...] = jnp.zeros(mark_ref.shape, mark_ref.dtype)
+    leaving = []
     seq = lax.axis_index("seq")
     core, odd = seq & 1, (seq >> 4) & 1
     square = (TOKENS, TOKENS)
@@ -100,12 +103,7 @@
         )
         for j in range(GROUP):
             head = mixed[:, j * HEAD_SIZE : (j + 1) * HEAD_SIZE]
-            turned = head.T.astype(jnp.bfloat16)
-            if other == 0:
-                out_ref[:, column(heads[j])] = turned
-            else:
-                at = z2 * span + j * HEAD_SIZE
-                half_ref[:, at : at + HEAD_SIZE] = turned
+            slab_ref[z2, :, j * HEAD_SIZE : (j + 1) * HEAD_SIZE] = head.T.astype(jnp.bfloat16)
             low, high = head[:HALF], head[HALF:]
             row = (z2 * 8 + j) * HALF
             shift = other * ROWS
@@ -113,29 +111,35 @@
             theirs_ref[shift + row : shift + row + HALF, :] = jnp.where(
                 core == 0, high, low
             ).astype(jnp.bfloat16)
-        if other == 0:
-            away = pl.ds(pl.multiple_of((z2 * 2 + 1 - odd) * span, span), span)
-            out_ref[:, away] = half_ref[:, z2 * span : (z2 + 1) * span]
-
-
-def attention(other, q, own, one, two, *half):
+        slab = pl.ds(pl.multiple_of(z * span, span), span)
+        leaving.append(pltpu.make_async_copy(slab_ref.at[z2], out_hbm.at[:, slab], sems.at[z2]))
+        leaving[z2].start()
+    for copy in leaving:
+        copy.wait()
+
+
+def attention(other, q, own, one, two, *attended):
     vmem = pl.BlockSpec(memory_space=pltpu.VMEM)
-    width = QUERY_HEADS * HEAD_SIZE
-    shapes = [(TOKENS, width // 2), (2 * ROWS, TOKENS)]
-    if other == 0:
-        shapes = [(TOKENS, width), (ROWS, TOKENS), (ROWS, TOKENS)]
+    hbm = pl.BlockSpec(memory_space=pltpu.HBM)
+    shapes = [(2 * ROWS, TOKENS), (16, TOKENS)] if other else [(ROWS, TOKENS), (ROWS, TOKENS)]
+    shapes = [(TOKENS, QUERY_HEADS * HEAD_SIZE)] + shapes
     return pl.pallas_call(
         functools.partial(attention_kernel, other),
         out_shape=[jax.ShapeDtypeStruct(shape, jnp.bfloat16) for shape in shapes],
-        in_specs=[vmem] * (4 + len(half)),
-        out_specs=[vmem] * len(shapes),
+        in_specs=[vmem] * 4 + [hbm] * len(attended),
+        out_specs=[hbm, vmem, vmem],
+        scratch_shapes=[
+            pltpu.VMEM((2, TOKENS, GROUP * HEAD_SIZE), jnp.bfloat16),
+            pltpu.SemaphoreType.DMA((2,)),
+        ],
+        input_output_aliases={4: 0} if attended else {},
         compiler_params=pltpu.CompilerParams(vmem_limit_bytes=VMEM_LIMIT),
         cost_estimate=pl.CostEstimate(
             flops=1 << 20, bytes_accessed=1 << 18, transcendentals=1 << 10
         )
         if other
         else pl.CostEstimate(flops=3 << 30, bytes_accessed=2 << 20, transcendentals=1 << 19),
-    )(q, own, one, two, *half)
+    )(q, own, one, two, *attended)
 
 
 def outer_kernel(second_ref, keep_ref, near_ref, far_ref, farthest_ref, out_ref, coeffs_ref):
@@ -252,7 +256,7 @@
     )(dest, keys, values, tag, coeffs, basis)
 
 
-def sort_kernel(first_ref, out_ref):
+def sort_kernel(first_ref, mark_ref, out_ref):
     f32, bf16 = jnp.float32, jnp.bfloat16
     pieces = first_ref[:, :, :TOKENS].astype(f32).reshape(R, TOKENS).astype(bf16)
     extra = first_ref[:, :, TOKENS:].astype(f32).reshape(R, TOKENS)
@@ -273,15 +277,15 @@
     )
 
 
-def sort(first):
+def sort(first, mark):
     vmem = pl.BlockSpec(memory_space=pltpu.VMEM)
     return pl.pallas_call(
         sort_kernel,
         out_shape=jax.ShapeDtypeStruct((SEQ, 4, (MEMBERS + 1) * TOKENS), jnp.bfloat16),
-        in_specs=[vmem],
+        in_specs=[vmem, vmem],
         out_specs=vmem,
         compiler_params=pltpu.CompilerParams(vmem_limit_bytes=VMEM_LIMIT),
-    )(first)
+    )(first, mark)
 
 
 def local(queries, keys, values, doc_ids, coeffs, shard_dest, basis):
@@ -292,12 +296,11 @@
     one = shifted(own, 1)
     first = exchange(packed, "seq")
 
-    half, far = attention(1, queries[0], own, one, two)
-    first, half = lax.optimization_barrier((first, half))
+    attended, far, mark = attention(1, queries[0], own, one, two)
     far = swapped(far, 16)
 
-    second = exchange(sort(first), "seq")
-    attended, keep, near = attention(0, queries[0], own, one, two, half)
+    second = exchange(sort(first, mark), "seq")
+    attended, keep, near = attention(0, queries[0], own, one, two, attended)
     near, far = lax.optimization_barrier((near, far))
     near = swapped(near, 1)
     farthest = swapped(far, 1)

time: 104 us -> 103 us (level)
  the two profiles are of different devices: /device:TPU:72 before, /device:TPU:64 now
where the time goes in v8:
time: 103 us; the launch traced here: 102 us
  starting transfers between devices  37.7 us (37%)
  waiting for transfers between devices  24.7 us (24%)
  blocking collectives  24.6 us (24%)
  Pallas kernels  10.4 us (10%)
  local copies, waits for them, and re-layouts  2.26 us (2%)
  between operations  1.46 us (1%)
    all_to_all x3, starting transfers between devices, exchange(): lax.all_to_all(block, axis, split_axis=0, concat_axis=0, axis_index_group...  25.6 us
    all_to_all x3, waiting for transfers between devices, exchange(): lax.all_to_all(block, axis, split_axis=0, concat_axis=0, axis_index_group...  24.7 us
    all_to_all x1, blocking collectives, exchange(): lax.all_to_all(block, axis, split_axis=0, concat_axis=0, axis_index_group...  24.6 us
    ppermute x3, starting transfers between devices, swapped(): return lax.ppermute(block, 'seq', [(i, i ^ partner) for i in range(SEQ)])  6.68 us
    pallas_call x2, Pallas kernels, attention(): pl.pallas_call(functools.partial(attention_kernel, other), out_shape=[jax...  5.67 us
    ppermute x2, starting transfers between devices, shifted(): lax.ppermute(block, 'seq', [(i, i + distance) for i in range(SEQ - distan...  5.41 us
    unnamed x9, local copies, waits for them, and re-layouts  2.19 us
    pallas_call x1, Pallas kernels, pack(): pl.pallas_call(pack_kernel, out_shape=(jax.ShapeDtypeStruct((TOKENS, 2 *...  2.13 us
  transfers between devices with their start and end apart: 8, of which 3 were waited for; matrix products, arithmetic and copies ran while one was open for 0% of the time, Pallas kernels for 7%

profile of v8, /device:TPU:64, one launch (start us, length us, event | category | flops | bytes accessed | tf_op | source)
XLA Modules:
  0.0 102.1 jit_solution(11737272288165528744)
XLA Ops:
  1.3 2.1 %shard_map.86 = (bf16[128,1152]{1,0:T(8,128)(2,1)}, bf16[64,4,256]{2,1,0:T(4,128)(2,1)}) custom-call(s32[1,1]{1,0:T(1,128)S(6)} %copy.16.dest_hbm, bf16[128,512]{1,0:T(8,128)(2,1)} %bitcast.16, bf16[128,512]{1,0:T(8,128)(2,1)} %bitcast.17, s32[1,128]{1,0:T(1,128)} %tag_hbm.1, bf16[128,256]{1,0:T(8,128)(2,1)} %bitcast.18, bf16[256,128]{1,0:T(8,128)(2,1)} %basis_hbm.1), custom_call_target="tpu_custom_call" | custom-call | tf_op jit(solution)/shard_map/pallas_call | solution.py:240
  3.4 3.5 %collective-permute-start.1 = (bf16[128,1152]{1,0:T(8,128)(2,1)}, bf16[128,1152]{1,0:T(8,128)(2,1)S(1)}, u32[]{:S(2)}, u32[]{:S(2)}) collective-permute-start(bf16[128,1152]{1,0:T(8,128)(2,1)} %get-tuple-element.12.own_ref), channel_id=1, source_target_pairs={{0,2},{1,3},{2,4},{3,5},{4,6},{5,7},{6,8},{7,9},{8,10},{9,11},{10,... | collective-permute-start | bytes 884744 | tf_op jit(solution)/shard_map/ppermute | solution.py:38
  6.9 1.9 %collective-permute-start = (bf16[128,1152]{1,0:T(8,128)(2,1)}, bf16[128,1152]{1,0:T(8,128)(2,1)S(1)}, u32[]{:S(2)}, u32[]{:S(2)}) collective-permute-start(bf16[128,1152]{1,0:T(8,128)(2,1)} %get-tuple-element.12.own_ref), channel_id=1, source_target_pairs={{0,1},{1,2},{2,3},{3,4},{4,5},{5,6},{6,7},{7,8},{8,9},{9,10},{10,1... | collective-permute-start | bytes 884744 | tf_op jit(solution)/shard_map/ppermute | solution.py:38
  8.8 12.2 %all-to-all-start = ((bf16[64,4,256]{2,1,0:T(4,128)(2,1)}), bf16[64,4,256]{2,1,0:T(4,128)(2,1)S(1)}, u32[]{:S(2)}, u32[]{:S(2)}) async-start(bf16[64,4,256]{2,1,0:T(4,128)(2,1)} %get-tuple-element.15), calls=%async_computation | async-start | bytes 262144 | tf_op jit(solution)/shard_map/all_to_all | solution.py:46
  21.1 0.0 collective-permute-done.1.two_ref
  21.1 0.0 collective-permute-done.one_ref
  21.1 0.0 copy-start
  21.1 1.2 %copy-done = bf16[1,128,4096]{2,1,0:T(8,128)(2,1)S(1)} copy-done((bf16[1,128,4096]{2,1,0:T(8,128)(2,1)S(1)}, bf16[1,128,4096]{2,1,0:T(8,128)(2,1)}, u32[]{:S(2)}) %copy-start) | copy-done | bytes 1048600
  22.3 0.0 copy-start.2
  22.3 1.0 copy-done.2
  23.3 0.0 copy-start.1
  23.3 3.2 %shard_map.87 = (bf16[128,4096]{1,0:T(8,128)(2,1)}, bf16[2048,128]{1,0:T(8,128)(2,1)}, bf16[16,128]{1,0:T(8,128)(2,1)S(1)}) custom-call(bf16[128,4096]{1,0:T(8,128)(2,1)S(1)} %bitcast.13, bf16[128,1152]{1,0:T(8,128)(2,1)S(1)} %copy-done.2, bf16[128,1152]{1,0:T(8,128)(2,1)S(1)} %collective-permute-done.one_ref, ...), custom_call_target="tpu_custom_call" | custom-call | flops 1048576 | bytes 262144 | tf_op jit(solution)/shard_map/pallas_call | solution.py:126
  26.5 2.4 %collective-permute-start.2 = (bf16[2048,128]{1,0:T(8,128)(2,1)}, bf16[2048,128]{1,0:T(8,128)(2,1)S(1)}, u32[]{:S(2)}, u32[]{:S(2)}) collective-permute-start(bf16[2048,128]{1,0:T(8,128)(2,1)} %get-tuple-element.19), channel_id=1, source_target_pairs={{0,16},{1,17},{2,18},{3,19},{4,20},{5,21},{6,22},{7,23},{8,24},{9,... | collective-permute-start | bytes 1572872 | tf_op jit(solution)/shard_map/ppermute | solution.py:42
  28.9 1.9 %all-to-all-done.first_ref = bf16[64,4,256]{2,1,0:T(4,128)(2,1)S(1)} async-done(((bf16[64,4,256]{2,1,0:T(4,128)(2,1)}), bf16[64,4,256]{2,1,0:T(4,128)(2,1)S(1)}, u32[]{:S(2)}, u32[]{:S(2)}) %all-to-all-start) | async-done | bytes 131104 | tf_op jit(solution)/shard_map/all_to_all | solution.py:46
  30.8 1.1 %shard_map.89 = bf16[64,4,640]{2,1,0:T(4,128)(2,1)} custom-call(bf16[64,4,256]{2,1,0:T(4,128)(2,1)S(1)} %all-to-all-done.first_ref, bf16[16,128]{1,0:T(8,128)(2,1)S(1)} %get-tuple-element.16.mark_ref), custom_call_target="tpu_custom_call" | custom-call | tf_op jit(solution)/shard_map/pallas_call | solution.py:282
  31.9 0.0 copy-start.3
  31.9 9.1 %all-to-all-start.1 = ((bf16[64,4,640]{2,1,0:T(4,128)(2,1)}), bf16[64,4,640]{2,1,0:T(4,128)(2,1)S(1)}, u32[]{:S(2)}, u32[]{:S(2)}) async-start(bf16[64,4,640]{2,1,0:T(4,128)(2,1)} %shard_map.89), calls=%async_computation.1 | async-start | bytes 655360 | tf_op jit(solution)/shard_map/all_to_all | solution.py:46
  41.0 0.0 copy-done.1
  41.0 0.0 copy-done.3
  41.0 2.4 %shard_map.88 = (bf16[128,4096]{1,0:T(8,128)(2,1)}, bf16[1024,128]{1,0:T(8,128)(2,1)S(1)}, bf16[1024,128]{1,0:T(8,128)(2,1)S(1)}) custom-call(bf16[128,4096]{1,0:T(8,128)(2,1)S(1)} %bitcast.14, bf16[128,1152]{1,0:T(8,128)(2,1)S(1)} %copy-done.3, bf16[128,1152]{1,0:T(8,128)(2,1)S(1)} %collective-permute-done.one_ref, ...), custom_call_target="tpu_custom_call", output_to_operand_aliasing={{0}: (4, {})} | custom-call | flops 3221225472 | bytes 2097152 | tf_op jit(solution)/shard_map/pallas_call | solution.py:126
  43.5 0.0 collective-permute-done.2.far_ref
  43.5 2.1 %collective-permute-start.4 = (bf16[2048,128]{1,0:T(8,128)(2,1)S(1)}, bf16[2048,128]{1,0:T(8,128)(2,1)S(1)}, u32[]{:S(2)}, u32[]{:S(2)}) collective-permute-start(bf16[2048,128]{1,0:T(8,128)(2,1)S(1)} %collective-permute-done.2.far_ref), channel_id=1, source_target_pairs={{0,1},{1,0},{2,3},{3,2},{4,5},{5,4},{6,7},{7,6},{8,9},{9,8},{10,11... | collective-permute-start | bytes 1572872 | tf_op jit(solution)/shard_map/ppermute | solution.py:42
  45.5 2.3 %collective-permute-start.3 = (bf16[1024,128]{1,0:T(8,128)(2,1)S(1)}, bf16[1024,128]{1,0:T(8,128)(2,1)S(1)}, u32[]{:S(2)}, u32[]{:S(2)}) collective-permute-start(bf16[1024,128]{1,0:T(8,128)(2,1)S(1)} %get-tuple-element.20), channel_id=1, source_target_pairs={{0,1},{1,0},{2,3},{3,2},{4,5},{5,4},{6,7},{7,6},{8,9},{9,8},{10,11... | collective-permute-start | bytes 786440 | tf_op jit(solution)/shard_map/ppermute | solution.py:42
  47.8 6.0 %all-to-all-done.1.second_ref = bf16[64,4,640]{2,1,0:T(4,128)(2,1)S(1)} async-done(((bf16[64,4,640]{2,1,0:T(4,128)(2,1)}), bf16[64,4,640]{2,1,0:T(4,128)(2,1)S(1)}, u32[]{:S(2)}, u32[]{:S(2)}) %all-to-all-start.1) | async-done | bytes 327712 | tf_op jit(solution)/shard_map/all_to_all | solution.py:46
  53.8 0.0 collective-permute-done.3.near_ref
  53.8 0.0 collective-permute-done.4.farthest_ref
  53.8 1.5 %shard_map.90 = bf16[1024,256]{1,0:T(8,128)(2,1)} custom-call(bf16[64,4,640]{2,1,0:T(4,128)(2,1)S(1)} %all-to-all-done.1.second_ref, bf16[1024,128]{1,0:T(8,128)(2,1)S(1)} %get-tuple-element.17.keep_ref, bf16[1024,128]{1,0:T(8,128)(2,1)S(1)} %collective-permute-done.3.near_ref, bf16[2048,128]{1,0:T(8,128)(2,1)S(1)} %collective-permute-done.2.far_ref, ...), custom_call_target="tpu_custom_call" | custom-call | tf_op jit(solution)/shard_map/pallas_call | solution.py:168
  55.3 4.3 %all-to-all-start.2 = ((bf16[16,64,256]{2,1,0:T(8,128)(2,1)}), bf16[16,64,256]{2,1,0:T(8,128)(2,1)S(1)}, u32[]{:S(2)}, u32[]{:S(2)}) async-start(bf16[16,64,256]{2,1,0:T(8,128)(2,1)} %bitcast.5), calls=%async_computation.2 | async-start | bytes 1048576 | tf_op jit(solution)/shard_map/all_to_all | solution.py:46
  59.6 16.8 %all-to-all-done.2 = bf16[16,64,256]{2,1,0:T(8,128)(2,1)S(1)} async-done(((bf16[16,64,256]{2,1,0:T(8,128)(2,1)}), bf16[16,64,256]{2,1,0:T(8,128)(2,1)S(1)}, u32[]{:S(2)}, u32[]{:S(2)}) %all-to-all-start.2) | async-done | bytes 524320 | tf_op jit(solution)/shard_map/all_to_all | solution.py:46
  76.4 0.1 reduce_sum.21
  76.6 24.6 %all_to_all.20 = bf16[8,96,256]{2,1,0:T(8,128)(2,1)S(1)} all-to-all(bf16[8,96,256]{2,1,0:T(8,128)(2,1)S(1)} %broadcast_in_dim.7), channel_id=1, replica_groups=mesh['rep'=8,'seq'=64] {'rep'}, dimensions={0} | all-to-all | bytes 786432 | tf_op jit(solution)/shard_map/all_to_all | solution.py:46
  101.2 0.8 convolution_multiply_fusion
  (6 shorter events, 0.1 us)
Async XLA Ops:
  3.4 17.7 %collective-permute-start.1 = (bf16[128,1152]{1,0:T(8,128)(2,1)}, bf16[128,1152]{1,0:T(8,128)(2,1)S(1)}, u32[]{:S(2)}, u32[]{:S(2)}) collective-permute-start(bf16[128,1152]{1,0:T(8,128)(2,1)} %get-tuple-element.12.own_ref), channel_id=1, source_target_pairs={{0,2},{1,3},{2,4},{3,5},{4,6},{5,7},{6,8},{7,9},{8,10},{9,11},{10,... | collective-permute-start | bytes 884744 | tf_op jit(solution)/shard_map/ppermute | solution.py:38
  6.9 14.2 %collective-permute-start = (bf16[128,1152]{1,0:T(8,128)(2,1)}, bf16[128,1152]{1,0:T(8,128)(2,1)S(1)}, u32[]{:S(2)}, u32[]{:S(2)}) collective-permute-start(bf16[128,1152]{1,0:T(8,128)(2,1)} %get-tuple-element.12.own_ref), channel_id=1, source_target_pairs={{0,1},{1,2},{2,3},{3,4},{4,5},{5,6},{6,7},{7,8},{8,9},{9,10},{10,1... | collective-permute-start | bytes 884744 | tf_op jit(solution)/shard_map/ppermute | solution.py:38
  8.8 21.9 %all-to-all-start = ((bf16[64,4,256]{2,1,0:T(4,128)(2,1)}), bf16[64,4,256]{2,1,0:T(4,128)(2,1)S(1)}, u32[]{:S(2)}, u32[]{:S(2)}) async-start(bf16[64,4,256]{2,1,0:T(4,128)(2,1)} %get-tuple-element.15), calls=%async_computation | async-start | bytes 262144 | tf_op jit(solution)/shard_map/all_to_all | solution.py:46
  21.1 1.2 %copy-start = (bf16[1,128,4096]{2,1,0:T(8,128)(2,1)S(1)}, bf16[1,128,4096]{2,1,0:T(8,128)(2,1)}, u32[]{:S(2)}) copy-start(bf16[1,128,4096]{2,1,0:T(8,128)(2,1)} %param.7) | copy-start | bytes 3145732
  22.3 1.0 copy-start.2
  23.3 17.7 %copy-start.1 = (bf16[1,128,4096]{2,1,0:T(8,128)(2,1)S(1)}, bf16[1,128,4096]{2,1,0:T(8,128)(2,1)}, u32[]{:S(2)}) copy-start(bf16[1,128,4096]{2,1,0:T(8,128)(2,1)} %param.7) | copy-start | bytes 3145732
  26.5 16.9 %collective-permute-start.2 = (bf16[2048,128]{1,0:T(8,128)(2,1)}, bf16[2048,128]{1,0:T(8,128)(2,1)S(1)}, u32[]{:S(2)}, u32[]{:S(2)}) collective-permute-start(bf16[2048,128]{1,0:T(8,128)(2,1)} %get-tuple-element.19), channel_id=1, source_target_pairs={{0,16},{1,17},{2,18},{3,19},{4,20},{5,21},{6,22},{7,23},{8,24},{9,... | collective-permute-start | bytes 1572872 | tf_op jit(solution)/shard_map/ppermute | solution.py:42
  31.9 9.1 %copy-start.3 = (bf16[128,1152]{1,0:T(8,128)(2,1)S(1)}, bf16[128,1152]{1,0:T(8,128)(2,1)}, u32[]{:S(2)}) copy-start(bf16[128,1152]{1,0:T(8,128)(2,1)} %get-tuple-element.12.own_ref) | copy-start | bytes 884740
  31.9 22.0 %all-to-all-start.1 = ((bf16[64,4,640]{2,1,0:T(4,128)(2,1)}), bf16[64,4,640]{2,1,0:T(4,128)(2,1)S(1)}, u32[]{:S(2)}, u32[]{:S(2)}) async-start(bf16[64,4,640]{2,1,0:T(4,128)(2,1)} %shard_map.89), calls=%async_computation.1 | async-start | bytes 655360 | tf_op jit(solution)/shard_map/all_to_all | solution.py:46
  43.5 10.4 %collective-permute-start.4 = (bf16[2048,128]{1,0:T(8,128)(2,1)S(1)}, bf16[2048,128]{1,0:T(8,128)(2,1)S(1)}, u32[]{:S(2)}, u32[]{:S(2)}) collective-permute-start(bf16[2048,128]{1,0:T(8,128)(2,1)S(1)} %collective-permute-done.2.far_ref), channel_id=1, source_target_pairs={{0,1},{1,0},{2,3},{3,2},{4,5},{5,4},{6,7},{7,6},{8,9},{9,8},{10,11... | collective-permute-start | bytes 1572872 | tf_op jit(solution)/shard_map/ppermute | solution.py:42
  45.5 8.3 %collective-permute-start.3 = (bf16[1024,128]{1,0:T(8,128)(2,1)S(1)}, bf16[1024,128]{1,0:T(8,128)(2,1)S(1)}, u32[]{:S(2)}, u32[]{:S(2)}) collective-permute-start(bf16[1024,128]{1,0:T(8,128)(2,1)S(1)} %get-tuple-element.20), channel_id=1, source_target_pairs={{0,1},{1,0},{2,3},{3,2},{4,5},{5,4},{6,7},{7,6},{8,9},{9,8},{10,11... | collective-permute-start | bytes 786440 | tf_op jit(solution)/shard_map/ppermute | solution.py:42
  55.3 21.1 %all-to-all-start.2 = ((bf16[16,64,256]{2,1,0:T(8,128)(2,1)}), bf16[16,64,256]{2,1,0:T(8,128)(2,1)S(1)}, u32[]{:S(2)}, u32[]{:S(2)}) async-start(bf16[16,64,256]{2,1,0:T(8,128)(2,1)} %bitcast.5), calls=%async_computation.2 | async-start | bytes 1048576 | tf_op jit(solution)/shard_map/all_to_all | solution.py:46

commit v9 on v8

--- a/solution.py
+++ b/solution.py
@@ -49,16 +49,35 @@
 
 
 def attention_kernel(other, q_ref, own_ref, one_ref, two_ref, *refs):
-    slab_ref, sems = refs[-2:]
     if other == 0:
-        _, out_hbm, mine_ref, theirs_ref = refs[:-2]
+        away_ref, out_hbm, mine_ref, theirs_ref, slab_ref, sems = refs
     else:
-        out_hbm, mine_ref, mark_ref = refs[:-2]
+        mine_ref, mark_ref = refs
         theirs_ref = mine_ref
         mark_ref[...] = jnp.zeros(mark_ref.shape, mark_ref.dtype)
     leaving = []
     seq = lax.axis_index("seq")
     core, odd = seq & 1, (seq >> 4) & 1
+    span = GROUP * HEAD_SIZE
+
+    def leave(z, at):
+        slab = pl.ds(pl.multiple_of(z * span, span), span)
+        leaving.append(pltpu.make_async_copy(slab_ref.at[at], out_hbm.at[:, slab], sems.at[at]))
+        leaving[-1].start()
+
+    if other == 0:
+        for z2 in range(2):
+            for j in range(GROUP):
+                row = (z2 * 8 + j) * HALF
+                mine = away_ref[row : row + HALF, :].astype(jnp.float32)
+                theirs = away_ref[ROWS + row : ROWS + row + HALF, :].astype(jnp.float32)
+                head = jnp.concatenate(
+                    [jnp.where(core == 0, mine, theirs), jnp.where(core == 0, theirs, mine)], axis=0
+                )
+                slab_ref[2 + z2, :, j * HEAD_SIZE : (j + 1) * HEAD_SIZE] = head.T.astype(
+                    jnp.bfloat16
+                )
+            leave(z2 * 2 + 1 - odd, 2 + z2)
     square = (TOKENS, TOKENS)
     lower = lax.broadcasted_iota(jnp.int32, square, 0) <= lax.broadcasted_iota(jnp.int32, square, 1)
     tags = lambda block: block[:, 2 * KV :].astype(jnp.float32)
@@ -70,7 +89,6 @@
     hidden = jnp.float32(-1e30)
     factor = HEAD_SIZE ** (-0.5) * LOG2E
     column = lambda start: pl.ds(pl.multiple_of(start, HEAD_SIZE), HEAD_SIZE)
-    span = GROUP * HEAD_SIZE
     for z2 in range(2):
         z = z2 * 2 + (odd if other == 0 else 1 - odd)
         at = z * HEAD_SIZE
@@ -103,7 +121,8 @@
         )
         for j in range(GROUP):
             head = mixed[:, j * HEAD_SIZE : (j + 1) * HEAD_SIZE]
-            slab_ref[z2, :, j * HEAD_SIZE : (j + 1) * HEAD_SIZE] = head.T.astype(jnp.bfloat16)
+            if other == 0:
+                slab_ref[z2, :, j * HEAD_SIZE : (j + 1) * HEAD_SIZE] = head.T.astype(jnp.bfloat16)
             low, high = head[:HALF], head[HALF:]
             row = (z2 * 8 + j) * HALF
             shift = other * ROWS
@@ -111,35 +130,36 @@
             theirs_ref[shift + row : shift + row + HALF, :] = jnp.where(
                 core == 0, high, low
             ).astype(jnp.bfloat16)
-        slab = pl.ds(pl.multiple_of(z * span, span), span)
-        leaving.append(pltpu.make_async_copy(slab_ref.at[z2], out_hbm.at[:, slab], sems.at[z2]))
-        leaving[z2].start()
+        if other == 0:
+            leave(z, z2)
     for copy in leaving:
         copy.wait()
 
 
-def attention(other, q, own, one, two, *attended):
+def attention(other, q, own, one, two, *away):
     vmem = pl.BlockSpec(memory_space=pltpu.VMEM)
     hbm = pl.BlockSpec(memory_space=pltpu.HBM)
-    shapes = [(2 * ROWS, TOKENS), (16, TOKENS)] if other else [(ROWS, TOKENS), (ROWS, TOKENS)]
-    shapes = [(TOKENS, QUERY_HEADS * HEAD_SIZE)] + shapes
+    shapes = [(2 * ROWS, TOKENS), (16, TOKENS)]
+    if other == 0:
+        shapes = [(TOKENS, QUERY_HEADS * HEAD_SIZE), (ROWS, TOKENS), (ROWS, TOKENS)]
     return pl.pallas_call(
         functools.partial(attention_kernel, other),
         out_shape=[jax.ShapeDtypeStruct(shape, jnp.bfloat16) for shape in shapes],
-        in_specs=[vmem] * 4 + [hbm] * len(attended),
-        out_specs=[hbm, vmem, vmem],
-        scratch_shapes=[
-            pltpu.VMEM((2, TOKENS, GROUP * HEAD_SIZE), jnp.bfloat16),
-            pltpu.SemaphoreType.DMA((2,)),
+        in_specs=[vmem] * (4 + len(away)),
+        out_specs=[vmem, vmem] if other else [hbm, vmem, vmem],
+        scratch_shapes=()
+        if other
+        else [
+            pltpu.VMEM((4, TOKENS, GROUP * HEAD_SIZE), jnp.bfloat16),
+            pltpu.SemaphoreType.DMA((4,)),
         ],
-        input_output_aliases={4: 0} if attended else {},
         compiler_params=pltpu.CompilerParams(vmem_limit_bytes=VMEM_LIMIT),
         cost_estimate=pl.CostEstimate(
             flops=1 << 20, bytes_accessed=1 << 18, transcendentals=1 << 10
         )
         if other
         else pl.CostEstimate(flops=3 << 30, bytes_accessed=2 << 20, transcendentals=1 << 19),
-    )(q, own, one, two, *attended)
+    )(q, own, one, two, *away)
 
 
 def outer_kernel(second_ref, keep_ref, near_ref, far_ref, farthest_ref, out_ref, coeffs_ref):
@@ -296,11 +316,11 @@
     one = shifted(own, 1)
     first = exchange(packed, "seq")
 
-    attended, far, mark = attention(1, queries[0], own, one, two)
-    far = swapped(far, 16)
+    away, mark = attention(1, queries[0], own, one, two)
+    far = swapped(away, 16)
 
     second = exchange(sort(first, mark), "seq")
-    attended, keep, near = attention(0, queries[0], own, one, two, attended)
+    attended, keep, near = attention(0, queries[0], own, one, two, away)
     near, far = lax.optimization_barrier((near, far))
     near = swapped(near, 1)
     farthest = swapped(far, 1)

time: 103 us -> 103 us (level)
  the two profiles are of different devices: /device:TPU:64 before, /device:TPU:72 now
where the time goes in v9:
time: 103 us; the launch traced here: 102 us
  starting transfers between devices  38.6 us (37%)
  blocking collectives  25.6 us (25%)
  waiting for transfers between devices  22.9 us (22%)
  Pallas kernels  10.7 us (10%)
  local copies, waits for them, and re-layouts  2.26 us (2%)
  between operations  1.44 us (1%)
    all_to_all x3, starting transfers between devices, exchange(): lax.all_to_all(block, axis, split_axis=0, concat_axis=0, axis_index_group...  26.4 us
    all_to_all x1, blocking collectives, exchange(): lax.all_to_all(block, axis, split_axis=0, concat_axis=0, axis_index_group...  25.6 us
    all_to_all x3, waiting for transfers between devices, exchange(): lax.all_to_all(block, axis, split_axis=0, concat_axis=0, axis_index_group...  22.9 us
    ppermute x3, starting transfers between devices, swapped(): return lax.ppermute(block, 'seq', [(i, i ^ partner) for i in range(SEQ)])  6.79 us
    pallas_call x2, Pallas kernels, attention(): pl.pallas_call(functools.partial(attention_kernel, other), out_shape=[jax...  6.03 us
    ppermute x2, starting transfers between devices, shifted(): lax.ppermute(block, 'seq', [(i, i + distance) for i in range(SEQ - distan...  5.41 us
    unnamed x9, local copies, waits for them, and re-layouts  2.19 us
    pallas_call x1, Pallas kernels, pack(): pl.pallas_call(pack_kernel, out_shape=(jax.ShapeDtypeStruct((TOKENS, 2 *...  2.11 us
  transfers between devices with their start and end apart: 8, of which 3 were waited for; matrix products, arithmetic and copies ran while one was open for 0% of the time, Pallas kernels for 7%

profile of v9, /device:TPU:72, one launch (start us, length us, event | category | flops | bytes accessed | tf_op | source)
XLA Modules:
  0.0 102.4 jit_solution(17355090262905326299)
XLA Ops:
  1.3 2.1 %shard_map.86 = (bf16[128,1152]{1,0:T(8,128)(2,1)}, bf16[64,4,256]{2,1,0:T(4,128)(2,1)}) custom-call(s32[1,1]{1,0:T(1,128)S(6)} %copy.14.dest_hbm, bf16[128,512]{1,0:T(8,128)(2,1)} %bitcast.16, bf16[128,512]{1,0:T(8,128)(2,1)} %bitcast.17, s32[1,128]{1,0:T(1,128)} %tag_hbm.1, bf16[128,256]{1,0:T(8,128)(2,1)} %bitcast.18, bf16[256,128]{1,0:T(8,128)(2,1)} %basis_hbm.1), custom_call_target="tpu_custom_call" | custom-call | tf_op jit(solution)/shard_map/pallas_call | solution.py:260
  3.4 1.9 %collective-permute-start = (bf16[128,1152]{1,0:T(8,128)(2,1)}, bf16[128,1152]{1,0:T(8,128)(2,1)S(1)}, u32[]{:S(2)}, u32[]{:S(2)}) collective-permute-start(bf16[128,1152]{1,0:T(8,128)(2,1)} %get-tuple-element.11.own_ref), channel_id=1, source_target_pairs={{0,1},{1,2},{2,3},{3,4},{4,5},{5,6},{6,7},{7,8},{8,9},{9,10},{10,1... | collective-permute-start | bytes 884744 | tf_op jit(solution)/shard_map/ppermute | solution.py:38
  5.3 3.5 %collective-permute-start.1 = (bf16[128,1152]{1,0:T(8,128)(2,1)}, bf16[128,1152]{1,0:T(8,128)(2,1)S(1)}, u32[]{:S(2)}, u32[]{:S(2)}) collective-permute-start(bf16[128,1152]{1,0:T(8,128)(2,1)} %get-tuple-element.11.own_ref), channel_id=1, source_target_pairs={{0,2},{1,3},{2,4},{3,5},{4,6},{5,7},{6,8},{7,9},{8,10},{9,11},{10,... | collective-permute-start | bytes 884744 | tf_op jit(solution)/shard_map/ppermute | solution.py:38
  8.8 11.8 %all-to-all-start = ((bf16[64,4,256]{2,1,0:T(4,128)(2,1)}), bf16[64,4,256]{2,1,0:T(4,128)(2,1)S(1)}, u32[]{:S(2)}, u32[]{:S(2)}) async-start(bf16[64,4,256]{2,1,0:T(4,128)(2,1)} %get-tuple-element.14), calls=%async_computation | async-start | bytes 262144 | tf_op jit(solution)/shard_map/all_to_all | solution.py:46
  20.7 0.0 collective-permute-done.one_ref
  20.7 0.0 collective-permute-done.1.two_ref
  20.7 0.0 copy-start
  20.7 1.2 %copy-done = bf16[1,128,4096]{2,1,0:T(8,128)(2,1)S(1)} copy-done((bf16[1,128,4096]{2,1,0:T(8,128)(2,1)S(1)}, bf16[1,128,4096]{2,1,0:T(8,128)(2,1)}, u32[]{:S(2)}) %copy-start) | copy-done | bytes 1048600
  21.9 0.0 copy-start.2
  21.9 1.0 copy-done.2
  22.9 0.0 copy-start.1
  22.9 2.4 %shard_map.87 = (bf16[2048,128]{1,0:T(8,128)(2,1)}, bf16[16,128]{1,0:T(8,128)(2,1)S(1)}) custom-call(bf16[128,4096]{1,0:T(8,128)(2,1)S(1)} %bitcast.13, bf16[128,1152]{1,0:T(8,128)(2,1)S(1)} %copy-done.2, bf16[128,1152]{1,0:T(8,128)(2,1)S(1)} %collective-permute-done.one_ref, bf16[128,1152]{1,0:T(8,128)(2,1)S(1)} %collective-permute-done.1.two_ref), custom_call_target="tpu_custom_call" | custom-call | flops 1048576 | bytes 262144 | tf_op jit(solution)/shard_map/pallas_call | solution.py:145
  25.3 2.5 %collective-permute-start.2 = (bf16[2048,128]{1,0:T(8,128)(2,1)}, bf16[2048,128]{1,0:T(8,128)(2,1)S(1)}, u32[]{:S(2)}, u32[]{:S(2)}) collective-permute-start(bf16[2048,128]{1,0:T(8,128)(2,1)} %get-tuple-element.12.refs_0_), channel_id=1, source_target_pairs={{0,16},{1,17},{2,18},{3,19},{4,20},{5,21},{6,22},{7,23},{8,24},{9,... | collective-permute-start | bytes 1572872 | tf_op jit(solution)/shard_map/ppermute | solution.py:42
  27.7 2.5 %all-to-all-done.first_ref = bf16[64,4,256]{2,1,0:T(4,128)(2,1)S(1)} async-done(((bf16[64,4,256]{2,1,0:T(4,128)(2,1)}), bf16[64,4,256]{2,1,0:T(4,128)(2,1)S(1)}, u32[]{:S(2)}, u32[]{:S(2)}) %all-to-all-start) | async-done | bytes 131104 | tf_op jit(solution)/shard_map/all_to_all | solution.py:46
  30.2 1.1 %shard_map.89 = bf16[64,4,640]{2,1,0:T(4,128)(2,1)} custom-call(bf16[64,4,256]{2,1,0:T(4,128)(2,1)S(1)} %all-to-all-done.first_ref, bf16[16,128]{1,0:T(8,128)(2,1)S(1)} %get-tuple-element.15.mark_ref), custom_call_target="tpu_custom_call" | custom-call | tf_op jit(solution)/shard_map/pallas_call | solution.py:302
  31.3 0.0 copy-start.3
  31.3 8.4 %all-to-all-start.1 = ((bf16[64,4,640]{2,1,0:T(4,128)(2,1)}), bf16[64,4,640]{2,1,0:T(4,128)(2,1)S(1)}, u32[]{:S(2)}, u32[]{:S(2)}) async-start(bf16[64,4,640]{2,1,0:T(4,128)(2,1)} %shard_map.89), calls=%async_computation.1 | async-start | bytes 655360 | tf_op jit(solution)/shard_map/all_to_all | solution.py:46
  39.7 0.0 copy-done.1
  39.7 0.0 copy-done.3
  39.7 3.6 %shard_map.88 = (bf16[128,4096]{1,0:T(8,128)(2,1)}, bf16[1024,128]{1,0:T(8,128)(2,1)S(1)}, bf16[1024,128]{1,0:T(8,128)(2,1)S(1)}) custom-call(bf16[128,4096]{1,0:T(8,128)(2,1)S(1)} %bitcast.14, bf16[128,1152]{1,0:T(8,128)(2,1)S(1)} %copy-done.3, bf16[128,1152]{1,0:T(8,128)(2,1)S(1)} %collective-permute-done.one_ref, ...), custom_call_target="tpu_custom_call" | custom-call | flops 3221225472 | bytes 2097152 | tf_op jit(solution)/shard_map/pallas_call | solution.py:145
  43.4 0.0 collective-permute-done.2.far_ref
  43.4 2.1 %collective-permute-start.4 = (bf16[2048,128]{1,0:T(8,128)(2,1)S(1)}, bf16[2048,128]{1,0:T(8,128)(2,1)S(1)}, u32[]{:S(2)}, u32[]{:S(2)}) collective-permute-start(bf16[2048,128]{1,0:T(8,128)(2,1)S(1)} %collective-permute-done.2.far_ref), channel_id=1, source_target_pairs={{0,1},{1,0},{2,3},{3,2},{4,5},{5,4},{6,7},{7,6},{8,9},{9,8},{10,11... | collective-permute-start | bytes 1572872 | tf_op jit(solution)/shard_map/ppermute | solution.py:42
  45.5 2.3 %collective-permute-start.3 = (bf16[1024,128]{1,0:T(8,128)(2,1)S(1)}, bf16[1024,128]{1,0:T(8,128)(2,1)S(1)}, u32[]{:S(2)}, u32[]{:S(2)}) collective-permute-start(bf16[1024,128]{1,0:T(8,128)(2,1)S(1)} %get-tuple-element.18), channel_id=1, source_target_pairs={{0,1},{1,0},{2,3},{3,2},{4,5},{5,4},{6,7},{7,6},{8,9},{9,8},{10,11... | collective-permute-start | bytes 786440 | tf_op jit(solution)/shard_map/ppermute | solution.py:42
  47.7 4.6 %all-to-all-done.1.second_ref = bf16[64,4,640]{2,1,0:T(4,128)(2,1)S(1)} async-done(((bf16[64,4,640]{2,1,0:T(4,128)(2,1)}), bf16[64,4,640]{2,1,0:T(4,128)(2,1)S(1)}, u32[]{:S(2)}, u32[]{:S(2)}) %all-to-all-start.1) | async-done | bytes 327712 | tf_op jit(solution)/shard_map/all_to_all | solution.py:46
  52.3 0.0 collective-permute-done.3.near_ref
  52.3 0.0 collective-permute-done.4.farthest_ref
  52.3 1.4 %shard_map.90 = bf16[1024,256]{1,0:T(8,128)(2,1)} custom-call(bf16[64,4,640]{2,1,0:T(4,128)(2,1)S(1)} %all-to-all-done.1.second_ref, bf16[1024,128]{1,0:T(8,128)(2,1)S(1)} %get-tuple-element.16.keep_ref, bf16[1024,128]{1,0:T(8,128)(2,1)S(1)} %collective-permute-done.3.near_ref, bf16[2048,128]{1,0:T(8,128)(2,1)S(1)} %collective-permute-done.2.far_ref, ...), custom_call_target="tpu_custom_call" | custom-call | tf_op jit(solution)/shard_map/pallas_call | solution.py:188
  53.8 6.2 %all-to-all-start.2 = ((bf16[16,64,256]{2,1,0:T(8,128)(2,1)}), bf16[16,64,256]{2,1,0:T(8,128)(2,1)S(1)}, u32[]{:S(2)}, u32[]{:S(2)}) async-start(bf16[16,64,256]{2,1,0:T(8,128)(2,1)} %bitcast.5), calls=%async_computation.2 | async-start | bytes 1048576 | tf_op jit(solution)/shard_map/all_to_all | solution.py:46
  60.0 15.8 %all-to-all-done.2 = bf16[16,64,256]{2,1,0:T(8,128)(2,1)S(1)} async-done(((bf16[16,64,256]{2,1,0:T(8,128)(2,1)}), bf16[16,64,256]{2,1,0:T(8,128)(2,1)S(1)}, u32[]{:S(2)}, u32[]{:S(2)}) %all-to-all-start.2) | async-done | bytes 524320 | tf_op jit(solution)/shard_map/all_to_all | solution.py:46
  75.8 0.1 reduce_sum.21
  75.9 25.6 %all_to_all.20 = bf16[8,96,256]{2,1,0:T(8,128)(2,1)S(1)} all-to-all(bf16[8,96,256]{2,1,0:T(8,128)(2,1)S(1)} %broadcast_in_dim.7), channel_id=1, replica_groups=mesh['rep'=8,'seq'=64] {'rep'}, dimensions={0} | all-to-all | bytes 786432 | tf_op jit(solution)/shard_map/all_to_all | solution.py:46
  101.6 0.8 convolution_multiply_fusion
  (6 shorter events, 0.1 us)
Async XLA Ops:
  3.4 17.3 %collective-permute-start = (bf16[128,1152]{1,0:T(8,128)(2,1)}, bf16[128,1152]{1,0:T(8,128)(2,1)S(1)}, u32[]{:S(2)}, u32[]{:S(2)}) collective-permute-start(bf16[128,1152]{1,0:T(8,128)(2,1)} %get-tuple-element.11.own_ref), channel_id=1, source_target_pairs={{0,1},{1,2},{2,3},{3,4},{4,5},{5,6},{6,7},{7,8},{8,9},{9,10},{10,1... | collective-permute-start | bytes 884744 | tf_op jit(solution)/shard_map/ppermute | solution.py:38
  5.3 15.4 %collective-permute-start.1 = (bf16[128,1152]{1,0:T(8,128)(2,1)}, bf16[128,1152]{1,0:T(8,128)(2,1)S(1)}, u32[]{:S(2)}, u32[]{:S(2)}) collective-permute-start(bf16[128,1152]{1,0:T(8,128)(2,1)} %get-tuple-element.11.own_ref), channel_id=1, source_target_pairs={{0,2},{1,3},{2,4},{3,5},{4,6},{5,7},{6,8},{7,9},{8,10},{9,11},{10,... | collective-permute-start | bytes 884744 | tf_op jit(solution)/shard_map/ppermute | solution.py:38
  8.8 21.4 %all-to-all-start = ((bf16[64,4,256]{2,1,0:T(4,128)(2,1)}), bf16[64,4,256]{2,1,0:T(4,128)(2,1)S(1)}, u32[]{:S(2)}, u32[]{:S(2)}) async-start(bf16[64,4,256]{2,1,0:T(4,128)(2,1)} %get-tuple-element.14), calls=%async_computation | async-start | bytes 262144 | tf_op jit(solution)/shard_map/all_to_all | solution.py:46
  20.7 1.2 %copy-start = (bf16[1,128,4096]{2,1,0:T(8,128)(2,1)S(1)}, bf16[1,128,4096]{2,1,0:T(8,128)(2,1)}, u32[]{:S(2)}) copy-start(bf16[1,128,4096]{2,1,0:T(8,128)(2,1)} %param.7) | copy-start | bytes 3145732
  21.9 1.0 copy-start.2
  22.9 16.8 %copy-start.1 = (bf16[1,128,4096]{2,1,0:T(8,128)(2,1)S(1)}, bf16[1,128,4096]{2,1,0:T(8,128)(2,1)}, u32[]{:S(2)}) copy-start(bf16[1,128,4096]{2,1,0:T(8,128)(2,1)} %param.7) | copy-start | bytes 3145732
  25.3 18.1 %collective-permute-start.2 = (bf16[2048,128]{1,0:T(8,128)(2,1)}, bf16[2048,128]{1,0:T(8,128)(2,1)S(1)}, u32[]{:S(2)}, u32[]{:S(2)}) collective-permute-start(bf16[2048,128]{1,0:T(8,128)(2,1)} %get-tuple-element.12.refs_0_), channel_id=1, source_target_pairs={{0,16},{1,17},{2,18},{3,19},{4,20},{5,21},{6,22},{7,23},{8,24},{9,... | collective-permute-start | bytes 1572872 | tf_op jit(solution)/shard_map/ppermute | solution.py:42
  31.3 8.4 %copy-start.3 = (bf16[128,1152]{1,0:T(8,128)(2,1)S(1)}, bf16[128,1152]{1,0:T(8,128)(2,1)}, u32[]{:S(2)}) copy-start(bf16[128,1152]{1,0:T(8,128)(2,1)} %get-tuple-element.11.own_ref) | copy-start | bytes 884740
  31.3 21.0 %all-to-all-start.1 = ((bf16[64,4,640]{2,1,0:T(4,128)(2,1)}), bf16[64,4,640]{2,1,0:T(4,128)(2,1)S(1)}, u32[]{:S(2)}, u32[]{:S(2)}) async-start(bf16[64,4,640]{2,1,0:T(4,128)(2,1)} %shard_map.89), calls=%async_computation.1 | async-start | bytes 655360 | tf_op jit(solution)/shard_map/all_to_all | solution.py:46
  43.4 8.9 %collective-permute-start.4 = (bf16[2048,128]{1,0:T(8,128)(2,1)S(1)}, bf16[2048,128]{1,0:T(8,128)(2,1)S(1)}, u32[]{:S(2)}, u32[]{:S(2)}) collective-permute-start(bf16[2048,128]{1,0:T(8,128)(2,1)S(1)} %collective-permute-done.2.far_ref), channel_id=1, source_target_pairs={{0,1},{1,0},{2,3},{3,2},{4,5},{5,4},{6,7},{7,6},{8,9},{9,8},{10,11... | collective-permute-start | bytes 1572872 | tf_op jit(solution)/shard_map/ppermute | solution.py:42
  45.5 6.8 %collective-permute-start.3 = (bf16[1024,128]{1,0:T(8,128)(2,1)S(1)}, bf16[1024,128]{1,0:T(8,128)(2,1)S(1)}, u32[]{:S(2)}, u32[]{:S(2)}) collective-permute-start(bf16[1024,128]{1,0:T(8,128)(2,1)S(1)} %get-tuple-element.18), channel_id=1, source_target_pairs={{0,1},{1,0},{2,3},{3,2},{4,5},{5,4},{6,7},{7,6},{8,9},{9,8},{10,11... | collective-permute-start | bytes 786440 | tf_op jit(solution)/shard_map/ppermute | solution.py:42
  53.8 22.0 %all-to-all-start.2 = ((bf16[16,64,256]{2,1,0:T(8,128)(2,1)}), bf16[16,64,256]{2,1,0:T(8,128)(2,1)S(1)}, u32[]{:S(2)}, u32[]{:S(2)}) async-start(bf16[16,64,256]{2,1,0:T(8,128)(2,1)} %bitcast.5), calls=%async_computation.2 | async-start | bytes 1048576 | tf_op jit(solution)/shard_map/all_to_all | solution.py:46

commit v10 on v9

--- a/solution.py
+++ b/solution.py
@@ -183,7 +183,7 @@
 
 
 def outer(second, keep, near, far, farthest):
-    step = ROWS // 2
+    step = ROWS
     block = lambda first: pl.BlockSpec((step, TOKENS), lambda i: (i + first, 0))
     return pl.pallas_call(
         outer_kernel,

time: 103 us -> 103 us (level)
  no operation moved by 1% of the time
where the time goes in v10:
time: 103 us; the launch traced here: 102 us
  starting transfers between devices  38.6 us (37%)
  blocking collectives  25.6 us (25%)
  waiting for transfers between devices  22.9 us (22%)
  Pallas kernels  10.5 us (10%)
  local copies, waits for them, and re-layouts  2.26 us (2%)
  between operations  1.44 us (1%)
    all_to_all x3, starting transfers between devices, exchange(): lax.all_to_all(block, axis, split_axis=0, concat_axis=0, axis_index_group...  26.4 us
    all_to_all x1, blocking collectives, exchange(): lax.all_to_all(block, axis, split_axis=0, concat_axis=0, axis_index_group...  25.6 us
    all_to_all x3, waiting for transfers between devices, exchange(): lax.all_to_all(block, axis, split_axis=0, concat_axis=0, axis_index_group...  22.9 us
    ppermute x3, starting transfers between devices, swapped(): return lax.ppermute(block, 'seq', [(i, i ^ partner) for i in range(SEQ)])  6.79 us
    pallas_call x2, Pallas kernels, attention(): pl.pallas_call(functools.partial(attention_kernel, other), out_shape=[jax...  6.03 us
    ppermute x2, starting transfers between devices, shifted(): lax.ppermute(block, 'seq', [(i, i + distance) for i in range(SEQ - distan...  5.41 us
    unnamed x9, local copies, waits for them, and re-layouts  2.19 us
    pallas_call x1, Pallas kernels, pack(): pl.pallas_call(pack_kernel, out_shape=(jax.ShapeDtypeStruct((TOKENS, 2 *...  2.11 us
  transfers between devices with their start and end apart: 8, of which 3 were waited for; matrix products, arithmetic and copies ran while one was open for 0% of the time, Pallas kernels for 7%

profile of v10, /device:TPU:72, one launch (start us, length us, event | category | flops | bytes accessed | tf_op | source)
XLA Modules:
  0.0 102.2 jit_solution(2734544159109407989)
XLA Ops:
  1.3 2.1 %shard_map.86 = (bf16[128,1152]{1,0:T(8,128)(2,1)}, bf16[64,4,256]{2,1,0:T(4,128)(2,1)}) custom-call(s32[1,1]{1,0:T(1,128)S(6)} %copy.14.dest_hbm, bf16[128,512]{1,0:T(8,128)(2,1)} %bitcast.16, bf16[128,512]{1,0:T(8,128)(2,1)} %bitcast.17, s32[1,128]{1,0:T(1,128)} %tag_hbm.1, bf16[128,256]{1,0:T(8,128)(2,1)} %bitcast.18, bf16[256,128]{1,0:T(8,128)(2,1)} %basis_hbm.1), custom_call_target="tpu_custom_call" | custom-call | tf_op jit(solution)/shard_map/pallas_call | solution.py:260
  3.4 1.9 %collective-permute-start = (bf16[128,1152]{1,0:T(8,128)(2,1)}, bf16[128,1152]{1,0:T(8,128)(2,1)S(1)}, u32[]{:S(2)}, u32[]{:S(2)}) collective-permute-start(bf16[128,1152]{1,0:T(8,128)(2,1)} %get-tuple-element.11.own_ref), channel_id=1, source_target_pairs={{0,1},{1,2},{2,3},{3,4},{4,5},{5,6},{6,7},{7,8},{8,9},{9,10},{10,1... | collective-permute-start | bytes 884744 | tf_op jit(solution)/shard_map/ppermute | solution.py:38
  5.3 3.5 %collective-permute-start.1 = (bf16[128,1152]{1,0:T(8,128)(2,1)}, bf16[128,1152]{1,0:T(8,128)(2,1)S(1)}, u32[]{:S(2)}, u32[]{:S(2)}) collective-permute-start(bf16[128,1152]{1,0:T(8,128)(2,1)} %get-tuple-element.11.own_ref), channel_id=1, source_target_pairs={{0,2},{1,3},{2,4},{3,5},{4,6},{5,7},{6,8},{7,9},{8,10},{9,11},{10,... | collective-permute-start | bytes 884744 | tf_op jit(solution)/shard_map/ppermute | solution.py:38
  8.8 11.8 %all-to-all-start = ((bf16[64,4,256]{2,1,0:T(4,128)(2,1)}), bf16[64,4,256]{2,1,0:T(4,128)(2,1)S(1)}, u32[]{:S(2)}, u32[]{:S(2)}) async-start(bf16[64,4,256]{2,1,0:T(4,128)(2,1)} %get-tuple-element.14), calls=%async_computation | async-start | bytes 262144 | tf_op jit(solution)/shard_map/all_to_all | solution.py:46
  20.7 0.0 collective-permute-done.one_ref
  20.7 0.0 collective-permute-done.1.two_ref
  20.7 0.0 copy-start
  20.7 1.2 %copy-done = bf16[1,128,4096]{2,1,0:T(8,128)(2,1)S(1)} copy-done((bf16[1,128,4096]{2,1,0:T(8,128)(2,1)S(1)}, bf16[1,128,4096]{2,1,0:T(8,128)(2,1)}, u32[]{:S(2)}) %copy-start) | copy-done | bytes 1048600
  21.9 0.0 copy-start.2
  21.9 1.0 copy-done.2
  22.9 0.0 copy-start.1
  22.9 2.4 %shard_map.87 = (bf16[2048,128]{1,0:T(8,128)(2,1)}, bf16[16,128]{1,0:T(8,128)(2,1)S(1)}) custom-call(bf16[128,4096]{1,0:T(8,128)(2,1)S(1)} %bitcast.13, bf16[128,1152]{1,0:T(8,128)(2,1)S(1)} %copy-done.2, bf16[128,1152]{1,0:T(8,128)(2,1)S(1)} %collective-permute-done.one_ref, bf16[128,1152]{1,0:T(8,128)(2,1)S(1)} %collective-permute-done.1.two_ref), custom_call_target="tpu_custom_call" | custom-call | flops 1048576 | bytes 262144 | tf_op jit(solution)/shard_map/pallas_call | solution.py:145
  25.3 2.5 %collective-permute-start.2 = (bf16[2048,128]{1,0:T(8,128)(2,1)}, bf16[2048,128]{1,0:T(8,128)(2,1)S(1)}, u32[]{:S(2)}, u32[]{:S(2)}) collective-permute-start(bf16[2048,128]{1,0:T(8,128)(2,1)} %get-tuple-element.12.refs_0_), channel_id=1, source_target_pairs={{0,16},{1,17},{2,18},{3,19},{4,20},{5,21},{6,22},{7,23},{8,24},{9,... | collective-permute-start | bytes 1572872 | tf_op jit(solution)/shard_map/ppermute | solution.py:42
  27.7 2.5 %all-to-all-done.first_ref = bf16[64,4,256]{2,1,0:T(4,128)(2,1)S(1)} async-done(((bf16[64,4,256]{2,1,0:T(4,128)(2,1)}), bf16[64,4,256]{2,1,0:T(4,128)(2,1)S(1)}, u32[]{:S(2)}, u32[]{:S(2)}) %all-to-all-start) | async-done | bytes 131104 | tf_op jit(solution)/shard_map/all_to_all | solution.py:46
  30.2 1.1 %shard_map.89 = bf16[64,4,640]{2,1,0:T(4,128)(2,1)} custom-call(bf16[64,4,256]{2,1,0:T(4,128)(2,1)S(1)} %all-to-all-done.first_ref, bf16[16,128]{1,0:T(8,128)(2,1)S(1)} %get-tuple-element.15.mark_ref), custom_call_target="tpu_custom_call" | custom-call | tf_op jit(solution)/shard_map/pallas_call | solution.py:302
  31.3 0.0 copy-start.3
  31.3 8.4 %all-to-all-start.1 = ((bf16[64,4,640]{2,1,0:T(4,128)(2,1)}), bf16[64,4,640]{2,1,0:T(4,128)(2,1)S(1)}, u32[]{:S(2)}, u32[]{:S(2)}) async-start(bf16[64,4,640]{2,1,0:T(4,128)(2,1)} %shard_map.89), calls=%async_computation.1 | async-start | bytes 655360 | tf_op jit(solution)/shard_map/all_to_all | solution.py:46
  39.7 0.0 copy-done.1
  39.7 0.0 copy-done.3
  39.7 3.6 %shard_map.88 = (bf16[128,4096]{1,0:T(8,128)(2,1)}, bf16[1024,128]{1,0:T(8,128)(2,1)S(1)}, bf16[1024,128]{1,0:T(8,128)(2,1)S(1)}) custom-call(bf16[128,4096]{1,0:T(8,128)(2,1)S(1)} %bitcast.14, bf16[128,1152]{1,0:T(8,128)(2,1)S(1)} %copy-done.3, bf16[128,1152]{1,0:T(8,128)(2,1)S(1)} %collective-permute-done.one_ref, ...), custom_call_target="tpu_custom_call" | custom-call | flops 3221225472 | bytes 2097152 | tf_op jit(solution)/shard_map/pallas_call | solution.py:145
  43.4 0.0 collective-permute-done.2.far_ref
  43.4 2.1 %collective-permute-start.4 = (bf16[2048,128]{1,0:T(8,128)(2,1)S(1)}, bf16[2048,128]{1,0:T(8,128)(2,1)S(1)}, u32[]{:S(2)}, u32[]{:S(2)}) collective-permute-start(bf16[2048,128]{1,0:T(8,128)(2,1)S(1)} %collective-permute-done.2.far_ref), channel_id=1, source_target_pairs={{0,1},{1,0},{2,3},{3,2},{4,5},{5,4},{6,7},{7,6},{8,9},{9,8},{10,11... | collective-permute-start | bytes 1572872 | tf_op jit(solution)/shard_map/ppermute | solution.py:42
  45.5 2.3 %collective-permute-start.3 = (bf16[1024,128]{1,0:T(8,128)(2,1)S(1)}, bf16[1024,128]{1,0:T(8,128)(2,1)S(1)}, u32[]{:S(2)}, u32[]{:S(2)}) collective-permute-start(bf16[1024,128]{1,0:T(8,128)(2,1)S(1)} %get-tuple-element.18), channel_id=1, source_target_pairs={{0,1},{1,0},{2,3},{3,2},{4,5},{5,4},{6,7},{7,6},{8,9},{9,8},{10,11... | collective-permute-start | bytes 786440 | tf_op jit(solution)/shard_map/ppermute | solution.py:42
  47.7 4.6 %all-to-all-done.1.second_ref = bf16[64,4,640]{2,1,0:T(4,128)(2,1)S(1)} async-done(((bf16[64,4,640]{2,1,0:T(4,128)(2,1)}), bf16[64,4,640]{2,1,0:T(4,128)(2,1)S(1)}, u32[]{:S(2)}, u32[]{:S(2)}) %all-to-all-start.1) | async-done | bytes 327712 | tf_op jit(solution)/shard_map/all_to_all | solution.py:46
  52.3 0.0 collective-permute-done.3.near_ref
  52.3 0.0 collective-permute-done.4.farthest_ref
  52.3 1.3 %shard_map.90 = bf16[1024,256]{1,0:T(8,128)(2,1)} custom-call(bf16[64,4,640]{2,1,0:T(4,128)(2,1)S(1)} %all-to-all-done.1.second_ref, bf16[1024,128]{1,0:T(8,128)(2,1)S(1)} %get-tuple-element.16.keep_ref, bf16[1024,128]{1,0:T(8,128)(2,1)S(1)} %collective-permute-done.3.near_ref, bf16[2048,128]{1,0:T(8,128)(2,1)S(1)} %collective-permute-done.2.far_ref, ...), custom_call_target="tpu_custom_call" | custom-call | tf_op jit(solution)/shard_map/pallas_call | solution.py:188
  53.6 6.2 %all-to-all-start.2 = ((bf16[16,64,256]{2,1,0:T(8,128)(2,1)}), bf16[16,64,256]{2,1,0:T(8,128)(2,1)S(1)}, u32[]{:S(2)}, u32[]{:S(2)}) async-start(bf16[16,64,256]{2,1,0:T(8,128)(2,1)} %bitcast.5), calls=%async_computation.2 | async-start | bytes 1048576 | tf_op jit(solution)/shard_map/all_to_all | solution.py:46
  59.8 15.8 %all-to-all-done.2 = bf16[16,64,256]{2,1,0:T(8,128)(2,1)S(1)} async-done(((bf16[16,64,256]{2,1,0:T(8,128)(2,1)}), bf16[16,64,256]{2,1,0:T(8,128)(2,1)S(1)}, u32[]{:S(2)}, u32[]{:S(2)}) %all-to-all-start.2) | async-done | bytes 524320 | tf_op jit(solution)/shard_map/all_to_all | solution.py:46
  75.6 0.1 reduce_sum.21
  75.8 25.6 %all_to_all.20 = bf16[8,96,256]{2,1,0:T(8,128)(2,1)S(1)} all-to-all(bf16[8,96,256]{2,1,0:T(8,128)(2,1)S(1)} %broadcast_in_dim.7), channel_id=1, replica_groups=mesh['rep'=8,'seq'=64] {'rep'}, dimensions={0} | all-to-all | bytes 786432 | tf_op jit(solution)/shard_map/all_to_all | solution.py:46
  101.4 0.8 convolution_multiply_fusion
  (6 shorter events, 0.1 us)
Async XLA Ops:
  3.4 17.3 %collective-permute-start = (bf16[128,1152]{1,0:T(8,128)(2,1)}, bf16[128,1152]{1,0:T(8,128)(2,1)S(1)}, u32[]{:S(2)}, u32[]{:S(2)}) collective-permute-start(bf16[128,1152]{1,0:T(8,128)(2,1)} %get-tuple-element.11.own_ref), channel_id=1, source_target_pairs={{0,1},{1,2},{2,3},{3,4},{4,5},{5,6},{6,7},{7,8},{8,9},{9,10},{10,1... | collective-permute-start | bytes 884744 | tf_op jit(solution)/shard_map/ppermute | solution.py:38
  5.3 15.4 %collective-permute-start.1 = (bf16[128,1152]{1,0:T(8,128)(2,1)}, bf16[128,1152]{1,0:T(8,128)(2,1)S(1)}, u32[]{:S(2)}, u32[]{:S(2)}) collective-permute-start(bf16[128,1152]{1,0:T(8,128)(2,1)} %get-tuple-element.11.own_ref), channel_id=1, source_target_pairs={{0,2},{1,3},{2,4},{3,5},{4,6},{5,7},{6,8},{7,9},{8,10},{9,11},{10,... | collective-permute-start | bytes 884744 | tf_op jit(solution)/shard_map/ppermute | solution.py:38
  8.8 21.4 %all-to-all-start = ((bf16[64,4,256]{2,1,0:T(4,128)(2,1)}), bf16[64,4,256]{2,1,0:T(4,128)(2,1)S(1)}, u32[]{:S(2)}, u32[]{:S(2)}) async-start(bf16[64,4,256]{2,1,0:T(4,128)(2,1)} %get-tuple-element.14), calls=%async_computation | async-start | bytes 262144 | tf_op jit(solution)/shard_map/all_to_all | solution.py:46
  20.7 1.2 %copy-start = (bf16[1,128,4096]{2,1,0:T(8,128)(2,1)S(1)}, bf16[1,128,4096]{2,1,0:T(8,128)(2,1)}, u32[]{:S(2)}) copy-start(bf16[1,128,4096]{2,1,0:T(8,128)(2,1)} %param.7) | copy-start | bytes 3145732
  21.9 1.0 copy-start.2
  22.9 16.8 %copy-start.1 = (bf16[1,128,4096]{2,1,0:T(8,128)(2,1)S(1)}, bf16[1,128,4096]{2,1,0:T(8,128)(2,1)}, u32[]{:S(2)}) copy-start(bf16[1,128,4096]{2,1,0:T(8,128)(2,1)} %param.7) | copy-start | bytes 3145732
  25.3 18.1 %collective-permute-start.2 = (bf16[2048,128]{1,0:T(8,128)(2,1)}, bf16[2048,128]{1,0:T(8,128)(2,1)S(1)}, u32[]{:S(2)}, u32[]{:S(2)}) collective-permute-start(bf16[2048,128]{1,0:T(8,128)(2,1)} %get-tuple-element.12.refs_0_), channel_id=1, source_target_pairs={{0,16},{1,17},{2,18},{3,19},{4,20},{5,21},{6,22},{7,23},{8,24},{9,... | collective-permute-start | bytes 1572872 | tf_op jit(solution)/shard_map/ppermute | solution.py:42
  31.3 8.4 %copy-start.3 = (bf16[128,1152]{1,0:T(8,128)(2,1)S(1)}, bf16[128,1152]{1,0:T(8,128)(2,1)}, u32[]{:S(2)}) copy-start(bf16[128,1152]{1,0:T(8,128)(2,1)} %get-tuple-element.11.own_ref) | copy-start | bytes 884740
  31.3 21.0 %all-to-all-start.1 = ((bf16[64,4,640]{2,1,0:T(4,128)(2,1)}), bf16[64,4,640]{2,1,0:T(4,128)(2,1)S(1)}, u32[]{:S(2)}, u32[]{:S(2)}) async-start(bf16[64,4,640]{2,1,0:T(4,128)(2,1)} %shard_map.89), calls=%async_computation.1 | async-start | bytes 655360 | tf_op jit(solution)/shard_map/all_to_all | solution.py:46
  43.4 8.9 %collective-permute-start.4 = (bf16[2048,128]{1,0:T(8,128)(2,1)S(1)}, bf16[2048,128]{1,0:T(8,128)(2,1)S(1)}, u32[]{:S(2)}, u32[]{:S(2)}) collective-permute-start(bf16[2048,128]{1,0:T(8,128)(2,1)S(1)} %collective-permute-done.2.far_ref), channel_id=1, source_target_pairs={{0,1},{1,0},{2,3},{3,2},{4,5},{5,4},{6,7},{7,6},{8,9},{9,8},{10,11... | collective-permute-start | bytes 1572872 | tf_op jit(solution)/shard_map/ppermute | solution.py:42
  45.5 6.8 %collective-permute-start.3 = (bf16[1024,128]{1,0:T(8,128)(2,1)S(1)}, bf16[1024,128]{1,0:T(8,128)(2,1)S(1)}, u32[]{:S(2)}, u32[]{:S(2)}) collective-permute-start(bf16[1024,128]{1,0:T(8,128)(2,1)S(1)} %get-tuple-element.18), channel_id=1, source_target_pairs={{0,1},{1,0},{2,3},{3,2},{4,5},{5,4},{6,7},{7,6},{8,9},{9,8},{10,11... | collective-permute-start | bytes 786440 | tf_op jit(solution)/shard_map/ppermute | solution.py:42
  53.6 22.1 %all-to-all-start.2 = ((bf16[16,64,256]{2,1,0:T(8,128)(2,1)}), bf16[16,64,256]{2,1,0:T(8,128)(2,1)S(1)}, u32[]{:S(2)}, u32[]{:S(2)}) async-start(bf16[16,64,256]{2,1,0:T(8,128)(2,1)} %bitcast.5), calls=%async_computation.2 | async-start | bytes 1048576 | tf_op jit(solution)/shard_map/all_to_all | solution.py:46
